TPU v7x, 512 devices: a whole 4x4x16 slice. The times are simulated.
512 devices in a mesh: lat: 8 (over z_lo), lon: 64 (over y, x, z_hi, core).
Axes of the slice: x: 4, y: 4, z: 16 (z_hi: 2, z_lo: 8; z = z_hi * 8 + z_lo), core: 2. Of those that a mesh axis runs over, the one named last changes fastest.
Arguments:
- anomalies: bfloat16 [16, 256, 16, 256], P('lat', 'lon'), may hold values from -6 to 6
- background_mean: float32 [16, 256, 16], P('lat', 'lon'), may hold values from -6 to 6
- obs_anom: bfloat16 [8, 32768, 256], P('lat', 'lon'), may hold values from -4 to 4
- innovation: bfloat16 [8, 32768], P('lat', 'lon'), may hold values from -6 to 6
- obs_precision: bfloat16 [8, 32768], P('lat', 'lon'), may hold values from 0.5 to 4
- obs_blocks: int32 [8, 64], P('lat', 'lon'), may hold values from 1 to 4
- localization: float32 [8, 64, 7680], P('lat', 'lon'), may hold values from 0.15 to 1
- loc_pattern: int32 [8, 64, 60], P('lat', 'lon'), may hold values 0 or 1
Outputs:
- analysis: bfloat16 [16, 256, 16, 256], P('lat', 'lon')
All inputs are finite; a program needn't handle non-finite values. Where the computation divides by a largest or mean magnitude, that divisor is 1e-20 or more. No bound on the sum of `loc_pattern` on one device may be relied on, other than what follows from the above.
Results may differ from a plain program's by a relative error of at most 0.0075.
Values may be sent and summed in bfloat16 or wider, within the bound.
No kernel may reach another device: no remote copies, remote signals or barrier semaphores. Data moves between devices by JAX's collectives and lax.ppermute only.
A program may use at most 64 MiB of HBM per device.

v0:
```python
import jax
import jax.numpy as jnp
import numpy as np
from jax import lax
from jax.sharding import PartitionSpec as P

LAT_REACH = 1
LON_REACH = 2
NSI = 5


block_rows = 128
highest = lax.Precision.HIGHEST


def shifted(value, axis, steps):
    count = lax.axis_size(axis)
    leading, last = (max(0, -steps), min(count, count - steps))
    return lax.ppermute(value, axis, [(source, source + steps) for source in range(leading, last)])


def as_sent(x):

    def short(part):
        return part.astype(jnp.bfloat16) if part.dtype == jnp.float32 else part

    return jax.tree.map(short, x)


def passed_along(block, axis, distance):
    devices = range(lax.axis_size(axis))
    route = [((i - distance) % len(devices), i) for i in devices]
    return lax.ppermute(block, axis, route)


def blend_table(groups, width):
    columns = np.arange(groups * width)
    offset = columns % width - (width - 1) / 2.0
    lower = np.where(offset < 0, columns // width, columns // width + 1)
    upper_share = np.where(offset < 0, (offset + width) / width, offset / width)
    slots = np.arange(groups + 2)[None, :]
    table = (1.0 - upper_share)[:, None] * (slots == lower[:, None]) + upper_share[:, None] * (
        slots == lower[:, None] + 1
    )
    return table.astype(np.float32)


def finish_weights(gram_matrix, projection, members):
    identity = jnp.eye(members, dtype=jnp.float32)
    system = gram_matrix + (members - 1.0) * identity
    bound = jnp.max(jnp.sum(jnp.abs(system), axis=2), axis=1)
    current = system / bound[:, None, None]
    inverse_root = jnp.broadcast_to(identity, system.shape)
    for sweep in range(NSI):
        factor = 1.5 * identity - 0.5 * jnp.einsum(
            "gij,gjk->gik", inverse_root, current, precision=highest
        )
        current = jnp.einsum("gij,gjk->gik", current, factor, precision=highest)
        inverse_root = jnp.einsum("gij,gjk->gik", factor, inverse_root, precision=highest)
    spread = inverse_root * jnp.sqrt((members - 1.0) / bound)[:, None, None]
    inner = jnp.einsum("gij,gj->gi", inverse_root, projection, precision=highest)
    centre = jnp.einsum("gij,gj->gi", inverse_root, inner, precision=highest) / bound[:, None]
    return spread + centre[:, :, None]


def join_tiles(items):
    return tuple((jnp.concatenate([entry[member] for entry in items], 0) for member in range(3)))


def along_lat(bundle):
    result = []
    for lat_off in range(-LAT_REACH, LAT_REACH + 1):
        if lat_off == 0:
            result.append(bundle)
        else:
            result.append(shifted((bundle[0], bundle[1], bundle[2]), "lat", -lat_off))
    return result


def along_lon(bundle):
    result = []
    for lon_off in range(-LON_REACH, LON_REACH + 1):
        if lon_off == 0:
            result.append(bundle)
        else:
            result.append(
                jax.tree.map(
                    lambda part, own: part.astype(own.dtype),
                    passed_along(as_sent(bundle), "lon", -lon_off),
                    bundle,
                )
            )
    return result


def local(
    anomalies,
    background_mean,
    obs_anom,
    innovation,
    obs_precision,
    obs_blocks,
    localization,
    loc_pattern,
):
    members = obs_anom.shape[2]
    obs_rows = obs_anom.shape[1]
    groups = localization.shape[1]
    tile_lon = anomalies.shape[1]
    live = jnp.arange(obs_rows, dtype=jnp.int32)[None, :] < obs_blocks * block_rows
    own = (obs_anom, innovation, obs_precision * live.astype(obs_precision.dtype))
    lat_count = 2 * LAT_REACH + 1
    lon_count = 2 * LON_REACH + 1
    pieces = []
    band = join_tiles(along_lat(own))
    beside_all = along_lon(band)
    for lat_idx in range(lat_count):
        for lon_idx in range(lon_count):
            pieces.append(tuple((entry[lat_idx] for entry in beside_all[lon_idx])))
    near_anom = jnp.concatenate([entry[0] for entry in pieces], 0)
    near_innovation = jnp.concatenate([entry[1] for entry in pieces], 0)
    near_precision = jnp.concatenate([entry[2] for entry in pieces], 0)
    local_weights = localization[0]
    pattern = loc_pattern[0]
    expanded = jnp.repeat(pattern, block_rows, axis=1).astype(jnp.float32)
    weights = local_weights * expanded * near_precision.astype(jnp.float32)[None, :]
    scaled = (near_anom[None, :, :] * weights[:, :, None]).astype(jnp.bfloat16)
    gram_matrix = jnp.einsum("gnk,nl->gkl", scaled, near_anom, preferred_element_type=jnp.float32)
    projection = jnp.einsum(
        "gnk,n->gk", scaled, near_innovation, preferred_element_type=jnp.float32
    )
    group_transform = finish_weights(gram_matrix, projection, members)
    edges = []
    for shift_by, chosen_group in ((1, groups - 1), (-1, 0)):
        edges.append(
            passed_along(
                group_transform[chosen_group].astype(jnp.bfloat16), "lon", shift_by
            ).astype(jnp.float32)
        )
    extended = jnp.concatenate([edges[0][None], group_transform, edges[1][None]], 0)
    table = jnp.asarray(blend_table(groups, tile_lon // groups), dtype=jnp.float32)
    column_weights = jnp.einsum("ce,eij->cij", table, extended, precision=highest).astype(
        jnp.bfloat16
    )
    moved = jnp.einsum(
        "acls,csk->aclk", anomalies, column_weights, preferred_element_type=jnp.float32
    )
    return (background_mean[..., None] + moved).astype(jnp.bfloat16)


def solution(mesh):
    in_specs = (
        P("lat", "lon", None, None),
        P("lat", "lon", None),
        P("lat", "lon", None),
        P("lat", "lon"),
        P("lat", "lon"),
        P("lat", "lon"),
        P("lat", "lon", None),
        P("lat", "lon", None),
    )
    out_specs = P("lat", "lon", None, None)
    return jax.shard_map(local, mesh=mesh, in_specs=in_specs, out_specs=out_specs, check_vma=False)
```

profile of v0, /device:TPU:64, one launch (start us, length us, event | category | flops | bytes accessed | tf_op | source)
XLA Modules:
  0.0 354.2 jit_solution(6062630413324961348)
XLA Ops:
  0.0 3.9 %collective-permute-start = (bf16[1,512,256]{2,1,0:T(8,128)(2,1)}, bf16[1,512,256]{2,1,0:T(8,128)(2,1)S(1)}, u32[]{:S(2)}, u32[]{:S(2)}) collective-permute-start(bf16[1,512,256]{2,1,0:T(8,128)(2,1)} %param.11), channel_id=1, source_target_pairs={{0,64},{64,128},{128,192},{192,256},{256,320},{320,384},{384,448},... | collective-permute-start | bytes 786440 | tf_op jit(solution)/shard_map/ppermute | solution.py:19
  4.0 2.0 collective-permute-start.1
  7.3 4.9 %collective-permute-start.7 = (bf16[1,512]{1,0:T(2,128)(2,1)S(1)}, bf16[1,512]{1,0:T(2,128)(2,1)S(1)}, u32[]{:S(2)}, u32[]{:S(2)}) collective-permute-start(bf16[1,512]{1,0:T(2,128)(2,1)S(1)} %get-tuple-element.30), channel_id=1, source_target_pairs={{64,0},{128,64},{192,128},{256,192},{320,256},{384,320},{448,384},... | collective-permute-start | bytes 3080 | tf_op jit(solution)/shard_map/ppermute | solution.py:19
  12.2 2.0 collective-permute-start.6
  14.2 3.9 %collective-permute-start.13 = (bf16[1,512]{1,0:T(2,128)(2,1)}, bf16[1,512]{1,0:T(2,128)(2,1)S(1)}, u32[]{:S(2)}, u32[]{:S(2)}) collective-permute-start(bf16[1,512]{1,0:T(2,128)(2,1)} %param.12), channel_id=1, source_target_pairs={{64,0},{128,64},{192,128},{256,192},{320,256},{384,320},{448,384},... | collective-permute-start | bytes 3080 | tf_op jit(solution)/shard_map/ppermute | solution.py:19
  20.3 3.2 collective-permute-start.12
  23.5 11.9 %collective-permute-start.8 = (bf16[3,512]{1,0:T(4,128)(2,1)S(1)}, bf16[3,512]{1,0:T(4,128)(2,1)S(1)}, u32[]{:S(2)}, u32[]{:S(2)}) collective-permute-start(bf16[3,512]{1,0:T(4,128)(2,1)S(1)} %pad_maximum_fusion.1), channel_id=1, source_target_pairs={{62,0},{63,1},{0,2},{1,3},{2,4},{3,5},{4,6},{5,7},{6,8},{7,9},{8,1... | collective-permute-start | bytes 9224 | tf_op jit(solution)/shard_map/ppermute | solution.py:33
  35.5 1.9 collective-permute-start.9
  37.4 16.6 %collective-permute-start.10 = (bf16[3,512]{1,0:T(4,128)(2,1)S(1)}, bf16[3,512]{1,0:T(4,128)(2,1)S(1)}, u32[]{:S(2)}, u32[]{:S(2)}) collective-permute-start(bf16[3,512]{1,0:T(4,128)(2,1)S(1)} %pad_maximum_fusion.1), channel_id=1, source_target_pairs={{1,0},{2,1},{3,2},{4,3},{5,4},{6,5},{7,6},{8,7},{9,8},{10,9},{11,1... | collective-permute-start | bytes 9224 | tf_op jit(solution)/shard_map/ppermute | solution.py:33
  54.8 2.6 collective-permute-start.11
  57.5 11.9 %collective-permute-start.14 = (bf16[3,512]{1,0:T(4,128)(2,1)S(1)}, bf16[3,512]{1,0:T(4,128)(2,1)S(1)}, u32[]{:S(2)}, u32[]{:S(2)}) collective-permute-start(bf16[3,512]{1,0:T(4,128)(2,1)S(1)} %pad_maximum_fusion.2), channel_id=1, source_target_pairs={{62,0},{63,1},{0,2},{1,3},{2,4},{3,5},{4,6},{5,7},{6,8},{7,9},{8,1... | collective-permute-start | bytes 9224 | tf_op jit(solution)/shard_map/ppermute | solution.py:33
  71.4 16.6 %collective-permute-start.16 = (bf16[3,512]{1,0:T(4,128)(2,1)S(1)}, bf16[3,512]{1,0:T(4,128)(2,1)S(1)}, u32[]{:S(2)}, u32[]{:S(2)}) collective-permute-start(bf16[3,512]{1,0:T(4,128)(2,1)S(1)} %pad_maximum_fusion.2), channel_id=1, source_target_pairs={{1,0},{2,1},{3,2},{4,3},{5,4},{6,5},{7,6},{8,7},{9,8},{10,9},{11,1... | collective-permute-start | bytes 9224 | tf_op jit(solution)/shard_map/ppermute | solution.py:33
  88.0 2.6 collective-permute-start.17
  91.8 11.9 %collective-permute-start.2 = (bf16[3,512,256]{2,1,0:T(8,128)(2,1)S(1)}, bf16[3,512,256]{2,1,0:T(8,128)(2,1)S(1)}, u32[]{:S(2)}, u32[]{:S(2)}) collective-permute-start(bf16[3,512,256]{2,1,0:T(8,128)(2,1)S(1)} %constant_dynamic-update-slice_fusion), channel_id=1, source_target_pairs={{62,0},{63,1},{0,2},{1,3},{2,4},{3,5},{4,6},{5,7},{6,8},{7,9},{8,1... | collective-permute-start | bytes 2359304 | tf_op jit(solution)/shard_map/ppermute | solution.py:33
  111.7 16.6 %collective-permute-start.4 = (bf16[3,512,256]{2,1,0:T(8,128)(2,1)S(1)}, bf16[3,512,256]{2,1,0:T(8,128)(2,1)S(1)}, u32[]{:S(2)}, u32[]{:S(2)}) collective-permute-start(bf16[3,512,256]{2,1,0:T(8,128)(2,1)S(1)} %constant_dynamic-update-slice_fusion), channel_id=1, source_target_pairs={{1,0},{2,1},{3,2},{4,3},{5,4},{6,5},{7,6},{8,7},{9,8},{10,9},{11,1... | collective-permute-start | bytes 2359304 | tf_op jit(solution)/shard_map/ppermute | solution.py:33
  128.3 2.8 collective-permute-start.5
  131.2 93.1 %collective-permute-done.2 = bf16[3,512,256]{2,1,0:T(8,128)(2,1)S(1)} collective-permute-done((bf16[3,512,256]{2,1,0:T(8,128)(2,1)S(1)}, bf16[3,512,256]{2,1,0:T(8,128)(2,1)S(1)}, u32[]{:S(2)}, u32[]{:S(2)}) %collective-permute-start.2) | collective-permute-done | bytes 786464 | tf_op jit(solution)/shard_map/ppermute | solution.py:33
  224.3 16.6 %collective-permute-done.3 = bf16[3,512,256]{2,1,0:T(8,128)(2,1)S(1)} collective-permute-done((bf16[3,512,256]{2,1,0:T(8,128)(2,1)S(1)}, bf16[3,512,256]{2,1,0:T(8,128)(2,1)S(1)}, u32[]{:S(2)}, u32[]{:S(2)}) %collective-permute-start.3) | collective-permute-done | bytes 786464 | tf_op jit(solution)/shard_map/ppermute | solution.py:33
  242.5 23.4 %collective-permute-done.5 = bf16[3,512,256]{2,1,0:T(8,128)(2,1)S(1)} collective-permute-done((bf16[3,512,256]{2,1,0:T(8,128)(2,1)S(1)}, bf16[3,512,256]{2,1,0:T(8,128)(2,1)S(1)}, u32[]{:S(2)}, u32[]{:S(2)}) %collective-permute-start.5) | collective-permute-done | bytes 786464 | tf_op jit(solution)/shard_map/ppermute | solution.py:33
  266.2 2.3 abs_reduce_fusion
  281.3 46.5 %collective-permute-start.19 = (bf16[256,256]{1,0:T(8,128)(2,1)S(1)}, bf16[256,256]{1,0:T(8,128)(2,1)S(1)}, u32[]{:S(2)}, u32[]{:S(2)}) collective-permute-start(bf16[256,256]{1,0:T(8,128)(2,1)S(1)} %get-tuple-element.32), channel_id=1, source_target_pairs={{1,0},{2,1},{3,2},{4,3},{5,4},{6,5},{7,6},{8,7},{9,8},{10,9},{11,1... | collective-permute-start | bytes 393224 | tf_op jit(solution)/shard_map/ppermute | solution.py:33
  327.7 2.1 collective-permute-start.18
  330.9 20.1 %collective-permute-done.18 = bf16[256,256]{1,0:T(8,128)(2,1)S(1)} collective-permute-done((bf16[256,256]{1,0:T(8,128)(2,1)S(1)}, bf16[256,256]{1,0:T(8,128)(2,1)S(1)}, u32[]{:S(2)}, u32[]{:S(2)}) %collective-permute-start.18) | collective-permute-done | bytes 131104 | tf_op jit(solution)/shard_map/ppermute | solution.py:33
  351.1 2.3 fusion.13
  (126 shorter events, 30.4 us)
Async XLA Ops:
  0.0 353.4 %copy-start = (bf16[2,4,16,256]{3,2,1,0:T(8,128)(2,1)S(1)}, bf16[2,4,16,256]{3,2,1,0:T(8,128)(2,1)}, u32[]{:S(2)}) copy-start(bf16[2,4,16,256]{3,2,1,0:T(8,128)(2,1)} %param.9) | copy-start | bytes 196612
  0.0 266.0 %copy-start.1 = (bf16[1,512,256]{2,1,0:T(8,128)(2,1)S(1)}, bf16[1,512,256]{2,1,0:T(8,128)(2,1)}, u32[]{:S(2)}) copy-start(bf16[1,512,256]{2,1,0:T(8,128)(2,1)} %param.11) | copy-start | bytes 786436
  0.0 90.7 %collective-permute-start = (bf16[1,512,256]{2,1,0:T(8,128)(2,1)}, bf16[1,512,256]{2,1,0:T(8,128)(2,1)S(1)}, u32[]{:S(2)}, u32[]{:S(2)}) collective-permute-start(bf16[1,512,256]{2,1,0:T(8,128)(2,1)} %param.11), channel_id=1, source_target_pairs={{0,64},{64,128},{128,192},{192,256},{256,320},{320,384},{384,448},... | collective-permute-start | bytes 786440 | tf_op jit(solution)/shard_map/ppermute | solution.py:19
  4.0 87.8 %collective-permute-start.1 = (bf16[1,512,256]{2,1,0:T(8,128)(2,1)}, bf16[1,512,256]{2,1,0:T(8,128)(2,1)S(1)}, u32[]{:S(2)}, u32[]{:S(2)}) collective-permute-start(bf16[1,512,256]{2,1,0:T(8,128)(2,1)} %param.11), channel_id=1, source_target_pairs={{64,0},{128,64},{192,128},{256,192},{320,256},{384,320},{448,384},... | collective-permute-start | bytes 786440 | tf_op jit(solution)/shard_map/ppermute | solution.py:19
  7.3 12.9 %collective-permute-start.7 = (bf16[1,512]{1,0:T(2,128)(2,1)S(1)}, bf16[1,512]{1,0:T(2,128)(2,1)S(1)}, u32[]{:S(2)}, u32[]{:S(2)}) collective-permute-start(bf16[1,512]{1,0:T(2,128)(2,1)S(1)} %get-tuple-element.30), channel_id=1, source_target_pairs={{64,0},{128,64},{192,128},{256,192},{320,256},{384,320},{448,384},... | collective-permute-start | bytes 3080 | tf_op jit(solution)/shard_map/ppermute | solution.py:19
  12.2 11.3 %collective-permute-start.6 = (bf16[1,512]{1,0:T(2,128)(2,1)S(1)}, bf16[1,512]{1,0:T(2,128)(2,1)S(1)}, u32[]{:S(2)}, u32[]{:S(2)}) collective-permute-start(bf16[1,512]{1,0:T(2,128)(2,1)S(1)} %get-tuple-element.30), channel_id=1, source_target_pairs={{0,64},{64,128},{128,192},{192,256},{256,320},{320,384},{384,448},... | collective-permute-start | bytes 3080 | tf_op jit(solution)/shard_map/ppermute | solution.py:19
  14.2 21.2 %collective-permute-start.13 = (bf16[1,512]{1,0:T(2,128)(2,1)}, bf16[1,512]{1,0:T(2,128)(2,1)S(1)}, u32[]{:S(2)}, u32[]{:S(2)}) collective-permute-start(bf16[1,512]{1,0:T(2,128)(2,1)} %param.12), channel_id=1, source_target_pairs={{64,0},{128,64},{192,128},{256,192},{320,256},{384,320},{448,384},... | collective-permute-start | bytes 3080 | tf_op jit(solution)/shard_map/ppermute | solution.py:19
  20.3 17.1 %collective-permute-start.12 = (bf16[1,512]{1,0:T(2,128)(2,1)}, bf16[1,512]{1,0:T(2,128)(2,1)S(1)}, u32[]{:S(2)}, u32[]{:S(2)}) collective-permute-start(bf16[1,512]{1,0:T(2,128)(2,1)} %param.12), channel_id=1, source_target_pairs={{0,64},{64,128},{128,192},{192,256},{256,320},{320,384},{384,448},... | collective-permute-start | bytes 3080 | tf_op jit(solution)/shard_map/ppermute | solution.py:19
  23.5 31.2 %collective-permute-start.8 = (bf16[3,512]{1,0:T(4,128)(2,1)S(1)}, bf16[3,512]{1,0:T(4,128)(2,1)S(1)}, u32[]{:S(2)}, u32[]{:S(2)}) collective-permute-start(bf16[3,512]{1,0:T(4,128)(2,1)S(1)} %pad_maximum_fusion.1), channel_id=1, source_target_pairs={{62,0},{63,1},{0,2},{1,3},{2,4},{3,5},{4,6},{5,7},{6,8},{7,9},{8,1... | collective-permute-start | bytes 9224 | tf_op jit(solution)/shard_map/ppermute | solution.py:33
  35.5 22.0 %collective-permute-start.9 = (bf16[3,512]{1,0:T(4,128)(2,1)S(1)}, bf16[3,512]{1,0:T(4,128)(2,1)S(1)}, u32[]{:S(2)}, u32[]{:S(2)}) collective-permute-start(bf16[3,512]{1,0:T(4,128)(2,1)S(1)} %pad_maximum_fusion.1), channel_id=1, source_target_pairs={{63,0},{0,1},{1,2},{2,3},{3,4},{4,5},{5,6},{6,7},{7,8},{8,9},{9,10... | collective-permute-start | bytes 9224 | tf_op jit(solution)/shard_map/ppermute | solution.py:33
  37.4 32.0 %collective-permute-start.10 = (bf16[3,512]{1,0:T(4,128)(2,1)S(1)}, bf16[3,512]{1,0:T(4,128)(2,1)S(1)}, u32[]{:S(2)}, u32[]{:S(2)}) collective-permute-start(bf16[3,512]{1,0:T(4,128)(2,1)S(1)} %pad_maximum_fusion.1), channel_id=1, source_target_pairs={{1,0},{2,1},{3,2},{4,3},{5,4},{6,5},{7,6},{8,7},{9,8},{10,9},{11,1... | collective-permute-start | bytes 9224 | tf_op jit(solution)/shard_map/ppermute | solution.py:33
  54.8 16.6 %collective-permute-start.11 = (bf16[3,512]{1,0:T(4,128)(2,1)S(1)}, bf16[3,512]{1,0:T(4,128)(2,1)S(1)}, u32[]{:S(2)}, u32[]{:S(2)}) collective-permute-start(bf16[3,512]{1,0:T(4,128)(2,1)S(1)} %pad_maximum_fusion.1), channel_id=1, source_target_pairs={{2,0},{3,1},{4,2},{5,3},{6,4},{7,5},{8,6},{9,7},{10,8},{11,9},{12,... | collective-permute-start | bytes 9224 | tf_op jit(solution)/shard_map/ppermute | solution.py:33
  57.5 30.6 %collective-permute-start.14 = (bf16[3,512]{1,0:T(4,128)(2,1)S(1)}, bf16[3,512]{1,0:T(4,128)(2,1)S(1)}, u32[]{:S(2)}, u32[]{:S(2)}) collective-permute-start(bf16[3,512]{1,0:T(4,128)(2,1)S(1)} %pad_maximum_fusion.2), channel_id=1, source_target_pairs={{62,0},{63,1},{0,2},{1,3},{2,4},{3,5},{4,6},{5,7},{6,8},{7,9},{8,1... | collective-permute-start | bytes 9224 | tf_op jit(solution)/shard_map/ppermute | solution.py:33
  69.4 34.3 %collective-permute-start.15 = (bf16[3,512]{1,0:T(4,128)(2,1)S(1)}, bf16[3,512]{1,0:T(4,128)(2,1)S(1)}, u32[]{:S(2)}, u32[]{:S(2)}) collective-permute-start(bf16[3,512]{1,0:T(4,128)(2,1)S(1)} %pad_maximum_fusion.2), channel_id=1, source_target_pairs={{63,0},{0,1},{1,2},{2,3},{3,4},{4,5},{5,6},{6,7},{7,8},{8,9},{9,10... | collective-permute-start | bytes 9224 | tf_op jit(solution)/shard_map/ppermute | solution.py:33
  71.4 32.3 %collective-permute-start.16 = (bf16[3,512]{1,0:T(4,128)(2,1)S(1)}, bf16[3,512]{1,0:T(4,128)(2,1)S(1)}, u32[]{:S(2)}, u32[]{:S(2)}) collective-permute-start(bf16[3,512]{1,0:T(4,128)(2,1)S(1)} %pad_maximum_fusion.2), channel_id=1, source_target_pairs={{1,0},{2,1},{3,2},{4,3},{5,4},{6,5},{7,6},{8,7},{9,8},{10,9},{11,1... | collective-permute-start | bytes 9224 | tf_op jit(solution)/shard_map/ppermute | solution.py:33
  88.0 19.6 %collective-permute-start.17 = (bf16[3,512]{1,0:T(4,128)(2,1)S(1)}, bf16[3,512]{1,0:T(4,128)(2,1)S(1)}, u32[]{:S(2)}, u32[]{:S(2)}) collective-permute-start(bf16[3,512]{1,0:T(4,128)(2,1)S(1)} %pad_maximum_fusion.2), channel_id=1, source_target_pairs={{2,0},{3,1},{4,2},{5,3},{6,4},{7,5},{8,6},{9,7},{10,8},{11,9},{12,... | collective-permute-start | bytes 9224 | tf_op jit(solution)/shard_map/ppermute | solution.py:33
  91.8 132.5 %collective-permute-start.2 = (bf16[3,512,256]{2,1,0:T(8,128)(2,1)S(1)}, bf16[3,512,256]{2,1,0:T(8,128)(2,1)S(1)}, u32[]{:S(2)}, u32[]{:S(2)}) collective-permute-start(bf16[3,512,256]{2,1,0:T(8,128)(2,1)S(1)} %constant_dynamic-update-slice_fusion), channel_id=1, source_target_pairs={{62,0},{63,1},{0,2},{1,3},{2,4},{3,5},{4,6},{5,7},{6,8},{7,9},{8,1... | collective-permute-start | bytes 2359304 | tf_op jit(solution)/shard_map/ppermute | solution.py:33
  105.7 135.2 %collective-permute-start.3 = (bf16[3,512,256]{2,1,0:T(8,128)(2,1)S(1)}, bf16[3,512,256]{2,1,0:T(8,128)(2,1)S(1)}, u32[]{:S(2)}, u32[]{:S(2)}) collective-permute-start(bf16[3,512,256]{2,1,0:T(8,128)(2,1)S(1)} %constant_dynamic-update-slice_fusion), channel_id=1, source_target_pairs={{63,0},{0,1},{1,2},{2,3},{3,4},{4,5},{5,6},{6,7},{7,8},{8,9},{9,10... | collective-permute-start | bytes 2359304 | tf_op jit(solution)/shard_map/ppermute | solution.py:33
  111.7 130.8 %collective-permute-start.4 = (bf16[3,512,256]{2,1,0:T(8,128)(2,1)S(1)}, bf16[3,512,256]{2,1,0:T(8,128)(2,1)S(1)}, u32[]{:S(2)}, u32[]{:S(2)}) collective-permute-start(bf16[3,512,256]{2,1,0:T(8,128)(2,1)S(1)} %constant_dynamic-update-slice_fusion), channel_id=1, source_target_pairs={{1,0},{2,1},{3,2},{4,3},{5,4},{6,5},{7,6},{8,7},{9,8},{10,9},{11,1... | collective-permute-start | bytes 2359304 | tf_op jit(solution)/shard_map/ppermute | solution.py:33
  128.3 137.6 %collective-permute-start.5 = (bf16[3,512,256]{2,1,0:T(8,128)(2,1)S(1)}, bf16[3,512,256]{2,1,0:T(8,128)(2,1)S(1)}, u32[]{:S(2)}, u32[]{:S(2)}) collective-permute-start(bf16[3,512,256]{2,1,0:T(8,128)(2,1)S(1)} %constant_dynamic-update-slice_fusion), channel_id=1, source_target_pairs={{2,0},{3,1},{4,2},{5,3},{6,4},{7,5},{8,6},{9,7},{10,8},{11,9},{12,... | collective-permute-start | bytes 2359304 | tf_op jit(solution)/shard_map/ppermute | solution.py:33
  276.7 51.1 %copy-start.4 = (f32[2,4,16]{2,1,0:T(4,128)S(1)}, f32[2,4,16]{2,1,0:T(4,128)}, u32[]{:S(2)}) copy-start(f32[2,4,16]{2,1,0:T(4,128)} %param.10) | copy-start | bytes 1540
  277.9 73.2 %copy-start.5 = (f32[4,3,1]{1,0,2:T(4,128)S(1)}, f32[4,3,1]{1,0,2:T(4,128)}, u32[]{:S(2)}) copy-start(f32[4,3,1]{1,0,2:T(4,128)} %constant.29) | copy-start | bytes 148
  281.3 49.6 %collective-permute-start.19 = (bf16[256,256]{1,0:T(8,128)(2,1)S(1)}, bf16[256,256]{1,0:T(8,128)(2,1)S(1)}, u32[]{:S(2)}, u32[]{:S(2)}) collective-permute-start(bf16[256,256]{1,0:T(8,128)(2,1)S(1)} %get-tuple-element.32), channel_id=1, source_target_pairs={{1,0},{2,1},{3,2},{4,3},{5,4},{6,5},{7,6},{8,7},{9,8},{10,9},{11,1... | collective-permute-start | bytes 393224 | tf_op jit(solution)/shard_map/ppermute | solution.py:33
  327.7 23.2 %collective-permute-start.18 = (bf16[256,256]{1,0:T(8,128)(2,1)S(1)}, bf16[256,256]{1,0:T(8,128)(2,1)S(1)}, u32[]{:S(2)}, u32[]{:S(2)}) collective-permute-start(bf16[256,256]{1,0:T(8,128)(2,1)S(1)} %get-tuple-element.32), channel_id=1, source_target_pairs={{63,0},{0,1},{1,2},{2,3},{3,4},{4,5},{5,6},{6,7},{7,8},{8,9},{9,10... | collective-permute-start | bytes 393224 | tf_op jit(solution)/shard_map/ppermute | solution.py:33
  (2 other events, 7.9 us)
where the time goes:
time: 355 us; the launch traced here: 354 us
  starting transfers between devices  168 us (47%)
  waiting for transfers between devices  156 us (44%)
  matrix products  15.2 us (4%)
  local copies, waits for them, and re-layouts  8.16 us (2%)
  other arithmetic  5.27 us (1%)
    ppermute x14, waiting for transfers between devices, passed_along(): return lax.ppermute(block, axis, route)  156 us
    ppermute x14, starting transfers between devices, passed_along(): return lax.ppermute(block, axis, route)  148 us
    ppermute x6, starting transfers between devices, shifted(): lax.ppermute(value, axis, [(source, source + steps) for source in range(l...  19.9 us
    unnamed x57, local copies, waits for them, and re-layouts  7.18 us
  transfers between devices with their start and end apart: 20, of which 6 were waited for; matrix products, arithmetic and copies ran while one was open for 3% of the time, Pallas kernels for 0%

commit v1 on v0

v1 whole, which is shorter than its diff:
```python
import jax
import jax.numpy as jnp
import numpy as np
from jax import lax
from jax.experimental import pallas as pl
from jax.experimental.pallas import tpu as pltpu
from jax.sharding import PartitionSpec as P

LAT_REACH = 1
LON_REACH = 2
NSI = 5
BLOCK_ROWS = 128
SIDE = 2
TEAM = 4
EXTRA = 16
VMEM_LIMIT = 40 * 1024 * 1024

ACROSS = (((1,), (1,)), ((), ()))
PLAIN = (((1,), (0,)), ((), ()))
VMEM = pl.BlockSpec(memory_space=pltpu.VMEM)
SMEM = pl.BlockSpec(memory_space=pltpu.SMEM)


def params():
    return pltpu.CompilerParams(vmem_limit_bytes=VMEM_LIMIT)


def dot(a, b, dims=PLAIN):
    return lax.dot_general(a, b, dims, preferred_element_type=jnp.float32)


def split(x):
    high = x.astype(jnp.bfloat16)
    return high, (x - high.astype(jnp.float32)).astype(jnp.bfloat16)


def dot3(a, b):
    return dot(a[0], b[0]) + (dot(a[0], b[1]) + dot(a[1], b[0]))


def prepare_kernel(blocks_ref, anom_ref, innov_ref, prec_ref, out_ref):
    rows = anom_ref.shape[0]
    members = anom_ref.shape[1]
    out_ref[pl.ds(0, members), :] = anom_ref[...].T
    lane = lax.broadcasted_iota(jnp.int32, (1, rows), 1)
    live = (lane < blocks_ref[0, 0] * BLOCK_ROWS).astype(jnp.float32)
    innov = innov_ref[...].astype(jnp.float32)
    prec = prec_ref[...].astype(jnp.float32) * live
    row = lax.broadcasted_iota(jnp.int32, (EXTRA, rows), 0)
    tail = jnp.where(row == 0, innov, jnp.where(row == 1, prec, 0.0))
    out_ref[pl.ds(members, EXTRA), :] = tail.astype(jnp.bfloat16)


def gram_kernel(side_ref, weight_ref, *refs):
    out_ref = refs[-1]
    tiles = refs[:-1]
    members = tiles[0].shape[0] - EXTRA
    half = members // 2
    side = side_ref[0, 0]

    def share(dest, count):
        total = None
        for place in range(count):
            tile = tiles[place]
            weight = weight_ref[dest, pl.ds(place, 1), :] * tile[pl.ds(members + 1, 1), :].astype(jnp.float32)
            scaled = (tile[...].astype(jnp.float32) * weight).astype(jnp.bfloat16)
            part = dot(scaled, tile[pl.ds(0, members), :], ACROSS)
            total = part if total is None else total + part
        return total

    row = lax.broadcasted_iota(jnp.int32, (half, half), 0)
    col = lax.broadcasted_iota(jnp.int32, (half, half), 1)
    edge_row = lax.broadcasted_iota(jnp.int32, (EXTRA, members), 0)
    for step in range(TEAM):
        far = step < SIDE
        dest = (SIDE * (1 - side) if far else SIDE * side) + step % SIDE
        total = share(dest, len(tiles) if far else len(tiles) // 2)
        first = total[:half, :half]
        last = total[half:members, half:]
        out_ref[dest, pl.ds(0, half), pl.ds(0, half)] = jnp.where(row <= col, first, last).astype(jnp.bfloat16)
        out_ref[dest, pl.ds(0, half), pl.ds(half, half)] = total[:half, half:].astype(jnp.bfloat16)
        diagonal = jnp.sum(jnp.where(row == col, last, 0.0), axis=0, keepdims=True)
        diagonal = jnp.concatenate([diagonal, diagonal], axis=1)
        projection = total[members:members + 1, :]
        tail = jnp.where(edge_row == 0, projection, jnp.where(edge_row == 1, diagonal, 0.0))
        out_ref[dest, pl.ds(half, EXTRA), :] = tail.astype(jnp.bfloat16)


def transform_kernel(part_ref, own_ref, core_ref, cross_ref, own_out, core_out, cross_out):
    members = part_ref.shape[2]
    half = members // 2
    total = part_ref[0].astype(jnp.float32)
    for index in range(1, TEAM):
        total = total + part_ref[index].astype(jnp.float32)
    mixed = total[:half, :half]
    beside = total[:half, half:]
    projection = total[half:half + 1, :]
    row = lax.broadcasted_iota(jnp.int32, (half, half), 0)
    col = lax.broadcasted_iota(jnp.int32, (half, half), 1)
    mixed_t = mixed.T
    first = jnp.where(row <= col, mixed, mixed_t)
    last = jnp.where(row == col, total[half + 1:half + 2, :half], jnp.where(row > col, mixed, mixed_t))
    gram = jnp.concatenate(
        [jnp.concatenate([first, beside], axis=1), jnp.concatenate([beside.T, last], axis=1)], axis=0
    )
    row = lax.broadcasted_iota(jnp.int32, (members, members), 0)
    col = lax.broadcasted_iota(jnp.int32, (members, members), 1)
    identity = (row == col).astype(jnp.float32)
    system = gram + (members - 1.0) * identity
    bound = jnp.max(jnp.sum(jnp.abs(system), axis=0, keepdims=True), axis=1, keepdims=True)
    current = system / bound
    inverse_root = None
    for sweep in range(NSI):
        if sweep == 0:
            factor = 1.5 * identity - 0.5 * current
            inverse_root = factor
        else:
            factor = 1.5 * identity - 0.5 * dot3(root_parts, split(current))
        factor_parts = split(factor)
        if sweep < NSI - 1:
            current = dot3(split(current), factor_parts)
        if sweep > 0:
            inverse_root = dot3(factor_parts, root_parts)
        root_parts = split(inverse_root)
    inner = dot3(split(jnp.broadcast_to(projection, (8, members))), root_parts)
    centre = dot3(split(inner), root_parts) / bound
    transform = inverse_root * jnp.sqrt((members - 1.0) / bound) + centre.T[:, 0:1]
    transform = transform.astype(jnp.bfloat16)
    own_out[...] = dot(own_ref[...], transform)
    core_out[...] = dot(core_ref[...], transform).astype(jnp.bfloat16)
    cross_out[...] = dot(cross_ref[...], transform).astype(jnp.bfloat16)


def shifts(lat_count, lon_count, move):
    pairs = []
    for lat in range(lat_count):
        for lon in range(lon_count):
            target = move(lat, lon)
            if target is not None:
                pairs.append((lat * lon_count + lon, target[0] * lon_count + target[1]))
    return pairs


def local(
    anomalies,
    background_mean,
    obs_anom,
    innovation,
    obs_precision,
    obs_blocks,
    localization,
    loc_pattern,
):
    members = obs_anom.shape[2]
    obs_rows = obs_anom.shape[1]
    tile_lat, tile_lon, levels, _ = anomalies.shape
    half = members // 2
    lat_count = lax.axis_size("lat")
    lon_count = lax.axis_size("lon")
    reach = 2 * LON_REACH + 1
    near_lat = 2 * LAT_REACH + 1
    place = lax.axis_index("lon") % TEAM
    side = place // SIDE
    even = place % 2 == 0

    def send(value, move):
        return lax.ppermute(value, ("lat", "lon"), shifts(lat_count, lon_count, move))

    def moved_by(lat_step, team_step):
        def move(lat, lon):
            target = lat + lat_step
            if not 0 <= target < lat_count:
                return None
            step = 0 if not team_step else (TEAM if lon % TEAM >= SIDE else -TEAM)
            return target, (lon + step) % lon_count

        return move

    own = pl.pallas_call(
        prepare_kernel,
        out_shape=jax.ShapeDtypeStruct((members + EXTRA, obs_rows), jnp.bfloat16),
        in_specs=[SMEM, VMEM, VMEM, VMEM],
        out_specs=VMEM,
        compiler_params=params(),
        name="prepare",
    )(obs_blocks, obs_anom[0], innovation, obs_precision)

    tiles = []
    for team_step in (0, 1):
        for lat_off in range(-LAT_REACH, LAT_REACH + 1):
            if lat_off == 0 and not team_step:
                tiles.append(own)
            else:
                tiles.append(send(own, moved_by(-lat_off, team_step)))

    pattern = jnp.repeat(loc_pattern[0], BLOCK_ROWS, axis=1).astype(jnp.float32)
    weights = (localization[0] * pattern).reshape(near_lat, reach, obs_rows)
    weights = jnp.pad(weights, ((0, 0), (3, 3), (0, 0)))
    weights = lax.dynamic_slice_in_dim(weights, 3 - place, 2 * TEAM, axis=1)
    order = ((2, 6), (3, 7), (4, 0), (5, 1))
    weights = jnp.stack([jnp.concatenate([weights[:, a], weights[:, b]], 0) for a, b in order])
    teams = [[team * TEAM + i for i in range(TEAM)] for team in range(lon_count // TEAM)]
    weights = lax.all_to_all(weights, "lon", 0, 0, axis_index_groups=teams, tiled=True)

    shares = pl.pallas_call(
        gram_kernel,
        out_shape=jax.ShapeDtypeStruct((TEAM, half + EXTRA, members), jnp.bfloat16),
        in_specs=[SMEM] + [VMEM] * (1 + len(tiles)),
        out_specs=VMEM,
        compiler_params=params(),
        name="gram",
    )(side.reshape(1, 1).astype(jnp.int32), weights, *tiles)

    def core_move(lat, lon):
        return lat, lon ^ 1

    def cross_move(lat, lon):
        return lat, (lon + (1 if lon % 2 else -1)) % lon_count

    left = anomalies[:, : tile_lon // 2].reshape(-1, members)
    right = anomalies[:, tile_lon // 2 :].reshape(-1, members)
    core_cols = send(jnp.where(even, right, left), core_move)
    cross_cols = send(jnp.where(even, left, right), cross_move)

    shares = lax.all_to_all(shares, "lon", 0, 0, axis_index_groups=teams, tiled=True)

    moved, core_back, cross_back = pl.pallas_call(
        transform_kernel,
        out_shape=(
            jax.ShapeDtypeStruct((tile_lat * tile_lon * levels, members), jnp.float32),
            jax.ShapeDtypeStruct(core_cols.shape, jnp.bfloat16),
            jax.ShapeDtypeStruct(cross_cols.shape, jnp.bfloat16),
        ),
        in_specs=[VMEM] * 4,
        out_specs=(VMEM, VMEM, VMEM),
        compiler_params=params(),
        name="transform",
    )(shares, anomalies.reshape(-1, members), core_cols, cross_cols)

    cross_back = send(cross_back, cross_move)
    core_back = send(core_back, core_move)
    offset = np.abs(np.arange(tile_lon) - (tile_lon - 1) / 2.0) / tile_lon
    other_share = jnp.asarray(offset, jnp.float32)[None, :, None, None]
    moved = moved.reshape(anomalies.shape)
    part = (tile_lat, tile_lon // 2, levels, members)
    from_left = jnp.where(even, cross_back, core_back).reshape(part)
    from_right = jnp.where(even, core_back, cross_back).reshape(part)
    others = jnp.concatenate([from_left, from_right], 1).astype(jnp.float32)
    total = background_mean[..., None] + (1.0 - other_share) * moved + other_share * others
    return total.astype(jnp.bfloat16)


def solution(mesh):
    in_specs = (
        P("lat", "lon", None, None),
        P("lat", "lon", None),
        P("lat", "lon", None),
        P("lat", "lon"),
        P("lat", "lon"),
        P("lat", "lon"),
        P("lat", "lon", None),
        P("lat", "lon", None),
    )
    out_specs = P("lat", "lon", None, None)
    return jax.shard_map(local, mesh=mesh, in_specs=in_specs, out_specs=out_specs, check_vma=False)
```

time: 355 us -> 108 us (0.30)
  the two profiles are of different devices: /device:TPU:64 before, /device:TPU:32 now
where the time goes in v1:
time: 108 us
  starting transfers between devices  61.2 us (57%)
  waiting for transfers between devices  33.9 us (31%)
  Pallas kernels  6.22 us (6%)
  local copies, waits for them, and re-layouts  3.95 us (4%)
  other arithmetic  1.53 us (1%)
    ppermute x9, starting transfers between devices, send(): lax.ppermute(value, ('lat', 'lon'), shifts(lat_count, lon_count, move))  45.9 us
    ppermute x9, waiting for transfers between devices, send(): lax.ppermute(value, ('lat', 'lon'), shifts(lat_count, lon_count, move))  21.1 us
    all_to_all x1, waiting for transfers between devices, local(): lax.all_to_all(weights, 'lon', 0, 0, axis_index_groups=teams, tiled=True)  12.8 us
    all_to_all x1, starting transfers between devices, local(): lax.all_to_all(weights, 'lon', 0, 0, axis_index_groups=teams, tiled=True)  11.8 us
    pallas_call x1, Pallas kernels, local(): pl.pallas_call(transform_kernel, out_shape=(jax.ShapeDtypeStruct((tile_la...  3.87 us
    unnamed x18, local copies, waits for them, and re-layouts  3.7 us
    all_to_all x1, starting transfers between devices, local(): lax.all_to_all(shares, 'lon', 0, 0, axis_index_groups=teams, tiled=True)  3.58 us
    pallas_call x1, Pallas kernels, local(): pl.pallas_call(gram_kernel, out_shape=jax.ShapeDtypeStruct((TEAM, half +...  2.24 us
  transfers between devices with their start and end apart: 11, of which 3 were waited for; matrix products, arithmetic and copies ran while one was open for 1% of the time, Pallas kernels for 0%

profile of v1, /device:TPU:32, one launch (start us, length us, event | category | flops | bytes accessed | tf_op | source)
XLA Modules:
  0.0 107.8 jit_solution(4766779351117009475)
XLA Ops:
  0.7 0.9 copy-done
  1.6 0.7 copy-done.3
  2.3 0.1 prepare.1.refs_1_
  2.4 3.8 %collective-permute-start = (bf16[272,512]{1,0:T(8,128)(2,1)S(1)}, bf16[272,512]{1,0:T(8,128)(2,1)S(1)}, u32[]{:S(2)}, u32[]{:S(2)}) collective-permute-start(bf16[272,512]{1,0:T(8,128)(2,1)S(1)} %prepare.1.refs_1_), channel_id=1, source_target_pairs={{0,64},{1,65},{2,66},{3,67},{4,68},{5,69},{6,70},{7,71},{8,72},{9,... | collective-permute-start | bytes 835592 | tf_op jit(solution)/shard_map/ppermute | solution.py:167
  6.3 4.9 %collective-permute-start.1 = (bf16[272,512]{1,0:T(8,128)(2,1)S(1)}, bf16[272,512]{1,0:T(8,128)(2,1)S(1)}, u32[]{:S(2)}, u32[]{:S(2)}) collective-permute-start(bf16[272,512]{1,0:T(8,128)(2,1)S(1)} %prepare.1.refs_1_), channel_id=1, source_target_pairs={{64,0},{65,1},{66,2},{67,3},{68,4},{69,5},{70,6},{71,7},{72,8},{73... | collective-permute-start | bytes 835592 | tf_op jit(solution)/shard_map/ppermute | solution.py:167
  11.2 5.6 %collective-permute-start.2 = (bf16[272,512]{1,0:T(8,128)(2,1)S(1)}, bf16[272,512]{1,0:T(8,128)(2,1)S(1)}, u32[]{:S(2)}, u32[]{:S(2)}) collective-permute-start(bf16[272,512]{1,0:T(8,128)(2,1)S(1)} %prepare.1.refs_1_), channel_id=1, source_target_pairs={{0,124},{1,125},{2,70},{3,71},{4,64},{5,65},{6,74},{7,75},{8,68},{... | collective-permute-start | bytes 835592 | tf_op jit(solution)/shard_map/ppermute | solution.py:167
  16.8 2.7 %collective-permute-start.3 = (bf16[272,512]{1,0:T(8,128)(2,1)S(1)}, bf16[272,512]{1,0:T(8,128)(2,1)S(1)}, u32[]{:S(2)}, u32[]{:S(2)}) collective-permute-start(bf16[272,512]{1,0:T(8,128)(2,1)S(1)} %prepare.1.refs_1_), channel_id=1, source_target_pairs={{0,60},{1,61},{2,6},{3,7},{4,0},{5,1},{6,10},{7,11},{8,4},{9,5},{1... | collective-permute-start | bytes 835592 | tf_op jit(solution)/shard_map/ppermute | solution.py:167
  19.5 2.0 %collective-permute-start.4 = (bf16[272,512]{1,0:T(8,128)(2,1)S(1)}, bf16[272,512]{1,0:T(8,128)(2,1)S(1)}, u32[]{:S(2)}, u32[]{:S(2)}) collective-permute-start(bf16[272,512]{1,0:T(8,128)(2,1)S(1)} %prepare.1.refs_1_), channel_id=1, source_target_pairs={{64,60},{65,61},{66,6},{67,7},{68,0},{69,1},{70,10},{71,11},{72,4}... | collective-permute-start | bytes 835592 | tf_op jit(solution)/shard_map/ppermute | solution.py:167
  21.6 0.6 copy-done.8
  22.5 0.7 copy-done.4
  23.4 0.6 pad_maximum_fusion
  24.0 11.8 %all-to-all-start = ((f32[4,6,512]{2,1,0:T(8,128)}), f32[4,6,512]{2,1,0:T(8,128)S(1)}, u32[]{:S(2)}, u32[]{:S(2)}) async-start(f32[4,6,512]{2,1,0:T(8,128)} %pad_maximum_fusion), calls=%async_computation | async-start | bytes 131072 | tf_op jit(solution)/shard_map/all_to_all | solution.py:203
  35.8 12.8 %all-to-all-done.weight_ref = f32[4,6,512]{2,1,0:T(8,128)S(1)} async-done(((f32[4,6,512]{2,1,0:T(8,128)}), f32[4,6,512]{2,1,0:T(8,128)S(1)}, u32[]{:S(2)}, u32[]{:S(2)}) %all-to-all-start) | async-done | bytes 49184 | tf_op jit(solution)/shard_map/all_to_all | solution.py:203
  48.7 2.2 %gram.1 = bf16[4,144,256]{2,1,0:T(8,128)(2,1)} custom-call(s32[1,1]{1,0:T(1,128)} %bitcast.side_ref, f32[4,6,512]{2,1,0:T(8,128)S(1)} %all-to-all-done.weight_ref, bf16[272,512]{1,0:T(8,128)(2,1)S(1)} %collective-permute-done.refs_0_, bf16[272,512]{1,0:T(8,128)(2,1)S(1)} %prepare.1.refs_1_, bf16[272,512]{1,0:T(8,128)(2,1)S(1)} %collective-permute-done.1.refs_2_, ...), custom_call_target="tpu_custom_call" | custom-call | tf_op jit(solution)/shard_map/gram/pallas_call | solution.py:205
  51.0 3.6 %all-to-all-start.1 = ((bf16[4,144,256]{2,1,0:T(8,128)(2,1)}), bf16[4,144,256]{2,1,0:T(8,128)(2,1)S(1)}, u32[]{:S(2)}, u32[]{:S(2)}) async-start(bf16[4,144,256]{2,1,0:T(8,128)(2,1)} %gram.1), calls=%async_computation.1 | async-start | bytes 589824 | tf_op jit(solution)/shard_map/all_to_all | solution.py:225
  54.6 2.4 %collective-permute-start.5 = (bf16[64,256]{1,0:T(8,128)(2,1)S(1)}, bf16[64,256]{1,0:T(8,128)(2,1)S(1)}, u32[]{:S(2)}, u32[]{:S(2)}) collective-permute-start(bf16[64,256]{1,0:T(8,128)(2,1)S(1)} %bitcast.40), channel_id=1, source_target_pairs={{0,1},{1,0},{2,3},{3,2},{4,5},{5,4},{6,7},{7,6},{8,9},{9,8},{10,11... | collective-permute-start | bytes 98312 | tf_op jit(solution)/shard_map/ppermute | solution.py:167
  56.9 15.8 %collective-permute-start.6 = (bf16[64,256]{1,0:T(8,128)(2,1)S(1)}, bf16[64,256]{1,0:T(8,128)(2,1)S(1)}, u32[]{:S(2)}, u32[]{:S(2)}) collective-permute-start(bf16[64,256]{1,0:T(8,128)(2,1)S(1)} %bitcast.39), channel_id=1, source_target_pairs={{0,63},{1,2},{2,1},{3,4},{4,3},{5,6},{6,5},{7,8},{8,7},{9,10},{10,... | collective-permute-start | bytes 98312 | tf_op jit(solution)/shard_map/ppermute | solution.py:167
  72.8 11.5 %collective-permute-done.6.cross_ref = bf16[64,256]{1,0:T(8,128)(2,1)S(1)} collective-permute-done((bf16[64,256]{1,0:T(8,128)(2,1)S(1)}, bf16[64,256]{1,0:T(8,128)(2,1)S(1)}, u32[]{:S(2)}, u32[]{:S(2)}) %collective-permute-start.6) | collective-permute-done | bytes 32800 | tf_op jit(solution)/shard_map/ppermute | solution.py:167
  84.3 3.9 %transform.1 = (f32[128,256]{1,0:T(8,128)S(1)}, bf16[64,256]{1,0:T(8,128)(2,1)S(1)}, bf16[64,256]{1,0:T(8,128)(2,1)S(1)}) custom-call(bf16[4,144,256]{2,1,0:T(8,128)(2,1)S(1)} %all-to-all-done.1.part_ref, bf16[128,256]{1,0:T(8,128)(2,1)S(1)} %bitcast.35, bf16[64,256]{1,0:T(8,128)(2,1)S(1)} %collective-permute-done.5.core_ref, ...), custom_call_target="tpu_custom_call" | custom-call | tf_op jit(solution)/shard_map/transform/pallas_call | solution.py:227
  88.2 6.7 %collective-permute-start.7 = (bf16[64,256]{1,0:T(8,128)(2,1)S(1)}, bf16[64,256]{1,0:T(8,128)(2,1)S(1)}, u32[]{:S(2)}, u32[]{:S(2)}) collective-permute-start(bf16[64,256]{1,0:T(8,128)(2,1)S(1)} %get-tuple-element.9), channel_id=1, source_target_pairs={{0,63},{1,2},{2,1},{3,4},{4,3},{5,6},{6,5},{7,8},{8,7},{9,10},{10,... | collective-permute-start | bytes 98312 | tf_op jit(solution)/shard_map/ppermute | solution.py:167
  94.8 1.9 %collective-permute-start.8 = (bf16[64,256]{1,0:T(8,128)(2,1)S(1)}, bf16[64,256]{1,0:T(8,128)(2,1)S(1)}, u32[]{:S(2)}, u32[]{:S(2)}) collective-permute-start(bf16[64,256]{1,0:T(8,128)(2,1)S(1)} %get-tuple-element.10), channel_id=1, source_target_pairs={{0,1},{1,0},{2,3},{3,2},{4,5},{5,4},{6,7},{7,6},{8,9},{9,8},{10,11... | collective-permute-start | bytes 98312 | tf_op jit(solution)/shard_map/ppermute | solution.py:167
  96.8 9.6 %collective-permute-done.7 = bf16[64,256]{1,0:T(8,128)(2,1)S(1)} collective-permute-done((bf16[64,256]{1,0:T(8,128)(2,1)S(1)}, bf16[64,256]{1,0:T(8,128)(2,1)S(1)}, u32[]{:S(2)}, u32[]{:S(2)}) %collective-permute-start.7) | collective-permute-done | bytes 32800 | tf_op jit(solution)/shard_map/ppermute | solution.py:167
  106.4 0.7 copy-done.5
  107.1 0.7 add_convert_fusion
  (34 shorter events, 0.5 us)
Async XLA Ops:
  0.0 0.7 copy-start.2
  0.7 0.9 copy-start
  1.6 0.7 copy-start.3
  2.4 46.2 %collective-permute-start = (bf16[272,512]{1,0:T(8,128)(2,1)S(1)}, bf16[272,512]{1,0:T(8,128)(2,1)S(1)}, u32[]{:S(2)}, u32[]{:S(2)}) collective-permute-start(bf16[272,512]{1,0:T(8,128)(2,1)S(1)} %prepare.1.refs_1_), channel_id=1, source_target_pairs={{0,64},{1,65},{2,66},{3,67},{4,68},{5,69},{6,70},{7,71},{8,72},{9,... | collective-permute-start | bytes 835592 | tf_op jit(solution)/shard_map/ppermute | solution.py:167
  6.3 42.4 %collective-permute-start.1 = (bf16[272,512]{1,0:T(8,128)(2,1)S(1)}, bf16[272,512]{1,0:T(8,128)(2,1)S(1)}, u32[]{:S(2)}, u32[]{:S(2)}) collective-permute-start(bf16[272,512]{1,0:T(8,128)(2,1)S(1)} %prepare.1.refs_1_), channel_id=1, source_target_pairs={{64,0},{65,1},{66,2},{67,3},{68,4},{69,5},{70,6},{71,7},{72,8},{73... | collective-permute-start | bytes 835592 | tf_op jit(solution)/shard_map/ppermute | solution.py:167
  11.2 37.5 %collective-permute-start.2 = (bf16[272,512]{1,0:T(8,128)(2,1)S(1)}, bf16[272,512]{1,0:T(8,128)(2,1)S(1)}, u32[]{:S(2)}, u32[]{:S(2)}) collective-permute-start(bf16[272,512]{1,0:T(8,128)(2,1)S(1)} %prepare.1.refs_1_), channel_id=1, source_target_pairs={{0,124},{1,125},{2,70},{3,71},{4,64},{5,65},{6,74},{7,75},{8,68},{... | collective-permute-start | bytes 835592 | tf_op jit(solution)/shard_map/ppermute | solution.py:167
  16.8 31.9 %collective-permute-start.3 = (bf16[272,512]{1,0:T(8,128)(2,1)S(1)}, bf16[272,512]{1,0:T(8,128)(2,1)S(1)}, u32[]{:S(2)}, u32[]{:S(2)}) collective-permute-start(bf16[272,512]{1,0:T(8,128)(2,1)S(1)} %prepare.1.refs_1_), channel_id=1, source_target_pairs={{0,60},{1,61},{2,6},{3,7},{4,0},{5,1},{6,10},{7,11},{8,4},{9,5},{1... | collective-permute-start | bytes 835592 | tf_op jit(solution)/shard_map/ppermute | solution.py:167
  19.5 29.2 %collective-permute-start.4 = (bf16[272,512]{1,0:T(8,128)(2,1)S(1)}, bf16[272,512]{1,0:T(8,128)(2,1)S(1)}, u32[]{:S(2)}, u32[]{:S(2)}) collective-permute-start(bf16[272,512]{1,0:T(8,128)(2,1)S(1)} %prepare.1.refs_1_), channel_id=1, source_target_pairs={{64,60},{65,61},{66,6},{67,7},{68,0},{69,1},{70,10},{71,11},{72,4}... | collective-permute-start | bytes 835592 | tf_op jit(solution)/shard_map/ppermute | solution.py:167
  21.6 0.7 copy-start.8
  22.4 0.8 copy-start.4
  24.0 24.6 %all-to-all-start = ((f32[4,6,512]{2,1,0:T(8,128)}), f32[4,6,512]{2,1,0:T(8,128)S(1)}, u32[]{:S(2)}, u32[]{:S(2)}) async-start(f32[4,6,512]{2,1,0:T(8,128)} %pad_maximum_fusion), calls=%async_computation | async-start | bytes 131072 | tf_op jit(solution)/shard_map/all_to_all | solution.py:203
  51.0 3.6 %copy-start.1 = (bf16[2,4,16,256]{3,2,1,0:T(8,128)(2,1)S(1)}, bf16[2,4,16,256]{3,2,1,0:T(8,128)(2,1)}, u32[]{:S(2)}) copy-start(bf16[2,4,16,256]{3,2,1,0:T(8,128)(2,1)} %param.9) | copy-start | bytes 196612
  51.0 33.3 %all-to-all-start.1 = ((bf16[4,144,256]{2,1,0:T(8,128)(2,1)}), bf16[4,144,256]{2,1,0:T(8,128)(2,1)S(1)}, u32[]{:S(2)}, u32[]{:S(2)}) async-start(bf16[4,144,256]{2,1,0:T(8,128)(2,1)} %gram.1), calls=%async_computation.1 | async-start | bytes 589824 | tf_op jit(solution)/shard_map/all_to_all | solution.py:225
  54.6 18.2 %collective-permute-start.5 = (bf16[64,256]{1,0:T(8,128)(2,1)S(1)}, bf16[64,256]{1,0:T(8,128)(2,1)S(1)}, u32[]{:S(2)}, u32[]{:S(2)}) collective-permute-start(bf16[64,256]{1,0:T(8,128)(2,1)S(1)} %bitcast.40), channel_id=1, source_target_pairs={{0,1},{1,0},{2,3},{3,2},{4,5},{5,4},{6,7},{7,6},{8,9},{9,8},{10,11... | collective-permute-start | bytes 98312 | tf_op jit(solution)/shard_map/ppermute | solution.py:167
  56.9 27.3 %collective-permute-start.6 = (bf16[64,256]{1,0:T(8,128)(2,1)S(1)}, bf16[64,256]{1,0:T(8,128)(2,1)S(1)}, u32[]{:S(2)}, u32[]{:S(2)}) collective-permute-start(bf16[64,256]{1,0:T(8,128)(2,1)S(1)} %bitcast.39), channel_id=1, source_target_pairs={{0,63},{1,2},{2,1},{3,4},{4,3},{5,6},{6,5},{7,8},{8,7},{9,10},{10,... | collective-permute-start | bytes 98312 | tf_op jit(solution)/shard_map/ppermute | solution.py:167
  88.2 18.2 %collective-permute-start.7 = (bf16[64,256]{1,0:T(8,128)(2,1)S(1)}, bf16[64,256]{1,0:T(8,128)(2,1)S(1)}, u32[]{:S(2)}, u32[]{:S(2)}) collective-permute-start(bf16[64,256]{1,0:T(8,128)(2,1)S(1)} %get-tuple-element.9), channel_id=1, source_target_pairs={{0,63},{1,2},{2,1},{3,4},{4,3},{5,6},{6,5},{7,8},{8,7},{9,10},{10,... | collective-permute-start | bytes 98312 | tf_op jit(solution)/shard_map/ppermute | solution.py:167
  94.8 11.5 %collective-permute-start.8 = (bf16[64,256]{1,0:T(8,128)(2,1)S(1)}, bf16[64,256]{1,0:T(8,128)(2,1)S(1)}, u32[]{:S(2)}, u32[]{:S(2)}) collective-permute-start(bf16[64,256]{1,0:T(8,128)(2,1)S(1)} %get-tuple-element.10), channel_id=1, source_target_pairs={{0,1},{1,0},{2,3},{3,2},{4,5},{5,4},{6,7},{7,6},{8,9},{9,8},{10,11... | collective-permute-start | bytes 98312 | tf_op jit(solution)/shard_map/ppermute | solution.py:167
  106.4 0.7 copy-start.5
  106.4 0.7 copy-start.6
  106.4 0.7 copy-start.7

commit v2 on v1

v2 whole, which is shorter than its diff:
```python
import jax
import jax.numpy as jnp
from jax import lax
from jax.experimental import pallas as pl
from jax.experimental.pallas import tpu as pltpu
from jax.sharding import PartitionSpec as P

LAT_REACH = 1
LON_REACH = 2
NEAR_LAT = 2 * LAT_REACH + 1
NEAR_LON = 2 * LON_REACH + 1
NSI = 5
BLOCK_ROWS = 128
SIDE = 2
TEAM = 4
EXTRA = 16
VMEM_LIMIT = 40 * 1024 * 1024

ACROSS = (((1,), (1,)), ((), ()))
PLAIN = (((1,), (0,)), ((), ()))
VMEM = pl.BlockSpec(memory_space=pltpu.VMEM)
SMEM = pl.BlockSpec(memory_space=pltpu.SMEM)
ANY = pl.BlockSpec(memory_space=pl.ANY)


def dot(a, b, dims=PLAIN):
    return lax.dot_general(a, b, dims, preferred_element_type=jnp.float32)


def split(x):
    high = x.astype(jnp.bfloat16)
    return high, (x - high.astype(jnp.float32)).astype(jnp.bfloat16)


def dot3(a, b):
    return dot(a[0], b[0]) + (dot(a[0], b[1]) + dot(a[1], b[0]))


def prepare_kernel(
    place_ref,
    blocks_ref,
    pattern_ref,
    anom_hbm,
    innov_hbm,
    prec_hbm,
    local_hbm,
    tile_ref,
    pack_ref,
    anom_ref,
    innov_ref,
    prec_ref,
    local_ref,
    weight_ref,
    sems,
):
    copies = []
    for index, (source, target) in enumerate(
        ((local_hbm, local_ref), (innov_hbm, innov_ref), (prec_hbm, prec_ref), (anom_hbm, anom_ref))
    ):
        copies.append(pltpu.make_async_copy(source, target, sems.at[index]))
        copies[-1].start()
    rows, members = anom_ref.shape
    place = place_ref[0, 0]
    blocks = rows // BLOCK_ROWS
    copies[0].wait()

    def weights(tiles):
        for kind, offset in enumerate(tiles):
            inside = (offset >= -LON_REACH) & (offset <= LON_REACH)
            offset = jnp.clip(offset, -LON_REACH, LON_REACH) + LON_REACH
            for lat in range(NEAR_LAT):
                near = lat * NEAR_LON + offset
                for block in range(blocks):
                    used = jnp.where(inside, pattern_ref[0, near * blocks + block], 0).astype(jnp.float32)
                    start = pl.multiple_of((near * blocks + block) * BLOCK_ROWS, BLOCK_ROWS)
                    weight_ref[pl.ds(kind * NEAR_LAT + lat, 1), pl.ds(block * BLOCK_ROWS, BLOCK_ROWS)] = (
                        local_ref[:, pl.ds(start, BLOCK_ROWS)] * used
                    )
        return weight_ref[...]

    weight_ref[...] = jnp.zeros_like(weight_ref)
    for reader in range(TEAM):
        beside = reader + (-TEAM if reader >= SIDE else TEAM)
        pack_ref[reader] = jnp.concatenate(split(weights((reader - place, beside - place))), axis=0)

    high, low = split(weights((0 * place, 1 - 2 * (place % 2))))
    copies[1].wait()
    copies[2].wait()
    lane = lax.broadcasted_iota(jnp.int32, (1, rows), 1)
    live = (lane < blocks_ref[0, 0] * BLOCK_ROWS).astype(jnp.float32)
    innov = innov_ref[...].astype(jnp.float32)
    prec = prec_ref[...].astype(jnp.float32) * live
    used = 2 * NEAR_LAT
    tail = [innov, prec, high.astype(jnp.float32)[:used], low.astype(jnp.float32)[:used]]
    tail.append(jnp.zeros((EXTRA - 2 - 2 * used, rows), jnp.float32))
    tile_ref[pl.ds(members, EXTRA), :] = jnp.concatenate(tail, axis=0).astype(jnp.bfloat16)
    copies[3].wait()
    tile_ref[pl.ds(0, members), :] = anom_ref[...].T


def pack_weights(pack_ref, dest):
    parts = pack_ref[dest].astype(jnp.float32)
    return parts[: EXTRA // 2] + parts[EXTRA // 2 :]


def outer_weights(place_ref, beside_ref, forward_ref):
    members = beside_ref.shape[0] - EXTRA
    place = place_ref[0, 0]
    used = 2 * NEAR_LAT
    direct = beside_ref[pl.ds(members, EXTRA), :].astype(jnp.float32)[2 : 2 + 2 * used]
    passed = forward_ref[...].astype(jnp.float32)[2 : 2 + 2 * used]
    outer = (place == 0) | (place == TEAM - 1)
    direct = direct[:NEAR_LAT] + direct[used : used + NEAR_LAT]
    passed = passed[NEAR_LAT:used] + passed[used + NEAR_LAT :]
    return jnp.where(outer, direct, passed)


def weighted(tile_ref, weight):
    members = tile_ref.shape[0] - EXTRA
    prec = tile_ref[pl.ds(members, EXTRA), :].astype(jnp.float32)[1:2]
    scaled = (tile_ref[...].astype(jnp.float32) * (weight * prec)).astype(jnp.bfloat16)
    return dot(scaled, tile_ref[pl.ds(0, members), :], ACROSS)


def early_kernel(place_ref, pack_ref, forward_ref, own_ref, below_ref, above_ref, beside_ref, out_ref):
    far = SIDE - place_ref[0, 0] // SIDE * SIDE
    for dest in range(TEAM):
        weight = pack_weights(pack_ref, dest)
        total = None
        for lat, tile_ref in enumerate((below_ref, own_ref, above_ref)):
            part = weighted(tile_ref, weight[lat : lat + 1])
            total = part if total is None else total + part
        out_ref[dest] = total
    row = NEAR_LAT + LAT_REACH
    for step in range(SIDE):
        weight = pack_weights(pack_ref, far + step)[row : row + 1]
        out_ref[far + step] += weighted(beside_ref, weight)
    weight = outer_weights(place_ref, beside_ref, forward_ref)
    out_ref[TEAM] = weighted(beside_ref, weight[LAT_REACH : LAT_REACH + 1])


def late_kernel(
    place_ref, pack_ref, forward_ref, beside_ref, below_ref, above_ref, share_ref, out_ref, side_ref, total_ref
):
    members = share_ref.shape[2]
    half = members // 2
    side = place_ref[0, 0] // SIDE
    far = SIDE - side * SIDE
    tiles = ((0, below_ref), (2 * LAT_REACH, above_ref))
    for step in range(SIDE):
        weight = pack_weights(pack_ref, far + step)
        total = share_ref[far + step]
        for lat, tile_ref in tiles:
            row = NEAR_LAT + lat
            total = total + weighted(tile_ref, weight[row : row + 1])
        total_ref[far + step] = total
        total_ref[SIDE - far + step] = share_ref[SIDE - far + step]
    weight = outer_weights(place_ref, beside_ref, forward_ref)
    total = share_ref[TEAM]
    for lat, tile_ref in tiles:
        total = total + weighted(tile_ref, weight[lat : lat + 1])
    total_ref[TEAM] = total

    row = lax.broadcasted_iota(jnp.int32, (half, half), 0)
    col = lax.broadcasted_iota(jnp.int32, (half, half), 1)

    def packed(total):
        first = total[:half, :half]
        last = total[half:members, half:]
        diagonal = jnp.sum(jnp.where(row == col, last, 0.0), axis=0, keepdims=True)
        body = jnp.concatenate([jnp.where(row <= col, first, last), total[:half, half:]], axis=1)
        tail = jnp.concatenate([total[members : members + 1], jnp.concatenate([diagonal, diagonal], axis=1)], axis=0)
        return body.astype(jnp.bfloat16), tail

    def padded(tails):
        rows = sum(tail.shape[0] for tail in tails)
        zeros = jnp.zeros((EXTRA - rows, members), jnp.float32)
        return jnp.concatenate([*tails, zeros], axis=0).astype(jnp.bfloat16)

    group = [packed(total_ref[dest]) for dest in range(TEAM)]
    outer = packed(total_ref[TEAM])

    def write(reader, parts):
        for slot, (body, _) in enumerate(parts):
            out_ref[reader, pl.ds(slot * half, half), :] = body
        out_ref[reader, pl.ds(members, EXTRA), :] = padded([tail for _, tail in parts])

    def write_side(part):
        side_ref[pl.ds(0, half), :] = part[0]
        side_ref[pl.ds(half, EXTRA), :] = padded([part[1]])

    nothing = tuple(jnp.zeros_like(part) for part in outer)
    write(1, (group[1], group[2]))
    write(2, (group[1], group[2]))

    @pl.when(side == 0)
    def _():
        write(0, (nothing, group[0]))
        write(3, (group[3], outer))
        write_side(group[3])

    @pl.when(side == 1)
    def _():
        write(0, (outer, group[0]))
        write(3, (group[3], nothing))
        write_side(group[0])


def transform_kernel(place_ref, part_ref, same_ref, other_ref, self_out, outer_out):
    members = part_ref.shape[2]
    half = members // 2
    place = place_ref[0, 0]
    total = part_ref[0].astype(jnp.float32)
    for index in range(1, TEAM):
        total = total + part_ref[index].astype(jnp.float32)
    side = same_ref[...].astype(jnp.float32) + other_ref[...].astype(jnp.float32)
    row = lax.broadcasted_iota(jnp.int32, (half, half), 0)
    col = lax.broadcasted_iota(jnp.int32, (half, half), 1)
    upper = row <= col
    diagonal = row == col
    full_row = lax.broadcasted_iota(jnp.int32, (members, members), 0)
    full_col = lax.broadcasted_iota(jnp.int32, (members, members), 1)
    identity = (full_row == full_col).astype(jnp.float32)

    systems, projections, bounds = [], [], []
    for slot in range(2):
        mine = (place < SIDE) if slot == 0 else (place >= SIDE)
        extra = jnp.where(mine, side, 0.0)
        body = total[slot * half : (slot + 1) * half] + extra[:half]
        tail = total[members + 2 * slot : members + 2 * slot + 2] + extra[half : half + 2]
        mixed = body[:, :half]
        beside = body[:, half:]
        mixed_t = mixed.T
        first = jnp.where(upper, mixed, mixed_t)
        last = jnp.where(diagonal, tail[1:2, :half], jnp.where(upper, mixed_t, mixed))
        gram = jnp.concatenate(
            [jnp.concatenate([first, beside], axis=1), jnp.concatenate([beside.T, last], axis=1)], axis=0
        )
        system = gram + (members - 1.0) * identity
        bound = jnp.max(jnp.sum(jnp.abs(system), axis=0, keepdims=True), axis=1, keepdims=True)
        systems.append(system / bound)
        projections.append(tail[0:1])
        bounds.append(bound)

    current = systems
    factor = [1.5 * identity - 0.5 * x for x in current]
    parts = [split(x) for x in factor]
    roots = parts
    for sweep in range(1, NSI):
        current = [dot3(split(x), f) for x, f in zip(current, parts)]
        factor = [1.5 * identity - 0.5 * dot3(r, split(x)) for r, x in zip(roots, current)]
        parts = [split(x) for x in factor]
        inverse_root = [dot3(f, r) for f, r in zip(parts, roots)]
        roots = [split(x) for x in inverse_root]
    transforms = []
    for root, parts, projection, bound in zip(inverse_root, roots, projections, bounds):
        inner = dot3(split(jnp.broadcast_to(projection, (8, members))), parts)
        centre = dot3(split(inner), parts) / bound
        transforms.append(root * jnp.sqrt((members - 1.0) / bound) + centre.T[:, 0:1])
    even = place % 2 == 0
    self_out[...] = jnp.where(even, transforms[1], transforms[0]).astype(jnp.bfloat16)
    outer_out[...] = jnp.where(even, transforms[0], transforms[1]).astype(jnp.bfloat16)


def other_shares(width):
    return [abs(column - (width - 1) / 2.0) / width for column in range(width)]


def moved_columns(state_ref, columns, transform_ref):
    tile_lat, _, levels, members = state_ref.shape
    rows = state_ref[:, columns].reshape(tile_lat * (columns.stop - columns.start) * levels, members)
    return dot(rows, transform_ref[...]).reshape(tile_lat, -1, levels, members)


def product_kernel(place_ref, self_ref, outer_ref, base_ref, state_ref, out_ref):
    width = state_ref.shape[1]
    half = width // 2
    shares = other_shares(width)
    moved = moved_columns(state_ref, slice(0, width), self_ref)

    def write(outer):
        beside = moved_columns(state_ref, outer, outer_ref)
        for column, other in enumerate(shares):
            value = base_ref[:, column] + (1.0 - other) * moved[:, column]
            if outer.start <= column < outer.stop:
                value = value + other * beside[:, column - outer.start]
            out_ref[:, column] = value

    even = place_ref[0, 0] % 2 == 0

    @pl.when(even)
    def _():
        write(slice(0, half))

    @pl.when(jnp.logical_not(even))
    def _():
        write(slice(half, width))


def blend_kernel(place_ref, inner_ref, part_ref, state_ref, out_ref):
    width = state_ref.shape[1]
    half = width // 2
    shares = other_shares(width)

    def write(inner):
        beside = moved_columns(state_ref, inner, inner_ref)
        for column, other in enumerate(shares):
            value = part_ref[:, column]
            if inner.start <= column < inner.stop:
                value = value + other * beside[:, column - inner.start]
            out_ref[:, column] = value.astype(jnp.bfloat16)

    even = place_ref[0, 0] % 2 == 0

    @pl.when(even)
    def _():
        write(slice(half, width))

    @pl.when(jnp.logical_not(even))
    def _():
        write(slice(0, half))


def shifts(lat_count, lon_count, move):
    pairs = []
    for lat in range(lat_count):
        for lon in range(lon_count):
            target = move(lat, lon)
            if target is not None and 0 <= target[0] < lat_count:
                pairs.append((lat * lon_count + lon, target[0] * lon_count + target[1] % lon_count))
    return pairs


def local(
    anomalies,
    background_mean,
    obs_anom,
    innovation,
    obs_precision,
    obs_blocks,
    localization,
    loc_pattern,
):
    members = obs_anom.shape[2]
    obs_rows = obs_anom.shape[1]
    half = members // 2
    lat_count = lax.axis_size("lat")
    lon_count = lax.axis_size("lon")
    teams = [[team * TEAM + i for i in range(TEAM)] for team in range(lon_count // TEAM)]
    place = (lax.axis_index("lon") % TEAM).astype(jnp.int32).reshape(1, 1)
    bf16, f32 = jnp.bfloat16, jnp.float32

    def call(kernel, outs, ins, *operands, scratch=(), limit=VMEM_LIMIT):
        return pl.pallas_call(
            kernel,
            out_shape=tuple(jax.ShapeDtypeStruct(*out) for out in outs),
            in_specs=ins,
            out_specs=(VMEM,) * len(outs),
            scratch_shapes=scratch,
            compiler_params=pltpu.CompilerParams(vmem_limit_bytes=limit),
            name=kernel.__name__.removesuffix("_kernel"),
        )(*operands)

    def send(value, move):
        return lax.ppermute(value, ("lat", "lon"), shifts(lat_count, lon_count, move))

    def exchange(value):
        return lax.all_to_all(value, "lon", 0, 0, axis_index_groups=teams, tiled=True)

    def up(lat, lon):
        return lat + 1, lon

    def down(lat, lon):
        return lat - 1, lon

    def other_core(lat, lon):
        return lat, lon ^ 1

    def along_x(lat, lon):
        return lat, lon + (TEAM if lon % TEAM >= SIDE else -TEAM)

    def back_same(lat, lon):
        step = {0: TEAM, TEAM - 1: -TEAM}.get(lon % TEAM)
        return None if step is None else (lat, lon + step)

    def back_other(lat, lon):
        step = {1: TEAM - 1, TEAM - 2: 1 - TEAM}.get(lon % TEAM)
        return None if step is None else (lat, lon + step)

    own, pack = call(
        prepare_kernel,
        [((members + EXTRA, obs_rows), bf16), ((TEAM, EXTRA, obs_rows), bf16)],
        [SMEM] * 3 + [ANY] * 4,
        place,
        obs_blocks,
        loc_pattern[0],
        obs_anom[0],
        innovation,
        obs_precision,
        localization[0],
        scratch=[
            pltpu.VMEM((obs_rows, members), bf16),
            pltpu.VMEM((1, obs_rows), bf16),
            pltpu.VMEM((1, obs_rows), bf16),
            pltpu.VMEM((1, localization.shape[2]), f32),
            pltpu.VMEM((EXTRA // 2, obs_rows), f32),
            pltpu.SemaphoreType.DMA((4,)),
        ],
        limit=56 * 1024 * 1024,
    )
    beside = send(own, along_x)
    below = send(own, up)
    above = send(own, down)
    pack = exchange(pack)
    beside_below = send(beside, up)
    beside_above = send(beside, down)
    forward = send(beside[members:], other_core)

    (shares,) = call(
        early_kernel,
        [((TEAM + 1, members + EXTRA, members), f32)],
        [SMEM] + [VMEM] * 6,
        place,
        pack,
        forward,
        own,
        below,
        above,
        beside,
    )
    shares, side = call(
        late_kernel,
        [((TEAM, members + EXTRA, members), bf16), ((half + EXTRA, members), bf16)],
        [SMEM] + [VMEM] * 6,
        place,
        pack,
        forward,
        beside,
        beside_below,
        beside_above,
        shares,
        scratch=[pltpu.VMEM((TEAM + 1, members + EXTRA, members), f32)],
    )
    shares = exchange(shares)
    same = send(side, back_same)
    other = send(side, back_other)

    transform, outer = call(
        transform_kernel,
        [((members, members), bf16)] * 2,
        [SMEM] + [VMEM] * 3,
        place,
        shares,
        same,
        other,
    )
    inner = send(transform, other_core)
    base = jnp.broadcast_to(background_mean[..., None], anomalies.shape)
    (part,) = call(
        product_kernel, [(anomalies.shape, f32)], [SMEM] + [VMEM] * 4, place, transform, outer, base, anomalies
    )
    (analysis,) = call(blend_kernel, [(anomalies.shape, bf16)], [SMEM] + [VMEM] * 3, place, inner, part, anomalies)
    return analysis


def solution(mesh):
    in_specs = (
        P("lat", "lon", None, None),
        P("lat", "lon", None),
        P("lat", "lon", None),
        P("lat", "lon"),
        P("lat", "lon"),
        P("lat", "lon"),
        P("lat", "lon", None),
        P("lat", "lon", None),
    )
    out_specs = P("lat", "lon", None, None)
    return jax.shard_map(local, mesh=mesh, in_specs=in_specs, out_specs=out_specs, check_vma=False)
```

time: 108 us -> 103 us (0.954)
  the two profiles are of different devices: /device:TPU:32 before, /device:TPU:33 now
where the time goes in v2:
time: 103 us; the launch traced here: 102 us
  starting transfers between devices  46.6 us (45%)
  waiting for transfers between devices  42.7 us (41%)
  Pallas kernels  10.9 us (11%)
  local copies, waits for them, and re-layouts  1.04 us (1%)
    all_to_all x2, waiting for transfers between devices, exchange(): lax.all_to_all(value, 'lon', 0, 0, axis_index_groups=teams, tiled=True)  40.6 us
    ppermute x9, starting transfers between devices, send(): lax.ppermute(value, ('lat', 'lon'), shifts(lat_count, lon_count, move))  25.4 us
    all_to_all x2, starting transfers between devices, exchange(): lax.all_to_all(value, 'lon', 0, 0, axis_index_groups=teams, tiled=True)  21.2 us
    pallas_call x6, Pallas kernels, call(): pl.pallas_call(kernel, out_shape=tuple((jax.ShapeDtypeStruct(*out) for ou...  10.9 us
    ppermute x9, waiting for transfers between devices, send(): lax.ppermute(value, ('lat', 'lon'), shifts(lat_count, lon_count, move))  2.07 us
  transfers between devices with their start and end apart: 11, of which 5 were waited for; matrix products, arithmetic and copies ran while one was open for 0% of the time, Pallas kernels for 2%

profile of v2, /device:TPU:33, one launch (start us, length us, event | category | flops | bytes accessed | tf_op | source)
XLA Modules:
  0.0 102.1 jit_solution(11395231248752169909)
XLA Ops:
  0.7 2.5 %prepare.1 = (bf16[272,512]{1,0:T(8,128)(2,1)}, bf16[4,16,512]{2,1,0:T(8,128)(2,1)}) custom-call(s32[1,1]{1,0:T(1,128)} %bitcast.place_ref, s32[1,1]{1,0:T(1,128)S(6)} %copy.9.blocks_ref, s32[1,60]{1,0:T(1,128)} %bitcast.6, bf16[512,256]{1,0:T(8,128)(2,1)} %bitcast.4, bf16[1,512]{1,0:T(2,128)(2,1)} %innov_hbm.1, bf16[1,512]{1,0:T(2,128)(2,1)} %prec_hbm.1, ...), custom_call_target="tpu_custom_call" | custom-call | tf_op jit(solution)/shard_map/prepare/pallas_call | solution.py:354
  3.2 6.8 %collective-permute-start = (bf16[272,512]{1,0:T(8,128)(2,1)}, bf16[272,512]{1,0:T(8,128)(2,1)S(1)}, u32[]{:S(2)}, u32[]{:S(2)}) collective-permute-start(bf16[272,512]{1,0:T(8,128)(2,1)} %get-tuple-element.12.own_ref), channel_id=1, source_target_pairs={{0,60},{1,61},{2,6},{3,7},{4,0},{5,1},{6,10},{7,11},{8,4},{9,5},{1... | collective-permute-start | bytes 835592 | tf_op jit(solution)/shard_map/ppermute | solution.py:365
  10.0 3.5 %collective-permute-start.4 = (bf16[272,512]{1,0:T(8,128)(2,1)}, bf16[272,512]{1,0:T(8,128)(2,1)S(1)}, u32[]{:S(2)}, u32[]{:S(2)}) collective-permute-start(bf16[272,512]{1,0:T(8,128)(2,1)} %get-tuple-element.12.own_ref), channel_id=1, source_target_pairs={{0,64},{1,65},{2,66},{3,67},{4,68},{5,69},{6,70},{7,71},{8,72},{9,... | collective-permute-start | bytes 835592 | tf_op jit(solution)/shard_map/ppermute | solution.py:365
  13.6 1.9 %collective-permute-start.5 = (bf16[272,512]{1,0:T(8,128)(2,1)}, bf16[272,512]{1,0:T(8,128)(2,1)S(1)}, u32[]{:S(2)}, u32[]{:S(2)}) collective-permute-start(bf16[272,512]{1,0:T(8,128)(2,1)} %get-tuple-element.12.own_ref), channel_id=1, source_target_pairs={{64,0},{65,1},{66,2},{67,3},{68,4},{69,5},{70,6},{71,7},{72,8},{73... | collective-permute-start | bytes 835592 | tf_op jit(solution)/shard_map/ppermute | solution.py:365
  15.5 0.1 collective-permute-done.beside_ref
  15.7 3.5 %collective-permute-start.2 = (bf16[272,512]{1,0:T(8,128)(2,1)S(1)}, bf16[272,512]{1,0:T(8,128)(2,1)S(1)}, u32[]{:S(2)}, u32[]{:S(2)}) collective-permute-start(bf16[272,512]{1,0:T(8,128)(2,1)S(1)} %collective-permute-done.beside_ref), channel_id=1, source_target_pairs={{0,64},{1,65},{2,66},{3,67},{4,68},{5,69},{6,70},{7,71},{8,72},{9,... | collective-permute-start | bytes 835592 | tf_op jit(solution)/shard_map/ppermute | solution.py:365
  19.2 1.9 %collective-permute-start.3 = (bf16[272,512]{1,0:T(8,128)(2,1)S(1)}, bf16[272,512]{1,0:T(8,128)(2,1)S(1)}, u32[]{:S(2)}, u32[]{:S(2)}) collective-permute-start(bf16[272,512]{1,0:T(8,128)(2,1)S(1)} %collective-permute-done.beside_ref), channel_id=1, source_target_pairs={{64,0},{65,1},{66,2},{67,3},{68,4},{69,5},{70,6},{71,7},{72,8},{73... | collective-permute-start | bytes 835592 | tf_op jit(solution)/shard_map/ppermute | solution.py:365
  21.1 16.8 %all-to-all-start = ((bf16[4,16,512]{2,1,0:T(8,128)(2,1)}), bf16[4,16,512]{2,1,0:T(8,128)(2,1)S(1)}, u32[]{:S(2)}, u32[]{:S(2)}) async-start(bf16[4,16,512]{2,1,0:T(8,128)(2,1)} %get-tuple-element.11), calls=%async_computation | async-start | bytes 131072 | tf_op jit(solution)/shard_map/all_to_all | solution.py:368
  37.9 1.9 %collective-permute-start.1 = (bf16[16,512]{1,0:T(8,128)(2,1)S(1)}, bf16[16,512]{1,0:T(8,128)(2,1)S(1)}, u32[]{:S(2)}, u32[]{:S(2)}) collective-permute-start(bf16[16,512]{1,0:T(8,128)(2,1)S(1)} %slice.4), channel_id=1, source_target_pairs={{0,1},{1,0},{2,3},{3,2},{4,5},{5,4},{6,7},{7,6},{8,9},{9,8},{10,11... | collective-permute-start | bytes 49160 | tf_op jit(solution)/shard_map/ppermute | solution.py:365
  39.8 10.1 %all-to-all-done.pack_ref = bf16[4,16,512]{2,1,0:T(8,128)(2,1)S(1)} async-done(((bf16[4,16,512]{2,1,0:T(8,128)(2,1)}), bf16[4,16,512]{2,1,0:T(8,128)(2,1)S(1)}, u32[]{:S(2)}, u32[]{:S(2)}) %all-to-all-start) | async-done | bytes 65568 | tf_op jit(solution)/shard_map/all_to_all | solution.py:368
  49.9 0.9 copy-done
  50.8 1.3 %early.1.share_ref = f32[5,272,256]{2,1,0:T(8,128)S(1)} custom-call(s32[1,1]{1,0:T(1,128)} %bitcast.place_ref, bf16[4,16,512]{2,1,0:T(8,128)(2,1)S(1)} %all-to-all-done.pack_ref, bf16[16,512]{1,0:T(8,128)(2,1)S(1)} %collective-permute-done.1.forward_ref, bf16[272,512]{1,0:T(8,128)(2,1)S(1)} %copy-done, ...), custom_call_target="tpu_custom_call" | custom-call | tf_op jit(solution)/shard_map/early/pallas_call | solution.py:354
  52.2 1.6 %late.1 = (bf16[4,272,256]{2,1,0:T(8,128)(2,1)}, bf16[144,256]{1,0:T(8,128)(2,1)S(1)}) custom-call(s32[1,1]{1,0:T(1,128)} %bitcast.place_ref, bf16[4,16,512]{2,1,0:T(8,128)(2,1)S(1)} %all-to-all-done.pack_ref, bf16[16,512]{1,0:T(8,128)(2,1)S(1)} %collective-permute-done.1.forward_ref, bf16[272,512]{1,0:T(8,128)(2,1)S(1)} %collective-permute-done.beside_ref, ...), custom_call_target="tpu_custom_call" | custom-call | tf_op jit(solution)/shard_map/late/pallas_call | solution.py:354
  53.8 4.4 %all-to-all-start.1 = ((bf16[4,272,256]{2,1,0:T(8,128)(2,1)}), bf16[4,272,256]{2,1,0:T(8,128)(2,1)S(1)}, u32[]{:S(2)}, u32[]{:S(2)}) async-start(bf16[4,272,256]{2,1,0:T(8,128)(2,1)} %get-tuple-element.13), calls=%async_computation.1 | async-start | bytes 1114112 | tf_op jit(solution)/shard_map/all_to_all | solution.py:368
  58.3 0.7 collective-permute-start.6
  58.9 2.3 %collective-permute-start.7 = (bf16[144,256]{1,0:T(8,128)(2,1)S(1)}, bf16[144,256]{1,0:T(8,128)(2,1)S(1)}, u32[]{:S(2)}, u32[]{:S(2)}) collective-permute-start(bf16[144,256]{1,0:T(8,128)(2,1)S(1)} %get-tuple-element.14), channel_id=1, source_target_pairs={{1,4},{2,63},{5,8},{6,3},{9,12},{10,7},{13,16},{14,11},{17,20},{18... | collective-permute-start | bytes 221192 | tf_op jit(solution)/shard_map/ppermute | solution.py:365
  61.3 1.4 %collective-permute-done.7.other_ref = bf16[144,256]{1,0:T(8,128)(2,1)S(1)} collective-permute-done((bf16[144,256]{1,0:T(8,128)(2,1)S(1)}, bf16[144,256]{1,0:T(8,128)(2,1)S(1)}, u32[]{:S(2)}, u32[]{:S(2)}) %collective-permute-start.7) | collective-permute-done | bytes 73760 | tf_op jit(solution)/shard_map/ppermute | solution.py:365
  62.6 30.6 %all-to-all-done.1.part_ref = bf16[4,272,256]{2,1,0:T(8,128)(2,1)S(1)} async-done(((bf16[4,272,256]{2,1,0:T(8,128)(2,1)}), bf16[4,272,256]{2,1,0:T(8,128)(2,1)S(1)}, u32[]{:S(2)}, u32[]{:S(2)}) %all-to-all-start.1) | async-done | bytes 557088 | tf_op jit(solution)/shard_map/all_to_all | solution.py:368
  93.2 4.3 %transform.1 = (bf16[256,256]{1,0:T(8,128)(2,1)S(1)}, bf16[256,256]{1,0:T(8,128)(2,1)S(1)}) custom-call(s32[1,1]{1,0:T(1,128)} %bitcast.place_ref, bf16[4,272,256]{2,1,0:T(8,128)(2,1)S(1)} %all-to-all-done.1.part_ref, bf16[144,256]{1,0:T(8,128)(2,1)S(1)} %collective-permute-done.6.same_ref, bf16[144,256]{1,0:T(8,128)(2,1)S(1)} %collective-permute-done.7.other_ref), custom_call_target="tpu_custom_call" | custom-call | tf_op jit(solution)/shard_map/transform/pallas_call | solution.py:354
  97.5 2.8 %collective-permute-start.8 = (bf16[256,256]{1,0:T(8,128)(2,1)S(1)}, bf16[256,256]{1,0:T(8,128)(2,1)S(1)}, u32[]{:S(2)}, u32[]{:S(2)}) collective-permute-start(bf16[256,256]{1,0:T(8,128)(2,1)S(1)} %get-tuple-element.15.self_ref), channel_id=1, source_target_pairs={{0,1},{1,0},{2,3},{3,2},{4,5},{5,4},{6,7},{7,6},{8,9},{9,8},{10,11... | collective-permute-start | bytes 393224 | tf_op jit(solution)/shard_map/ppermute | solution.py:365
  100.3 0.1 broadcast_in_dim.2.base_ref
  100.4 0.3 product.1.part_ref
  100.7 0.5 collective-permute-done.8.inner_ref
  101.3 0.8 blend.1
  (12 shorter events, 0.0 us)
Async XLA Ops:
  3.2 12.5 %collective-permute-start = (bf16[272,512]{1,0:T(8,128)(2,1)}, bf16[272,512]{1,0:T(8,128)(2,1)S(1)}, u32[]{:S(2)}, u32[]{:S(2)}) collective-permute-start(bf16[272,512]{1,0:T(8,128)(2,1)} %get-tuple-element.12.own_ref), channel_id=1, source_target_pairs={{0,60},{1,61},{2,6},{3,7},{4,0},{5,1},{6,10},{7,11},{8,4},{9,5},{1... | collective-permute-start | bytes 835592 | tf_op jit(solution)/shard_map/ppermute | solution.py:365
  10.0 39.8 %collective-permute-start.4 = (bf16[272,512]{1,0:T(8,128)(2,1)}, bf16[272,512]{1,0:T(8,128)(2,1)S(1)}, u32[]{:S(2)}, u32[]{:S(2)}) collective-permute-start(bf16[272,512]{1,0:T(8,128)(2,1)} %get-tuple-element.12.own_ref), channel_id=1, source_target_pairs={{0,64},{1,65},{2,66},{3,67},{4,68},{5,69},{6,70},{7,71},{8,72},{9,... | collective-permute-start | bytes 835592 | tf_op jit(solution)/shard_map/ppermute | solution.py:365
  13.6 36.3 %collective-permute-start.5 = (bf16[272,512]{1,0:T(8,128)(2,1)}, bf16[272,512]{1,0:T(8,128)(2,1)S(1)}, u32[]{:S(2)}, u32[]{:S(2)}) collective-permute-start(bf16[272,512]{1,0:T(8,128)(2,1)} %get-tuple-element.12.own_ref), channel_id=1, source_target_pairs={{64,0},{65,1},{66,2},{67,3},{68,4},{69,5},{70,6},{71,7},{72,8},{73... | collective-permute-start | bytes 835592 | tf_op jit(solution)/shard_map/ppermute | solution.py:365
  15.7 36.5 %collective-permute-start.2 = (bf16[272,512]{1,0:T(8,128)(2,1)S(1)}, bf16[272,512]{1,0:T(8,128)(2,1)S(1)}, u32[]{:S(2)}, u32[]{:S(2)}) collective-permute-start(bf16[272,512]{1,0:T(8,128)(2,1)S(1)} %collective-permute-done.beside_ref), channel_id=1, source_target_pairs={{0,64},{1,65},{2,66},{3,67},{4,68},{5,69},{6,70},{7,71},{8,72},{9,... | collective-permute-start | bytes 835592 | tf_op jit(solution)/shard_map/ppermute | solution.py:365
  19.2 33.0 %collective-permute-start.3 = (bf16[272,512]{1,0:T(8,128)(2,1)S(1)}, bf16[272,512]{1,0:T(8,128)(2,1)S(1)}, u32[]{:S(2)}, u32[]{:S(2)}) collective-permute-start(bf16[272,512]{1,0:T(8,128)(2,1)S(1)} %collective-permute-done.beside_ref), channel_id=1, source_target_pairs={{64,0},{65,1},{66,2},{67,3},{68,4},{69,5},{70,6},{71,7},{72,8},{73... | collective-permute-start | bytes 835592 | tf_op jit(solution)/shard_map/ppermute | solution.py:365
  21.1 28.7 %all-to-all-start = ((bf16[4,16,512]{2,1,0:T(8,128)(2,1)}), bf16[4,16,512]{2,1,0:T(8,128)(2,1)S(1)}, u32[]{:S(2)}, u32[]{:S(2)}) async-start(bf16[4,16,512]{2,1,0:T(8,128)(2,1)} %get-tuple-element.11), calls=%async_computation | async-start | bytes 131072 | tf_op jit(solution)/shard_map/all_to_all | solution.py:368
  37.9 12.0 %collective-permute-start.1 = (bf16[16,512]{1,0:T(8,128)(2,1)S(1)}, bf16[16,512]{1,0:T(8,128)(2,1)S(1)}, u32[]{:S(2)}, u32[]{:S(2)}) collective-permute-start(bf16[16,512]{1,0:T(8,128)(2,1)S(1)} %slice.4), channel_id=1, source_target_pairs={{0,1},{1,0},{2,3},{3,2},{4,5},{5,4},{6,7},{7,6},{8,9},{9,8},{10,11... | collective-permute-start | bytes 49160 | tf_op jit(solution)/shard_map/ppermute | solution.py:365
  49.9 1.0 copy-start
  53.8 46.5 %copy-start.2 = (f32[2,4,16]{2,1,0:T(4,128)S(1)}, f32[2,4,16]{2,1,0:T(4,128)}, u32[]{:S(2)}) copy-start(f32[2,4,16]{2,1,0:T(4,128)} %param.9) | copy-start | bytes 1540
  53.8 46.6 %copy-start.1 = (bf16[2,4,16,256]{3,2,1,0:T(8,128)(2,1)S(1)}, bf16[2,4,16,256]{3,2,1,0:T(8,128)(2,1)}, u32[]{:S(2)}) copy-start(bf16[2,4,16,256]{3,2,1,0:T(8,128)(2,1)} %state_ref.3) | copy-start | bytes 196612
  53.8 39.4 %all-to-all-start.1 = ((bf16[4,272,256]{2,1,0:T(8,128)(2,1)}), bf16[4,272,256]{2,1,0:T(8,128)(2,1)S(1)}, u32[]{:S(2)}, u32[]{:S(2)}) async-start(bf16[4,272,256]{2,1,0:T(8,128)(2,1)} %get-tuple-element.13), calls=%async_computation.1 | async-start | bytes 1114112 | tf_op jit(solution)/shard_map/all_to_all | solution.py:368
  58.3 3.0 %collective-permute-start.6 = (bf16[144,256]{1,0:T(8,128)(2,1)S(1)}, bf16[144,256]{1,0:T(8,128)(2,1)S(1)}, u32[]{:S(2)}, u32[]{:S(2)}) collective-permute-start(bf16[144,256]{1,0:T(8,128)(2,1)S(1)} %get-tuple-element.14), channel_id=1, source_target_pairs={{0,4},{3,63},{4,8},{7,3},{8,12},{11,7},{12,16},{15,11},{16,20},{19... | collective-permute-start | bytes 221192 | tf_op jit(solution)/shard_map/ppermute | solution.py:365
  58.9 3.7 %collective-permute-start.7 = (bf16[144,256]{1,0:T(8,128)(2,1)S(1)}, bf16[144,256]{1,0:T(8,128)(2,1)S(1)}, u32[]{:S(2)}, u32[]{:S(2)}) collective-permute-start(bf16[144,256]{1,0:T(8,128)(2,1)S(1)} %get-tuple-element.14), channel_id=1, source_target_pairs={{1,4},{2,63},{5,8},{6,3},{9,12},{10,7},{13,16},{14,11},{17,20},{18... | collective-permute-start | bytes 221192 | tf_op jit(solution)/shard_map/ppermute | solution.py:365
  97.5 3.7 %collective-permute-start.8 = (bf16[256,256]{1,0:T(8,128)(2,1)S(1)}, bf16[256,256]{1,0:T(8,128)(2,1)S(1)}, u32[]{:S(2)}, u32[]{:S(2)}) collective-permute-start(bf16[256,256]{1,0:T(8,128)(2,1)S(1)} %get-tuple-element.15.self_ref), channel_id=1, source_target_pairs={{0,1},{1,0},{2,3},{3,2},{4,5},{5,4},{6,7},{7,6},{8,9},{9,8},{10,11... | collective-permute-start | bytes 393224 | tf_op jit(solution)/shard_map/ppermute | solution.py:365

commit v3 on v2

--- a/solution.py
+++ b/solution.py
@@ -98,17 +98,28 @@
     tile_ref[pl.ds(0, members), :] = anom_ref[...].T
 
 
-def pack_weights(pack_ref, dest):
-    parts = pack_ref[dest].astype(jnp.float32)
+def joined(pack):
+    parts = pack.astype(jnp.float32)
     return parts[: EXTRA // 2] + parts[EXTRA // 2 :]
 
 
-def outer_weights(place_ref, beside_ref, forward_ref):
+def team_weights(place_ref, pack_ref, cross_ref, core_ref, index):
+    return joined(
+        (
+            lambda: pack_ref[place_ref[0, 0]],
+            lambda: core_ref[0],
+            lambda: cross_ref[0],
+            lambda: core_ref[1],
+        )[index]()
+    )
+
+
+def outer_weights(place_ref, beside_ref, core_ref):
     members = beside_ref.shape[0] - EXTRA
     place = place_ref[0, 0]
     used = 2 * NEAR_LAT
     direct = beside_ref[pl.ds(members, EXTRA), :].astype(jnp.float32)[2 : 2 + 2 * used]
-    passed = forward_ref[...].astype(jnp.float32)[2 : 2 + 2 * used]
+    passed = core_ref[2].astype(jnp.float32)[2 : 2 + 2 * used]
     outer = (place == 0) | (place == TEAM - 1)
     direct = direct[:NEAR_LAT] + direct[used : used + NEAR_LAT]
     passed = passed[NEAR_LAT:used] + passed[used + NEAR_LAT :]
@@ -122,98 +133,117 @@
     return dot(scaled, tile_ref[pl.ds(0, members), :], ACROSS)
 
 
-def early_kernel(place_ref, pack_ref, forward_ref, own_ref, below_ref, above_ref, beside_ref, out_ref):
-    far = SIDE - place_ref[0, 0] // SIDE * SIDE
-    for dest in range(TEAM):
-        weight = pack_weights(pack_ref, dest)
+def early_kernel(
+    place_ref, pack_ref, cross_ref, core_ref, own_ref, below_ref, above_ref, beside_ref, out_ref
+):
+    for index in range(TEAM):
+        weight = team_weights(place_ref, pack_ref, cross_ref, core_ref, index)
         total = None
         for lat, tile_ref in enumerate((below_ref, own_ref, above_ref)):
             part = weighted(tile_ref, weight[lat : lat + 1])
             total = part if total is None else total + part
-        out_ref[dest] = total
-    row = NEAR_LAT + LAT_REACH
-    for step in range(SIDE):
-        weight = pack_weights(pack_ref, far + step)[row : row + 1]
-        out_ref[far + step] += weighted(beside_ref, weight)
-    weight = outer_weights(place_ref, beside_ref, forward_ref)
+        if index >= SIDE:
+            row = NEAR_LAT + LAT_REACH
+            total = total + weighted(beside_ref, weight[row : row + 1])
+        out_ref[index] = total
+    weight = outer_weights(place_ref, beside_ref, core_ref)
     out_ref[TEAM] = weighted(beside_ref, weight[LAT_REACH : LAT_REACH + 1])
 
 
-def late_kernel(
-    place_ref, pack_ref, forward_ref, beside_ref, below_ref, above_ref, share_ref, out_ref, side_ref, total_ref
-):
-    members = share_ref.shape[2]
+def packed(total):
+    members = total.shape[1]
     half = members // 2
-    side = place_ref[0, 0] // SIDE
-    far = SIDE - side * SIDE
-    tiles = ((0, below_ref), (2 * LAT_REACH, above_ref))
-    for step in range(SIDE):
-        weight = pack_weights(pack_ref, far + step)
-        total = share_ref[far + step]
-        for lat, tile_ref in tiles:
-            row = NEAR_LAT + lat
-            total = total + weighted(tile_ref, weight[row : row + 1])
-        total_ref[far + step] = total
-        total_ref[SIDE - far + step] = share_ref[SIDE - far + step]
-    weight = outer_weights(place_ref, beside_ref, forward_ref)
-    total = share_ref[TEAM]
-    for lat, tile_ref in tiles:
-        total = total + weighted(tile_ref, weight[lat : lat + 1])
-    total_ref[TEAM] = total
-
     row = lax.broadcasted_iota(jnp.int32, (half, half), 0)
     col = lax.broadcasted_iota(jnp.int32, (half, half), 1)
-
-    def packed(total):
-        first = total[:half, :half]
-        last = total[half:members, half:]
-        diagonal = jnp.sum(jnp.where(row == col, last, 0.0), axis=0, keepdims=True)
-        body = jnp.concatenate([jnp.where(row <= col, first, last), total[:half, half:]], axis=1)
-        tail = jnp.concatenate([total[members : members + 1], jnp.concatenate([diagonal, diagonal], axis=1)], axis=0)
-        return body.astype(jnp.bfloat16), tail
-
-    def padded(tails):
-        rows = sum(tail.shape[0] for tail in tails)
-        zeros = jnp.zeros((EXTRA - rows, members), jnp.float32)
-        return jnp.concatenate([*tails, zeros], axis=0).astype(jnp.bfloat16)
-
-    group = [packed(total_ref[dest]) for dest in range(TEAM)]
-    outer = packed(total_ref[TEAM])
-
-    def write(reader, parts):
-        for slot, (body, _) in enumerate(parts):
-            out_ref[reader, pl.ds(slot * half, half), :] = body
-        out_ref[reader, pl.ds(members, EXTRA), :] = padded([tail for _, tail in parts])
-
-    def write_side(part):
-        side_ref[pl.ds(0, half), :] = part[0]
-        side_ref[pl.ds(half, EXTRA), :] = padded([part[1]])
-
-    nothing = tuple(jnp.zeros_like(part) for part in outer)
-    write(1, (group[1], group[2]))
-    write(2, (group[1], group[2]))
-
-    @pl.when(side == 0)
-    def _():
-        write(0, (nothing, group[0]))
-        write(3, (group[3], outer))
-        write_side(group[3])
-
-    @pl.when(side == 1)
-    def _():
-        write(0, (outer, group[0]))
-        write(3, (group[3], nothing))
-        write_side(group[0])
-
-
-def transform_kernel(place_ref, part_ref, same_ref, other_ref, self_out, outer_out):
-    members = part_ref.shape[2]
+    first = total[:half, :half]
+    last = total[half:members, half:]
+    diagonal = jnp.sum(jnp.where(row == col, last, 0.0), axis=0, keepdims=True)
+    body = jnp.concatenate([jnp.where(row <= col, first, last), total[:half, half:]], axis=1)
+    return body, jnp.concatenate(
+        [total[members : members + 1], jnp.concatenate([diagonal, diagonal], axis=1)], axis=0
+    )
+
+
+def put(out_ref, parts):
+    half, members = next(part[0].shape for part in parts if part is not None)
+    tails = []
+    for slot, part in enumerate(parts):
+        body, tail = part or (jnp.zeros((half, members), jnp.float32), jnp.zeros((2, members), jnp.float32))
+        out_ref[pl.ds(slot * half, half), :] = body.astype(out_ref.dtype)
+        tails.append(tail)
+    tails.append(jnp.zeros((EXTRA - 2 * len(parts), members), jnp.float32))
+    out_ref[pl.ds(len(parts) * half, EXTRA), :] = jnp.concatenate(tails, axis=0).astype(out_ref.dtype)
+
+
+def late_kernel(
+    place_ref,
+    cross_ref,
+    core_ref,
+    beside_ref,
+    below_ref,
+    above_ref,
+    share_ref,
+    give_ref,
+    keep_ref,
+    body_ref,
+    tail_ref,
+):
+    tiles = ((0, below_ref), (2 * LAT_REACH, above_ref))
+    for index in range(TEAM + 1):
+        total = share_ref[index]
+        if index >= SIDE:
+            if index < TEAM:
+                weight = joined(cross_ref[0] if index == SIDE else core_ref[1])[NEAR_LAT:]
+            else:
+                weight = outer_weights(place_ref, beside_ref, core_ref)
+            for lat, tile_ref in tiles:
+                total = total + weighted(tile_ref, weight[lat : lat + 1])
+        body, tail = packed(total)
+        body_ref[index] = body
+        tail_ref[index, pl.ds(0, 2), :] = tail
+
+    def write(place):
+        def part(index):
+            return body_ref[index], tail_ref[index, pl.ds(0, 2), :]
+
+        middle = [part(1 ^ place), part(2 ^ place)]
+        if place in (0, TEAM - 1):
+            put(give_ref, (*middle, part(3), part(TEAM)))
+            put(keep_ref, (*middle, part(0), None))
+        else:
+            put(give_ref, (*middle, part(1), None))
+            put(keep_ref, (*middle, part(2), part(TEAM)))
+
+    for place in range(TEAM):
+        pl.when(place_ref[0, 0] == place)(lambda place=place: write(place))
+
+
+def gather_kernel(place_ref, keep_ref, give_ref, cross_out, keep_out, side_out):
+    half = (keep_ref.shape[0] - EXTRA) // 4
+    total = keep_ref[...] + give_ref[...].astype(jnp.float32)
+    tails = total[4 * half :]
+    parts = [(total[slot * half : (slot + 1) * half], tails[2 * slot : 2 * slot + 2]) for slot in range(4)]
+
+    def write(place):
+        middle, ends = parts[:2], parts[2:]
+        if place in (0, TEAM - 1):
+            put(cross_out, middle)
+            put(keep_out, (None, ends[0]) if place == 0 else (ends[0], None))
+        else:
+            put(cross_out, ends if place == 1 else ends[::-1])
+            put(keep_out, middle)
+        put(side_out, ends[:1])
+
+    for place in range(TEAM):
+        pl.when(place_ref[0, 0] == place)(lambda place=place: write(place))
+
+
+def transform_kernel(place_ref, keep_ref, cross_ref, side_ref, self_out, outer_out):
+    members = keep_ref.shape[1]
     half = members // 2
     place = place_ref[0, 0]
-    total = part_ref[0].astype(jnp.float32)
-    for index in range(1, TEAM):
-        total = total + part_ref[index].astype(jnp.float32)
-    side = same_ref[...].astype(jnp.float32) + other_ref[...].astype(jnp.float32)
+    total = keep_ref[...] + cross_ref[...].astype(jnp.float32)
+    side = side_ref[...].astype(jnp.float32)
     row = lax.broadcasted_iota(jnp.int32, (half, half), 0)
     col = lax.broadcasted_iota(jnp.int32, (half, half), 1)
     upper = row <= col
@@ -346,7 +376,6 @@
     half = members // 2
     lat_count = lax.axis_size("lat")
     lon_count = lax.axis_size("lon")
-    teams = [[team * TEAM + i for i in range(TEAM)] for team in range(lon_count // TEAM)]
     place = (lax.axis_index("lon") % TEAM).astype(jnp.int32).reshape(1, 1)
     bf16, f32 = jnp.bfloat16, jnp.float32
 
@@ -364,9 +393,6 @@
     def send(value, move):
         return lax.ppermute(value, ("lat", "lon"), shifts(lat_count, lon_count, move))
 
-    def exchange(value):
-        return lax.all_to_all(value, "lon", 0, 0, axis_index_groups=teams, tiled=True)
-
     def up(lat, lon):
         return lat + 1, lon
 
@@ -379,11 +405,10 @@
     def along_x(lat, lon):
         return lat, lon + (TEAM if lon % TEAM >= SIDE else -TEAM)
 
-    def back_same(lat, lon):
-        step = {0: TEAM, TEAM - 1: -TEAM}.get(lon % TEAM)
-        return None if step is None else (lat, lon + step)
-
-    def back_other(lat, lon):
+    def across_z(lat, lon):
+        return lat, lon ^ 2
+
+    def side_move(lat, lon):
         step = {1: TEAM - 1, TEAM - 2: 1 - TEAM}.get(lon % TEAM)
         return None if step is None else (lat, lon + step)
 
@@ -408,51 +433,64 @@
         ],
         limit=56 * 1024 * 1024,
     )
+    index = place[0, 0]
+    far = jnp.where(index % 2 == 0, jnp.stack([pack[2], pack[3]]), jnp.stack([pack[3], pack[2]]))
+    near = jnp.where(index % 2 == 0, jnp.stack([pack[0], pack[1]]), jnp.stack([pack[1], pack[0]]))
+    far, near = jnp.where(index < SIDE, far, near), jnp.where(index < SIDE, near, far)
+    cross = send(far, across_z)
     beside = send(own, along_x)
     below = send(own, up)
     above = send(own, down)
-    pack = exchange(pack)
     beside_below = send(beside, up)
     beside_above = send(beside, down)
-    forward = send(beside[members:], other_core)
+    core = send(jnp.stack([near[1], cross[1], beside[members:]]), other_core)
 
     (shares,) = call(
         early_kernel,
         [((TEAM + 1, members + EXTRA, members), f32)],
-        [SMEM] + [VMEM] * 6,
+        [SMEM] + [VMEM] * 7,
         place,
         pack,
-        forward,
+        cross,
+        core,
         own,
         below,
         above,
         beside,
     )
-    shares, side = call(
+    give, keep = call(
         late_kernel,
-        [((TEAM, members + EXTRA, members), bf16), ((half + EXTRA, members), bf16)],
+        [((4 * half + EXTRA, members), bf16), ((4 * half + EXTRA, members), f32)],
         [SMEM] + [VMEM] * 6,
         place,
-        pack,
-        forward,
+        cross,
+        core,
         beside,
         beside_below,
         beside_above,
         shares,
-        scratch=[pltpu.VMEM((TEAM + 1, members + EXTRA, members), f32)],
-    )
-    shares = exchange(shares)
-    same = send(side, back_same)
-    other = send(side, back_other)
+        scratch=[pltpu.VMEM((TEAM + 1, half, members), f32), pltpu.VMEM((TEAM + 1, 8, members), f32)],
+    )
+    give = send(give, other_core)
+    shares, keep, side = call(
+        gather_kernel,
+        [((members + EXTRA, members), bf16), ((members + EXTRA, members), f32), ((half + EXTRA, members), bf16)],
+        [SMEM] + [VMEM] * 2,
+        place,
+        keep,
+        give,
+    )
+    shares = send(shares, across_z)
+    side = send(side, side_move)
 
     transform, outer = call(
         transform_kernel,
         [((members, members), bf16)] * 2,
         [SMEM] + [VMEM] * 3,
         place,
+        keep,
         shares,
-        same,
-        other,
+        side,
     )
     inner = send(transform, other_core)
     base = jnp.broadcast_to(background_mean[..., None], anomalies.shape)

time: 103 us -> 87.1 us (0.85)
  the two profiles are of different devices: /device:TPU:33 before, /device:TPU:97 now
where the time goes in v3:
time: 87.1 us; the launch traced here: 86.4 us
  starting transfers between devices  49.9 us (57%)
  waiting for transfers between devices  22.1 us (25%)
  Pallas kernels  10.1 us (12%)
  local copies, waits for them, and re-layouts  2.67 us (3%)
  between operations  0.91 us (1%)
    ppermute x11, starting transfers between devices, send(): lax.ppermute(value, ('lat', 'lon'), shifts(lat_count, lon_count, move))  49.9 us
    ppermute x11, waiting for transfers between devices, send(): lax.ppermute(value, ('lat', 'lon'), shifts(lat_count, lon_count, move))  22.1 us
    pallas_call x7, Pallas kernels, call(): pl.pallas_call(kernel, out_shape=tuple((jax.ShapeDtypeStruct(*out) for ou...  10.1 us
    unnamed x8, local copies, waits for them, and re-layouts  1.81 us
  transfers between devices with their start and end apart: 11, of which 6 were waited for; matrix products, arithmetic and copies ran while one was open for 2% of the time, Pallas kernels for 2%

profile of v3, /device:TPU:97, one launch (start us, length us, event | category | flops | bytes accessed | tf_op | source)
XLA Modules:
  0.0 86.4 jit_solution(3095870621818156889)
XLA Ops:
  0.7 2.5 %prepare.1 = (bf16[272,512]{1,0:T(8,128)(2,1)}, bf16[4,16,512]{2,1,0:T(8,128)(2,1)}) custom-call(s32[1,1]{1,0:T(1,128)} %bitcast.place_ref, s32[1,1]{1,0:T(1,128)S(6)} %copy.9.blocks_ref, s32[1,60]{1,0:T(1,128)} %bitcast.8, bf16[512,256]{1,0:T(8,128)(2,1)} %bitcast.6, bf16[1,512]{1,0:T(2,128)(2,1)} %innov_hbm.1, bf16[1,512]{1,0:T(2,128)(2,1)} %prec_hbm.1, ...), custom_call_target="tpu_custom_call" | custom-call | tf_op jit(solution)/shard_map/prepare/pallas_call | solution.py:383
  3.2 6.8 %collective-permute-start.1 = (bf16[272,512]{1,0:T(8,128)(2,1)}, bf16[272,512]{1,0:T(8,128)(2,1)S(1)}, u32[]{:S(2)}, u32[]{:S(2)}) collective-permute-start(bf16[272,512]{1,0:T(8,128)(2,1)} %get-tuple-element.15.own_ref), channel_id=1, source_target_pairs={{0,60},{1,61},{2,6},{3,7},{4,0},{5,1},{6,10},{7,11},{8,4},{9,5},{1... | collective-permute-start | bytes 835592 | tf_op jit(solution)/shard_map/ppermute | solution.py:394
  10.0 4.8 %collective-permute-start.5 = (bf16[272,512]{1,0:T(8,128)(2,1)}, bf16[272,512]{1,0:T(8,128)(2,1)S(1)}, u32[]{:S(2)}, u32[]{:S(2)}) collective-permute-start(bf16[272,512]{1,0:T(8,128)(2,1)} %get-tuple-element.15.own_ref), channel_id=1, source_target_pairs={{0,64},{1,65},{2,66},{3,67},{4,68},{5,69},{6,70},{7,71},{8,72},{9,... | collective-permute-start | bytes 835592 | tf_op jit(solution)/shard_map/ppermute | solution.py:394
  14.8 1.9 %collective-permute-start.6 = (bf16[272,512]{1,0:T(8,128)(2,1)}, bf16[272,512]{1,0:T(8,128)(2,1)S(1)}, u32[]{:S(2)}, u32[]{:S(2)}) collective-permute-start(bf16[272,512]{1,0:T(8,128)(2,1)} %get-tuple-element.15.own_ref), channel_id=1, source_target_pairs={{64,0},{65,1},{66,2},{67,3},{68,4},{69,5},{70,6},{71,7},{72,8},{73... | collective-permute-start | bytes 835592 | tf_op jit(solution)/shard_map/ppermute | solution.py:394
  16.7 0.8 fusion
  17.5 0.8 broadcast_select_fusion
  18.3 7.6 %collective-permute-start = (bf16[2,16,512]{2,1,0:T(8,128)(2,1)S(1)}, bf16[2,16,512]{2,1,0:T(8,128)(2,1)S(1)}, u32[]{:S(2)}, u32[]{:S(2)}) collective-permute-start(bf16[2,16,512]{2,1,0:T(8,128)(2,1)S(1)} %get-tuple-element.23), channel_id=1, source_target_pairs={{0,2},{1,3},{2,0},{3,1},{4,6},{5,7},{6,4},{7,5},{8,10},{9,11},{10,... | collective-permute-start | bytes 98312 | tf_op jit(solution)/shard_map/ppermute | solution.py:394
  26.0 5.7 %collective-permute-done.cross_ref = bf16[2,16,512]{2,1,0:T(8,128)(2,1)S(1)} collective-permute-done((bf16[2,16,512]{2,1,0:T(8,128)(2,1)S(1)}, bf16[2,16,512]{2,1,0:T(8,128)(2,1)S(1)}, u32[]{:S(2)}, u32[]{:S(2)}) %collective-permute-start) | collective-permute-done | bytes 32800 | tf_op jit(solution)/shard_map/ppermute | solution.py:394
  31.7 4.8 %collective-permute-start.3 = (bf16[272,512]{1,0:T(8,128)(2,1)S(1)}, bf16[272,512]{1,0:T(8,128)(2,1)S(1)}, u32[]{:S(2)}, u32[]{:S(2)}) collective-permute-start(bf16[272,512]{1,0:T(8,128)(2,1)S(1)} %collective-permute-done.1.beside_ref), channel_id=1, source_target_pairs={{0,64},{1,65},{2,66},{3,67},{4,68},{5,69},{6,70},{7,71},{8,72},{9,... | collective-permute-start | bytes 835592 | tf_op jit(solution)/shard_map/ppermute | solution.py:394
  36.5 1.9 %collective-permute-start.4 = (bf16[272,512]{1,0:T(8,128)(2,1)S(1)}, bf16[272,512]{1,0:T(8,128)(2,1)S(1)}, u32[]{:S(2)}, u32[]{:S(2)}) collective-permute-start(bf16[272,512]{1,0:T(8,128)(2,1)S(1)} %collective-permute-done.1.beside_ref), channel_id=1, source_target_pairs={{64,0},{65,1},{66,2},{67,3},{68,4},{69,5},{70,6},{71,7},{72,8},{73... | collective-permute-start | bytes 835592 | tf_op jit(solution)/shard_map/ppermute | solution.py:394
  38.5 4.6 %collective-permute-start.2 = (bf16[3,16,512]{2,1,0:T(8,128)(2,1)S(1)}, bf16[3,16,512]{2,1,0:T(8,128)(2,1)S(1)}, u32[]{:S(2)}, u32[]{:S(2)}) collective-permute-start(bf16[3,16,512]{2,1,0:T(8,128)(2,1)S(1)} %pad_maximum_fusion), channel_id=1, source_target_pairs={{0,1},{1,0},{2,3},{3,2},{4,5},{5,4},{6,7},{7,6},{8,9},{9,8},{10,11... | collective-permute-start | bytes 147464 | tf_op jit(solution)/shard_map/ppermute | solution.py:394
  43.1 0.8 collective-permute-done.2.core_ref
  44.0 0.8 copy-done
  44.8 1.0 %copy-done.1 = bf16[272,512]{1,0:T(8,128)(2,1)S(1)} copy-done((bf16[272,512]{1,0:T(8,128)(2,1)S(1)}, bf16[272,512]{1,0:T(8,128)(2,1)}, u32[]{:S(2)}) %copy-start.1) | copy-done | bytes 278552
  45.8 1.3 %early.1.share_ref = f32[5,272,256]{2,1,0:T(8,128)S(1)} custom-call(s32[1,1]{1,0:T(1,128)} %bitcast.place_ref, bf16[4,16,512]{2,1,0:T(8,128)(2,1)S(1)} %copy-done, bf16[2,16,512]{2,1,0:T(8,128)(2,1)S(1)} %collective-permute-done.cross_ref, bf16[3,16,512]{2,1,0:T(8,128)(2,1)S(1)} %collective-permute-done.2.core_ref, bf16[272,512]{1,0:T(8,128)(2,1)S(1)} %copy-done.1, ...), custom_call_target="tpu_custom_call" | custom-call | tf_op jit(solution)/shard_map/early/pallas_call | solution.py:383
  47.9 3.6 %collective-permute-start.7 = (bf16[528,256]{1,0:T(8,128)(2,1)S(1)}, bf16[528,256]{1,0:T(8,128)(2,1)S(1)}, u32[]{:S(2)}, u32[]{:S(2)}) collective-permute-start(bf16[528,256]{1,0:T(8,128)(2,1)S(1)} %get-tuple-element.17), channel_id=1, source_target_pairs={{0,1},{1,0},{2,3},{3,2},{4,5},{5,4},{6,7},{7,6},{8,9},{9,8},{10,11... | collective-permute-start | bytes 811016 | tf_op jit(solution)/shard_map/ppermute | solution.py:394
  51.6 1.2 %collective-permute-done.7.give_ref = bf16[528,256]{1,0:T(8,128)(2,1)S(1)} collective-permute-done((bf16[528,256]{1,0:T(8,128)(2,1)S(1)}, bf16[528,256]{1,0:T(8,128)(2,1)S(1)}, u32[]{:S(2)}, u32[]{:S(2)}) %collective-permute-start.7) | collective-permute-done | bytes 270368 | tf_op jit(solution)/shard_map/ppermute | solution.py:394
  52.8 7.2 %collective-permute-start.8 = (bf16[272,256]{1,0:T(8,128)(2,1)S(1)}, bf16[272,256]{1,0:T(8,128)(2,1)S(1)}, u32[]{:S(2)}, u32[]{:S(2)}) collective-permute-start(bf16[272,256]{1,0:T(8,128)(2,1)S(1)} %get-tuple-element.19), channel_id=1, source_target_pairs={{0,2},{1,3},{2,0},{3,1},{4,6},{5,7},{6,4},{7,5},{8,10},{9,11},{10,... | collective-permute-start | bytes 417800 | tf_op jit(solution)/shard_map/ppermute | solution.py:394
  60.1 3.5 %collective-permute-start.9 = (bf16[144,256]{1,0:T(8,128)(2,1)S(1)}, bf16[144,256]{1,0:T(8,128)(2,1)S(1)}, u32[]{:S(2)}, u32[]{:S(2)}) collective-permute-start(bf16[144,256]{1,0:T(8,128)(2,1)S(1)} %get-tuple-element.20), channel_id=1, source_target_pairs={{1,4},{2,63},{5,8},{6,3},{9,12},{10,7},{13,16},{14,11},{17,20},{18... | collective-permute-start | bytes 221192 | tf_op jit(solution)/shard_map/ppermute | solution.py:394
  63.5 1.4 %collective-permute-done.9.side_ref = bf16[144,256]{1,0:T(8,128)(2,1)S(1)} collective-permute-done((bf16[144,256]{1,0:T(8,128)(2,1)S(1)}, bf16[144,256]{1,0:T(8,128)(2,1)S(1)}, u32[]{:S(2)}, u32[]{:S(2)}) %collective-permute-start.9) | collective-permute-done | bytes 73760 | tf_op jit(solution)/shard_map/ppermute | solution.py:394
  64.9 12.4 %collective-permute-done.8.cross_ref = bf16[272,256]{1,0:T(8,128)(2,1)S(1)} collective-permute-done((bf16[272,256]{1,0:T(8,128)(2,1)S(1)}, bf16[272,256]{1,0:T(8,128)(2,1)S(1)}, u32[]{:S(2)}, u32[]{:S(2)}) %collective-permute-start.8) | collective-permute-done | bytes 139296 | tf_op jit(solution)/shard_map/ppermute | solution.py:394
  77.3 4.3 %transform.1 = (bf16[256,256]{1,0:T(8,128)(2,1)S(1)}, bf16[256,256]{1,0:T(8,128)(2,1)S(1)}) custom-call(s32[1,1]{1,0:T(1,128)} %bitcast.place_ref, f32[272,256]{1,0:T(8,128)S(1)} %get-tuple-element.18.keep_ref, bf16[272,256]{1,0:T(8,128)(2,1)S(1)} %collective-permute-done.8.cross_ref, bf16[144,256]{1,0:T(8,128)(2,1)S(1)} %collective-permute-done.9.side_ref), custom_call_target="tpu_custom_call" | custom-call | tf_op jit(solution)/shard_map/transform/pallas_call | solution.py:383
  81.6 3.0 %collective-permute-start.10 = (bf16[256,256]{1,0:T(8,128)(2,1)S(1)}, bf16[256,256]{1,0:T(8,128)(2,1)S(1)}, u32[]{:S(2)}, u32[]{:S(2)}) collective-permute-start(bf16[256,256]{1,0:T(8,128)(2,1)S(1)} %get-tuple-element.21.self_ref), channel_id=1, source_target_pairs={{0,1},{1,0},{2,3},{3,2},{4,5},{5,4},{6,7},{7,6},{8,9},{9,8},{10,11... | collective-permute-start | bytes 393224 | tf_op jit(solution)/shard_map/ppermute | solution.py:394
  85.7 0.8 blend.1
  (20 shorter events, 1.8 us)
Async XLA Ops:
  3.2 28.5 %collective-permute-start.1 = (bf16[272,512]{1,0:T(8,128)(2,1)}, bf16[272,512]{1,0:T(8,128)(2,1)S(1)}, u32[]{:S(2)}, u32[]{:S(2)}) collective-permute-start(bf16[272,512]{1,0:T(8,128)(2,1)} %get-tuple-element.15.own_ref), channel_id=1, source_target_pairs={{0,60},{1,61},{2,6},{3,7},{4,0},{5,1},{6,10},{7,11},{8,4},{9,5},{1... | collective-permute-start | bytes 835592 | tf_op jit(solution)/shard_map/ppermute | solution.py:394
  10.0 33.1 %collective-permute-start.5 = (bf16[272,512]{1,0:T(8,128)(2,1)}, bf16[272,512]{1,0:T(8,128)(2,1)S(1)}, u32[]{:S(2)}, u32[]{:S(2)}) collective-permute-start(bf16[272,512]{1,0:T(8,128)(2,1)} %get-tuple-element.15.own_ref), channel_id=1, source_target_pairs={{0,64},{1,65},{2,66},{3,67},{4,68},{5,69},{6,70},{7,71},{8,72},{9,... | collective-permute-start | bytes 835592 | tf_op jit(solution)/shard_map/ppermute | solution.py:394
  14.8 28.3 %collective-permute-start.6 = (bf16[272,512]{1,0:T(8,128)(2,1)}, bf16[272,512]{1,0:T(8,128)(2,1)S(1)}, u32[]{:S(2)}, u32[]{:S(2)}) collective-permute-start(bf16[272,512]{1,0:T(8,128)(2,1)} %get-tuple-element.15.own_ref), channel_id=1, source_target_pairs={{64,0},{65,1},{66,2},{67,3},{68,4},{69,5},{70,6},{71,7},{72,8},{73... | collective-permute-start | bytes 835592 | tf_op jit(solution)/shard_map/ppermute | solution.py:394
  18.3 13.4 %collective-permute-start = (bf16[2,16,512]{2,1,0:T(8,128)(2,1)S(1)}, bf16[2,16,512]{2,1,0:T(8,128)(2,1)S(1)}, u32[]{:S(2)}, u32[]{:S(2)}) collective-permute-start(bf16[2,16,512]{2,1,0:T(8,128)(2,1)S(1)} %get-tuple-element.23), channel_id=1, source_target_pairs={{0,2},{1,3},{2,0},{3,1},{4,6},{5,7},{6,4},{7,5},{8,10},{9,11},{10,... | collective-permute-start | bytes 98312 | tf_op jit(solution)/shard_map/ppermute | solution.py:394
  31.7 15.4 %collective-permute-start.3 = (bf16[272,512]{1,0:T(8,128)(2,1)S(1)}, bf16[272,512]{1,0:T(8,128)(2,1)S(1)}, u32[]{:S(2)}, u32[]{:S(2)}) collective-permute-start(bf16[272,512]{1,0:T(8,128)(2,1)S(1)} %collective-permute-done.1.beside_ref), channel_id=1, source_target_pairs={{0,64},{1,65},{2,66},{3,67},{4,68},{5,69},{6,70},{7,71},{8,72},{9,... | collective-permute-start | bytes 835592 | tf_op jit(solution)/shard_map/ppermute | solution.py:394
  36.5 10.6 %collective-permute-start.4 = (bf16[272,512]{1,0:T(8,128)(2,1)S(1)}, bf16[272,512]{1,0:T(8,128)(2,1)S(1)}, u32[]{:S(2)}, u32[]{:S(2)}) collective-permute-start(bf16[272,512]{1,0:T(8,128)(2,1)S(1)} %collective-permute-done.1.beside_ref), channel_id=1, source_target_pairs={{64,0},{65,1},{66,2},{67,3},{68,4},{69,5},{70,6},{71,7},{72,8},{73... | collective-permute-start | bytes 835592 | tf_op jit(solution)/shard_map/ppermute | solution.py:394
  38.5 5.5 %collective-permute-start.2 = (bf16[3,16,512]{2,1,0:T(8,128)(2,1)S(1)}, bf16[3,16,512]{2,1,0:T(8,128)(2,1)S(1)}, u32[]{:S(2)}, u32[]{:S(2)}) collective-permute-start(bf16[3,16,512]{2,1,0:T(8,128)(2,1)S(1)} %pad_maximum_fusion), channel_id=1, source_target_pairs={{0,1},{1,0},{2,3},{3,2},{4,5},{5,4},{6,7},{7,6},{8,9},{9,8},{10,11... | collective-permute-start | bytes 147464 | tf_op jit(solution)/shard_map/ppermute | solution.py:394
  44.0 0.8 copy-start
  44.8 1.0 %copy-start.1 = (bf16[272,512]{1,0:T(8,128)(2,1)S(1)}, bf16[272,512]{1,0:T(8,128)(2,1)}, u32[]{:S(2)}) copy-start(bf16[272,512]{1,0:T(8,128)(2,1)} %get-tuple-element.15.own_ref) | copy-start | bytes 835588
  47.1 37.6 %copy-start.3 = (f32[2,4,16]{2,1,0:T(4,128)S(1)}, f32[2,4,16]{2,1,0:T(4,128)}, u32[]{:S(2)}) copy-start(f32[2,4,16]{2,1,0:T(4,128)} %param.9) | copy-start | bytes 1540
  47.1 37.7 %copy-start.2 = (bf16[2,4,16,256]{3,2,1,0:T(8,128)(2,1)S(1)}, bf16[2,4,16,256]{3,2,1,0:T(8,128)(2,1)}, u32[]{:S(2)}) copy-start(bf16[2,4,16,256]{3,2,1,0:T(8,128)(2,1)} %state_ref.3) | copy-start | bytes 196612
  47.9 4.8 %collective-permute-start.7 = (bf16[528,256]{1,0:T(8,128)(2,1)S(1)}, bf16[528,256]{1,0:T(8,128)(2,1)S(1)}, u32[]{:S(2)}, u32[]{:S(2)}) collective-permute-start(bf16[528,256]{1,0:T(8,128)(2,1)S(1)} %get-tuple-element.17), channel_id=1, source_target_pairs={{0,1},{1,0},{2,3},{3,2},{4,5},{5,4},{6,7},{7,6},{8,9},{9,8},{10,11... | collective-permute-start | bytes 811016 | tf_op jit(solution)/shard_map/ppermute | solution.py:394
  52.8 24.5 %collective-permute-start.8 = (bf16[272,256]{1,0:T(8,128)(2,1)S(1)}, bf16[272,256]{1,0:T(8,128)(2,1)S(1)}, u32[]{:S(2)}, u32[]{:S(2)}) collective-permute-start(bf16[272,256]{1,0:T(8,128)(2,1)S(1)} %get-tuple-element.19), channel_id=1, source_target_pairs={{0,2},{1,3},{2,0},{3,1},{4,6},{5,7},{6,4},{7,5},{8,10},{9,11},{10,... | collective-permute-start | bytes 417800 | tf_op jit(solution)/shard_map/ppermute | solution.py:394
  60.1 4.9 %collective-permute-start.9 = (bf16[144,256]{1,0:T(8,128)(2,1)S(1)}, bf16[144,256]{1,0:T(8,128)(2,1)S(1)}, u32[]{:S(2)}, u32[]{:S(2)}) collective-permute-start(bf16[144,256]{1,0:T(8,128)(2,1)S(1)} %get-tuple-element.20), channel_id=1, source_target_pairs={{1,4},{2,63},{5,8},{6,3},{9,12},{10,7},{13,16},{14,11},{17,20},{18... | collective-permute-start | bytes 221192 | tf_op jit(solution)/shard_map/ppermute | solution.py:394
  81.6 4.0 %collective-permute-start.10 = (bf16[256,256]{1,0:T(8,128)(2,1)S(1)}, bf16[256,256]{1,0:T(8,128)(2,1)S(1)}, u32[]{:S(2)}, u32[]{:S(2)}) collective-permute-start(bf16[256,256]{1,0:T(8,128)(2,1)S(1)} %get-tuple-element.21.self_ref), channel_id=1, source_target_pairs={{0,1},{1,0},{2,3},{3,2},{4,5},{5,4},{6,7},{7,6},{8,9},{9,8},{10,11... | collective-permute-start | bytes 393224 | tf_op jit(solution)/shard_map/ppermute | solution.py:394

commit v4 on v3

--- a/solution.py
+++ b/solution.py
@@ -14,7 +14,8 @@
 SIDE = 2
 TEAM = 4
 EXTRA = 16
-VMEM_LIMIT = 40 * 1024 * 1024
+RELAY_ROWS = 208
+VMEM_LIMIT = 32 * 1024 * 1024
 
 ACROSS = (((1,), (1,)), ((), ()))
 PLAIN = (((1,), (0,)), ((), ()))
@@ -45,7 +46,8 @@
     prec_hbm,
     local_hbm,
     tile_ref,
-    pack_ref,
+    near_ref,
+    far_ref,
     anom_ref,
     innov_ref,
     prec_ref,
@@ -79,9 +81,11 @@
         return weight_ref[...]
 
     weight_ref[...] = jnp.zeros_like(weight_ref)
-    for reader in range(TEAM):
-        beside = reader + (-TEAM if reader >= SIDE else TEAM)
-        pack_ref[reader] = jnp.concatenate(split(weights((reader - place, beside - place))), axis=0)
+    for index in range(TEAM):
+        reader = place ^ index
+        beside = reader + jnp.where(reader >= SIDE, -TEAM, TEAM)
+        pack_ref = near_ref if index < SIDE else far_ref
+        pack_ref[index % SIDE] = jnp.concatenate(split(weights((reader - place, beside - place))), axis=0)
 
     high, low = split(weights((0 * place, 1 - 2 * (place % 2))))
     copies[1].wait()
@@ -103,15 +107,11 @@
     return parts[: EXTRA // 2] + parts[EXTRA // 2 :]
 
 
-def team_weights(place_ref, pack_ref, cross_ref, core_ref, index):
-    return joined(
-        (
-            lambda: pack_ref[place_ref[0, 0]],
-            lambda: core_ref[0],
-            lambda: cross_ref[0],
-            lambda: core_ref[1],
-        )[index]()
-    )
+def relay_kernel(near_ref, cross_ref, beside_ref, out_ref):
+    depth = beside_ref.shape[0]
+    out_ref[pl.ds(0, EXTRA), :] = near_ref[1]
+    out_ref[pl.ds(EXTRA, EXTRA), :] = cross_ref[1]
+    out_ref[pl.ds(2 * EXTRA, RELAY_ROWS), :] = beside_ref[pl.ds(depth - RELAY_ROWS, RELAY_ROWS), :]
 
 
 def outer_weights(place_ref, beside_ref, core_ref):
@@ -119,7 +119,7 @@
     place = place_ref[0, 0]
     used = 2 * NEAR_LAT
     direct = beside_ref[pl.ds(members, EXTRA), :].astype(jnp.float32)[2 : 2 + 2 * used]
-    passed = core_ref[2].astype(jnp.float32)[2 : 2 + 2 * used]
+    passed = core_ref[pl.ds(core_ref.shape[0] - EXTRA, EXTRA), :].astype(jnp.float32)[2 : 2 + 2 * used]
     outer = (place == 0) | (place == TEAM - 1)
     direct = direct[:NEAR_LAT] + direct[used : used + NEAR_LAT]
     passed = passed[NEAR_LAT:used] + passed[used + NEAR_LAT :]
@@ -134,10 +134,10 @@
 
 
 def early_kernel(
-    place_ref, pack_ref, cross_ref, core_ref, own_ref, below_ref, above_ref, beside_ref, out_ref
+    place_ref, near_ref, cross_ref, core_ref, own_ref, below_ref, above_ref, beside_ref, out_ref
 ):
-    for index in range(TEAM):
-        weight = team_weights(place_ref, pack_ref, cross_ref, core_ref, index)
+    for index, pack in enumerate((near_ref[0], core_ref[pl.ds(0, EXTRA), :], cross_ref[0], core_ref[pl.ds(EXTRA, EXTRA), :])):
+        weight = joined(pack)
         total = None
         for lat, tile_ref in enumerate((below_ref, own_ref, above_ref)):
             part = weighted(tile_ref, weight[lat : lat + 1])
@@ -193,7 +193,7 @@
         total = share_ref[index]
         if index >= SIDE:
             if index < TEAM:
-                weight = joined(cross_ref[0] if index == SIDE else core_ref[1])[NEAR_LAT:]
+                weight = joined(cross_ref[0] if index == SIDE else core_ref[pl.ds(EXTRA, EXTRA), :])[NEAR_LAT:]
             else:
                 weight = outer_weights(place_ref, beside_ref, core_ref)
             for lat, tile_ref in tiles:
@@ -412,9 +412,9 @@
         step = {1: TEAM - 1, TEAM - 2: 1 - TEAM}.get(lon % TEAM)
         return None if step is None else (lat, lon + step)
 
-    own, pack = call(
+    own, near, far = call(
         prepare_kernel,
-        [((members + EXTRA, obs_rows), bf16), ((TEAM, EXTRA, obs_rows), bf16)],
+        [((members + EXTRA, obs_rows), bf16)] + [((SIDE, EXTRA, obs_rows), bf16)] * 2,
         [SMEM] * 3 + [ANY] * 4,
         place,
         obs_blocks,
@@ -433,24 +433,28 @@
         ],
         limit=56 * 1024 * 1024,
     )
-    index = place[0, 0]
-    far = jnp.where(index % 2 == 0, jnp.stack([pack[2], pack[3]]), jnp.stack([pack[3], pack[2]]))
-    near = jnp.where(index % 2 == 0, jnp.stack([pack[0], pack[1]]), jnp.stack([pack[1], pack[0]]))
-    far, near = jnp.where(index < SIDE, far, near), jnp.where(index < SIDE, near, far)
     cross = send(far, across_z)
     beside = send(own, along_x)
     below = send(own, up)
     above = send(own, down)
     beside_below = send(beside, up)
     beside_above = send(beside, down)
-    core = send(jnp.stack([near[1], cross[1], beside[members:]]), other_core)
+    (core,) = call(
+        relay_kernel,
+        [((2 * EXTRA + RELAY_ROWS, obs_rows), bf16)],
+        [VMEM] * 3,
+        near,
+        cross,
+        beside,
+    )
+    core = send(core, other_core)
 
     (shares,) = call(
         early_kernel,
         [((TEAM + 1, members + EXTRA, members), f32)],
         [SMEM] + [VMEM] * 7,
         place,
-        pack,
+        near,
         cross,
         core,
         own,

time: 87.1 us -> 78.6 us (0.902)
  starting transfers between devices: 49.9 us -> 44.9 us
  waiting for transfers between devices: 22.1 us -> 19.5 us
    ppermute x11, starting transfers between devices: 49.9 us -> 44.9 us  [send(): lax.ppermute(value, ('lat', 'lon'), shifts(lat_count, lon_count, move))]
    ppermute x11, waiting for transfers between devices: 22.1 us -> 19.5 us  [send(): lax.ppermute(value, ('lat', 'lon'), shifts(lat_count, lon_count, move))]
    unnamed x8 -> x10, local copies, waits for them, and re-layouts: 1.81 us -> 2.48 us
    pallas_call x7 -> x8, Pallas kernels: 10.1 us -> 10.1 us  [call(): pl.pallas_call(kernel, out_shape=tuple((jax.ShapeDtypeStruct(*out) for ou...]
  transfers between devices with their start and end apart: 11 -> 11, of which waited for: 6 -> 5; matrix products, arithmetic and copies ran while one was open for 2% -> 0% of each run, Pallas kernels for 2% -> 2%
where the time goes in v4:
time: 78.6 us; the launch traced here: 78 us
  starting transfers between devices  44.9 us (57%)
  waiting for transfers between devices  19.5 us (25%)
  Pallas kernels  10.1 us (13%)
  local copies, waits for them, and re-layouts  2.56 us (3%)
  between operations  0.89 us (1%)
    ppermute x11, starting transfers between devices, send(): lax.ppermute(value, ('lat', 'lon'), shifts(lat_count, lon_count, move))  44.9 us
    ppermute x11, waiting for transfers between devices, send(): lax.ppermute(value, ('lat', 'lon'), shifts(lat_count, lon_count, move))  19.5 us
    pallas_call x8, Pallas kernels, call(): pl.pallas_call(kernel, out_shape=tuple((jax.ShapeDtypeStruct(*out) for ou...  10.1 us
    unnamed x10, local copies, waits for them, and re-layouts  2.48 us
  transfers between devices with their start and end apart: 11, of which 5 were waited for; matrix products, arithmetic and copies ran while one was open for 0% of the time, Pallas kernels for 2%

profile of v4, /device:TPU:97, one launch (start us, length us, event | category | flops | bytes accessed | tf_op | source)
XLA Modules:
  0.0 78.0 jit_solution(3476977160761099903)
XLA Ops:
  0.7 2.5 %prepare.1 = (bf16[272,512]{1,0:T(8,128)(2,1)}, bf16[2,16,512]{2,1,0:T(8,128)(2,1)}, bf16[2,16,512]{2,1,0:T(8,128)(2,1)}) custom-call(s32[1,1]{1,0:T(1,128)} %bitcast.place_ref, s32[1,1]{1,0:T(1,128)S(6)} %copy.9.blocks_ref, s32[1,60]{1,0:T(1,128)} %bitcast.6, bf16[512,256]{1,0:T(8,128)(2,1)} %bitcast.4, bf16[1,512]{1,0:T(2,128)(2,1)} %innov_hbm.1, ...), custom_call_target="tpu_custom_call" | custom-call | tf_op jit(solution)/shard_map/prepare/pallas_call | solution.py:383
  3.2 6.8 %collective-permute-start.1 = (bf16[272,512]{1,0:T(8,128)(2,1)}, bf16[272,512]{1,0:T(8,128)(2,1)S(1)}, u32[]{:S(2)}, u32[]{:S(2)}) collective-permute-start(bf16[272,512]{1,0:T(8,128)(2,1)} %get-tuple-element.17.own_ref), channel_id=1, source_target_pairs={{0,60},{1,61},{2,6},{3,7},{4,0},{5,1},{6,10},{7,11},{8,4},{9,5},{1... | collective-permute-start | bytes 835592 | tf_op jit(solution)/shard_map/ppermute | solution.py:394
  10.0 9.0 %collective-permute-start = (bf16[2,16,512]{2,1,0:T(8,128)(2,1)}, bf16[2,16,512]{2,1,0:T(8,128)(2,1)S(1)}, u32[]{:S(2)}, u32[]{:S(2)}) collective-permute-start(bf16[2,16,512]{2,1,0:T(8,128)(2,1)} %get-tuple-element.15), channel_id=1, source_target_pairs={{0,2},{1,3},{2,0},{3,1},{4,6},{5,7},{6,4},{7,5},{8,10},{9,11},{10,... | collective-permute-start | bytes 98312 | tf_op jit(solution)/shard_map/ppermute | solution.py:394
  19.1 2.6 %collective-permute-start.5 = (bf16[272,512]{1,0:T(8,128)(2,1)}, bf16[272,512]{1,0:T(8,128)(2,1)S(1)}, u32[]{:S(2)}, u32[]{:S(2)}) collective-permute-start(bf16[272,512]{1,0:T(8,128)(2,1)} %get-tuple-element.17.own_ref), channel_id=1, source_target_pairs={{0,64},{1,65},{2,66},{3,67},{4,68},{5,69},{6,70},{7,71},{8,72},{9,... | collective-permute-start | bytes 835592 | tf_op jit(solution)/shard_map/ppermute | solution.py:394
  21.7 2.6 %collective-permute-start.6 = (bf16[272,512]{1,0:T(8,128)(2,1)}, bf16[272,512]{1,0:T(8,128)(2,1)S(1)}, u32[]{:S(2)}, u32[]{:S(2)}) collective-permute-start(bf16[272,512]{1,0:T(8,128)(2,1)} %get-tuple-element.17.own_ref), channel_id=1, source_target_pairs={{64,0},{65,1},{66,2},{67,3},{68,4},{69,5},{70,6},{71,7},{72,8},{73... | collective-permute-start | bytes 835592 | tf_op jit(solution)/shard_map/ppermute | solution.py:394
  24.4 3.9 %collective-permute-start.3 = (bf16[272,512]{1,0:T(8,128)(2,1)S(1)}, bf16[272,512]{1,0:T(8,128)(2,1)S(1)}, u32[]{:S(2)}, u32[]{:S(2)}) collective-permute-start(bf16[272,512]{1,0:T(8,128)(2,1)S(1)} %collective-permute-done.1.beside_ref), channel_id=1, source_target_pairs={{0,64},{1,65},{2,66},{3,67},{4,68},{5,69},{6,70},{7,71},{8,72},{9,... | collective-permute-start | bytes 835592 | tf_op jit(solution)/shard_map/ppermute | solution.py:394
  28.2 1.9 %collective-permute-start.4 = (bf16[272,512]{1,0:T(8,128)(2,1)S(1)}, bf16[272,512]{1,0:T(8,128)(2,1)S(1)}, u32[]{:S(2)}, u32[]{:S(2)}) collective-permute-start(bf16[272,512]{1,0:T(8,128)(2,1)S(1)} %collective-permute-done.1.beside_ref), channel_id=1, source_target_pairs={{64,0},{65,1},{66,2},{67,3},{68,4},{69,5},{70,6},{71,7},{72,8},{73... | collective-permute-start | bytes 835592 | tf_op jit(solution)/shard_map/ppermute | solution.py:394
  30.2 0.7 copy-done.2
  31.0 4.0 %collective-permute-start.2 = (bf16[240,512]{1,0:T(8,128)(2,1)S(1)}, bf16[240,512]{1,0:T(8,128)(2,1)S(1)}, u32[]{:S(2)}, u32[]{:S(2)}) collective-permute-start(bf16[240,512]{1,0:T(8,128)(2,1)S(1)} %relay.1), channel_id=1, source_target_pairs={{0,1},{1,0},{2,3},{3,2},{4,5},{5,4},{6,7},{7,6},{8,9},{9,8},{10,11... | collective-permute-start | bytes 737288 | tf_op jit(solution)/shard_map/ppermute | solution.py:394
  35.0 1.1 %collective-permute-done.2.core_ref = bf16[240,512]{1,0:T(8,128)(2,1)S(1)} collective-permute-done((bf16[240,512]{1,0:T(8,128)(2,1)S(1)}, bf16[240,512]{1,0:T(8,128)(2,1)S(1)}, u32[]{:S(2)}, u32[]{:S(2)}) %collective-permute-start.2) | collective-permute-done | bytes 245792 | tf_op jit(solution)/shard_map/ppermute | solution.py:394
  36.1 1.0 %copy-done = bf16[272,512]{1,0:T(8,128)(2,1)S(1)} copy-done((bf16[272,512]{1,0:T(8,128)(2,1)S(1)}, bf16[272,512]{1,0:T(8,128)(2,1)}, u32[]{:S(2)}) %copy-start) | copy-done | bytes 278552
  37.0 0.8 copy-done.3
  37.8 1.3 %early.1.share_ref = f32[5,272,256]{2,1,0:T(8,128)S(1)} custom-call(s32[1,1]{1,0:T(1,128)} %bitcast.place_ref, bf16[2,16,512]{2,1,0:T(8,128)(2,1)S(1)} %copy-done.3, bf16[2,16,512]{2,1,0:T(8,128)(2,1)S(1)} %collective-permute-done.cross_ref, bf16[240,512]{1,0:T(8,128)(2,1)S(1)} %collective-permute-done.2.core_ref, bf16[272,512]{1,0:T(8,128)(2,1)S(1)} %copy-done, ...), custom_call_target="tpu_custom_call" | custom-call | tf_op jit(solution)/shard_map/early/pallas_call | solution.py:383
  39.2 0.7 late.1
  39.9 3.1 %collective-permute-start.7 = (bf16[528,256]{1,0:T(8,128)(2,1)S(1)}, bf16[528,256]{1,0:T(8,128)(2,1)S(1)}, u32[]{:S(2)}, u32[]{:S(2)}) collective-permute-start(bf16[528,256]{1,0:T(8,128)(2,1)S(1)} %get-tuple-element.19), channel_id=1, source_target_pairs={{0,1},{1,0},{2,3},{3,2},{4,5},{5,4},{6,7},{7,6},{8,9},{9,8},{10,11... | collective-permute-start | bytes 811016 | tf_op jit(solution)/shard_map/ppermute | solution.py:394
  43.1 1.2 %collective-permute-done.7.give_ref = bf16[528,256]{1,0:T(8,128)(2,1)S(1)} collective-permute-done((bf16[528,256]{1,0:T(8,128)(2,1)S(1)}, bf16[528,256]{1,0:T(8,128)(2,1)S(1)}, u32[]{:S(2)}, u32[]{:S(2)}) %collective-permute-start.7) | collective-permute-done | bytes 270368 | tf_op jit(solution)/shard_map/ppermute | solution.py:394
  44.4 7.1 %collective-permute-start.8 = (bf16[272,256]{1,0:T(8,128)(2,1)S(1)}, bf16[272,256]{1,0:T(8,128)(2,1)S(1)}, u32[]{:S(2)}, u32[]{:S(2)}) collective-permute-start(bf16[272,256]{1,0:T(8,128)(2,1)S(1)} %get-tuple-element.21), channel_id=1, source_target_pairs={{0,2},{1,3},{2,0},{3,1},{4,6},{5,7},{6,4},{7,5},{8,10},{9,11},{10,... | collective-permute-start | bytes 417800 | tf_op jit(solution)/shard_map/ppermute | solution.py:394
  51.4 1.3 %collective-permute-start.9 = (bf16[144,256]{1,0:T(8,128)(2,1)S(1)}, bf16[144,256]{1,0:T(8,128)(2,1)S(1)}, u32[]{:S(2)}, u32[]{:S(2)}) collective-permute-start(bf16[144,256]{1,0:T(8,128)(2,1)S(1)} %get-tuple-element.22), channel_id=1, source_target_pairs={{1,4},{2,63},{5,8},{6,3},{9,12},{10,7},{13,16},{14,11},{17,20},{18... | collective-permute-start | bytes 221192 | tf_op jit(solution)/shard_map/ppermute | solution.py:394
  52.7 1.4 %collective-permute-done.9.side_ref = bf16[144,256]{1,0:T(8,128)(2,1)S(1)} collective-permute-done((bf16[144,256]{1,0:T(8,128)(2,1)S(1)}, bf16[144,256]{1,0:T(8,128)(2,1)S(1)}, u32[]{:S(2)}, u32[]{:S(2)}) %collective-permute-start.9) | collective-permute-done | bytes 73760 | tf_op jit(solution)/shard_map/ppermute | solution.py:394
  54.1 15.3 %collective-permute-done.8.cross_ref = bf16[272,256]{1,0:T(8,128)(2,1)S(1)} collective-permute-done((bf16[272,256]{1,0:T(8,128)(2,1)S(1)}, bf16[272,256]{1,0:T(8,128)(2,1)S(1)}, u32[]{:S(2)}, u32[]{:S(2)}) %collective-permute-start.8) | collective-permute-done | bytes 139296 | tf_op jit(solution)/shard_map/ppermute | solution.py:394
  69.5 4.3 %transform.1 = (bf16[256,256]{1,0:T(8,128)(2,1)S(1)}, bf16[256,256]{1,0:T(8,128)(2,1)S(1)}) custom-call(s32[1,1]{1,0:T(1,128)} %bitcast.place_ref, f32[272,256]{1,0:T(8,128)S(1)} %get-tuple-element.20.keep_ref, bf16[272,256]{1,0:T(8,128)(2,1)S(1)} %collective-permute-done.8.cross_ref, bf16[144,256]{1,0:T(8,128)(2,1)S(1)} %collective-permute-done.9.side_ref), custom_call_target="tpu_custom_call" | custom-call | tf_op jit(solution)/shard_map/transform/pallas_call | solution.py:383
  73.8 2.5 %collective-permute-start.10 = (bf16[256,256]{1,0:T(8,128)(2,1)S(1)}, bf16[256,256]{1,0:T(8,128)(2,1)S(1)}, u32[]{:S(2)}, u32[]{:S(2)}) collective-permute-start(bf16[256,256]{1,0:T(8,128)(2,1)S(1)} %get-tuple-element.23.self_ref), channel_id=1, source_target_pairs={{0,1},{1,0},{2,3},{3,2},{4,5},{5,4},{6,7},{7,6},{8,9},{9,8},{10,11... | collective-permute-start | bytes 393224 | tf_op jit(solution)/shard_map/ppermute | solution.py:394
  76.7 0.5 collective-permute-done.10.inner_ref
  77.2 0.8 %blend.1 = bf16[2,4,16,256]{3,2,1,0:T(8,128)(2,1)} custom-call(s32[1,1]{1,0:T(1,128)} %bitcast.place_ref, bf16[256,256]{1,0:T(8,128)(2,1)S(1)} %collective-permute-done.10.inner_ref, f32[2,4,16,256]{3,2,1,0:T(8,128)S(1)} %product.1.part_ref, bf16[2,4,16,256]{3,2,1,0:T(8,128)(2,1)S(1)} %copy-done.1), custom_call_target="tpu_custom_call" | custom-call | tf_op jit(solution)/shard_map/blend/pallas_call | solution.py:383
  (17 shorter events, 0.6 us)
Async XLA Ops:
  3.2 21.2 %collective-permute-start.1 = (bf16[272,512]{1,0:T(8,128)(2,1)}, bf16[272,512]{1,0:T(8,128)(2,1)S(1)}, u32[]{:S(2)}, u32[]{:S(2)}) collective-permute-start(bf16[272,512]{1,0:T(8,128)(2,1)} %get-tuple-element.17.own_ref), channel_id=1, source_target_pairs={{0,60},{1,61},{2,6},{3,7},{4,0},{5,1},{6,10},{7,11},{8,4},{9,5},{1... | collective-permute-start | bytes 835592 | tf_op jit(solution)/shard_map/ppermute | solution.py:394
  10.0 20.1 %collective-permute-start = (bf16[2,16,512]{2,1,0:T(8,128)(2,1)}, bf16[2,16,512]{2,1,0:T(8,128)(2,1)S(1)}, u32[]{:S(2)}, u32[]{:S(2)}) collective-permute-start(bf16[2,16,512]{2,1,0:T(8,128)(2,1)} %get-tuple-element.15), channel_id=1, source_target_pairs={{0,2},{1,3},{2,0},{3,1},{4,6},{5,7},{6,4},{7,5},{8,10},{9,11},{10,... | collective-permute-start | bytes 98312 | tf_op jit(solution)/shard_map/ppermute | solution.py:394
  19.1 15.9 %collective-permute-start.5 = (bf16[272,512]{1,0:T(8,128)(2,1)}, bf16[272,512]{1,0:T(8,128)(2,1)S(1)}, u32[]{:S(2)}, u32[]{:S(2)}) collective-permute-start(bf16[272,512]{1,0:T(8,128)(2,1)} %get-tuple-element.17.own_ref), channel_id=1, source_target_pairs={{0,64},{1,65},{2,66},{3,67},{4,68},{5,69},{6,70},{7,71},{8,72},{9,... | collective-permute-start | bytes 835592 | tf_op jit(solution)/shard_map/ppermute | solution.py:394
  21.7 13.2 %collective-permute-start.6 = (bf16[272,512]{1,0:T(8,128)(2,1)}, bf16[272,512]{1,0:T(8,128)(2,1)S(1)}, u32[]{:S(2)}, u32[]{:S(2)}) collective-permute-start(bf16[272,512]{1,0:T(8,128)(2,1)} %get-tuple-element.17.own_ref), channel_id=1, source_target_pairs={{64,0},{65,1},{66,2},{67,3},{68,4},{69,5},{70,6},{71,7},{72,8},{73... | collective-permute-start | bytes 835592 | tf_op jit(solution)/shard_map/ppermute | solution.py:394
  24.4 14.8 %collective-permute-start.3 = (bf16[272,512]{1,0:T(8,128)(2,1)S(1)}, bf16[272,512]{1,0:T(8,128)(2,1)S(1)}, u32[]{:S(2)}, u32[]{:S(2)}) collective-permute-start(bf16[272,512]{1,0:T(8,128)(2,1)S(1)} %collective-permute-done.1.beside_ref), channel_id=1, source_target_pairs={{0,64},{1,65},{2,66},{3,67},{4,68},{5,69},{6,70},{7,71},{8,72},{9,... | collective-permute-start | bytes 835592 | tf_op jit(solution)/shard_map/ppermute | solution.py:394
  28.2 10.9 %collective-permute-start.4 = (bf16[272,512]{1,0:T(8,128)(2,1)S(1)}, bf16[272,512]{1,0:T(8,128)(2,1)S(1)}, u32[]{:S(2)}, u32[]{:S(2)}) collective-permute-start(bf16[272,512]{1,0:T(8,128)(2,1)S(1)} %collective-permute-done.1.beside_ref), channel_id=1, source_target_pairs={{64,0},{65,1},{66,2},{67,3},{68,4},{69,5},{70,6},{71,7},{72,8},{73... | collective-permute-start | bytes 835592 | tf_op jit(solution)/shard_map/ppermute | solution.py:394
  30.2 0.8 copy-start.2
  31.0 5.1 %collective-permute-start.2 = (bf16[240,512]{1,0:T(8,128)(2,1)S(1)}, bf16[240,512]{1,0:T(8,128)(2,1)S(1)}, u32[]{:S(2)}, u32[]{:S(2)}) collective-permute-start(bf16[240,512]{1,0:T(8,128)(2,1)S(1)} %relay.1), channel_id=1, source_target_pairs={{0,1},{1,0},{2,3},{3,2},{4,5},{5,4},{6,7},{7,6},{8,9},{9,8},{10,11... | collective-permute-start | bytes 737288 | tf_op jit(solution)/shard_map/ppermute | solution.py:394
  36.1 1.0 %copy-start = (bf16[272,512]{1,0:T(8,128)(2,1)S(1)}, bf16[272,512]{1,0:T(8,128)(2,1)}, u32[]{:S(2)}) copy-start(bf16[272,512]{1,0:T(8,128)(2,1)} %get-tuple-element.17.own_ref) | copy-start | bytes 835588
  37.0 0.8 copy-start.3
  39.1 37.1 %copy-start.4 = (f32[2,4,16]{2,1,0:T(4,128)S(1)}, f32[2,4,16]{2,1,0:T(4,128)}, u32[]{:S(2)}) copy-start(f32[2,4,16]{2,1,0:T(4,128)} %param.9) | copy-start | bytes 1540
  39.1 37.2 %copy-start.1 = (bf16[2,4,16,256]{3,2,1,0:T(8,128)(2,1)S(1)}, bf16[2,4,16,256]{3,2,1,0:T(8,128)(2,1)}, u32[]{:S(2)}) copy-start(bf16[2,4,16,256]{3,2,1,0:T(8,128)(2,1)} %state_ref.3) | copy-start | bytes 196612
  39.9 4.3 %collective-permute-start.7 = (bf16[528,256]{1,0:T(8,128)(2,1)S(1)}, bf16[528,256]{1,0:T(8,128)(2,1)S(1)}, u32[]{:S(2)}, u32[]{:S(2)}) collective-permute-start(bf16[528,256]{1,0:T(8,128)(2,1)S(1)} %get-tuple-element.19), channel_id=1, source_target_pairs={{0,1},{1,0},{2,3},{3,2},{4,5},{5,4},{6,7},{7,6},{8,9},{9,8},{10,11... | collective-permute-start | bytes 811016 | tf_op jit(solution)/shard_map/ppermute | solution.py:394
  44.4 25.1 %collective-permute-start.8 = (bf16[272,256]{1,0:T(8,128)(2,1)S(1)}, bf16[272,256]{1,0:T(8,128)(2,1)S(1)}, u32[]{:S(2)}, u32[]{:S(2)}) collective-permute-start(bf16[272,256]{1,0:T(8,128)(2,1)S(1)} %get-tuple-element.21), channel_id=1, source_target_pairs={{0,2},{1,3},{2,0},{3,1},{4,6},{5,7},{6,4},{7,5},{8,10},{9,11},{10,... | collective-permute-start | bytes 417800 | tf_op jit(solution)/shard_map/ppermute | solution.py:394
  51.4 2.7 %collective-permute-start.9 = (bf16[144,256]{1,0:T(8,128)(2,1)S(1)}, bf16[144,256]{1,0:T(8,128)(2,1)S(1)}, u32[]{:S(2)}, u32[]{:S(2)}) collective-permute-start(bf16[144,256]{1,0:T(8,128)(2,1)S(1)} %get-tuple-element.22), channel_id=1, source_target_pairs={{1,4},{2,63},{5,8},{6,3},{9,12},{10,7},{13,16},{14,11},{17,20},{18... | collective-permute-start | bytes 221192 | tf_op jit(solution)/shard_map/ppermute | solution.py:394
  73.8 3.5 %collective-permute-start.10 = (bf16[256,256]{1,0:T(8,128)(2,1)S(1)}, bf16[256,256]{1,0:T(8,128)(2,1)S(1)}, u32[]{:S(2)}, u32[]{:S(2)}) collective-permute-start(bf16[256,256]{1,0:T(8,128)(2,1)S(1)} %get-tuple-element.23.self_ref), channel_id=1, source_target_pairs={{0,1},{1,0},{2,3},{3,2},{4,5},{5,4},{6,7},{7,6},{8,9},{9,8},{10,11... | collective-permute-start | bytes 393224 | tf_op jit(solution)/shard_map/ppermute | solution.py:394

commit v5 on v4

--- a/solution.py
+++ b/solution.py
@@ -133,15 +133,20 @@
     return dot(scaled, tile_ref[pl.ds(0, members), :], ACROSS)
 
 
+def outer_lats(place_ref, weight):
+    below, above = weight[:1], weight[2 * LAT_REACH : 2 * LAT_REACH + 1]
+    even = place_ref[0, 0] % 2 == 0
+    return jnp.where(even, below, above), jnp.where(even, above, below)
+
+
 def early_kernel(
-    place_ref, near_ref, cross_ref, core_ref, own_ref, below_ref, above_ref, beside_ref, out_ref
+    place_ref, near_ref, cross_ref, core_ref, own_ref, first_ref, second_ref, beside_ref, out_ref
 ):
     for index, pack in enumerate((near_ref[0], core_ref[pl.ds(0, EXTRA), :], cross_ref[0], core_ref[pl.ds(EXTRA, EXTRA), :])):
         weight = joined(pack)
-        total = None
-        for lat, tile_ref in enumerate((below_ref, own_ref, above_ref)):
-            part = weighted(tile_ref, weight[lat : lat + 1])
-            total = part if total is None else total + part
+        first, second = outer_lats(place_ref, weight)
+        total = weighted(own_ref, weight[LAT_REACH : LAT_REACH + 1])
+        total = total + weighted(first_ref, first) + weighted(second_ref, second)
         if index >= SIDE:
             row = NEAR_LAT + LAT_REACH
             total = total + weighted(beside_ref, weight[row : row + 1])
@@ -180,15 +185,14 @@
     cross_ref,
     core_ref,
     beside_ref,
-    below_ref,
-    above_ref,
+    first_ref,
+    second_ref,
     share_ref,
     give_ref,
     keep_ref,
     body_ref,
     tail_ref,
 ):
-    tiles = ((0, below_ref), (2 * LAT_REACH, above_ref))
     for index in range(TEAM + 1):
         total = share_ref[index]
         if index >= SIDE:
@@ -196,8 +200,8 @@
                 weight = joined(cross_ref[0] if index == SIDE else core_ref[pl.ds(EXTRA, EXTRA), :])[NEAR_LAT:]
             else:
                 weight = outer_weights(place_ref, beside_ref, core_ref)
-            for lat, tile_ref in tiles:
-                total = total + weighted(tile_ref, weight[lat : lat + 1])
+            first, second = outer_lats(place_ref, weight)
+            total = total + weighted(first_ref, first) + weighted(second_ref, second)
         body, tail = packed(total)
         body_ref[index] = body
         tail_ref[index, pl.ds(0, 2), :] = tail
@@ -379,10 +383,10 @@
     place = (lax.axis_index("lon") % TEAM).astype(jnp.int32).reshape(1, 1)
     bf16, f32 = jnp.bfloat16, jnp.float32
 
-    def call(kernel, outs, ins, *operands, scratch=(), limit=VMEM_LIMIT):
+    def call(kernel, outs, ins, *operands, scratch=(), limit=VMEM_LIMIT, pinned=False):
         return pl.pallas_call(
             kernel,
-            out_shape=tuple(jax.ShapeDtypeStruct(*out) for out in outs),
+            out_shape=tuple((pltpu.VMEM if pinned else jax.ShapeDtypeStruct)(*out) for out in outs),
             in_specs=ins,
             out_specs=(VMEM,) * len(outs),
             scratch_shapes=scratch,
@@ -393,11 +397,11 @@
     def send(value, move):
         return lax.ppermute(value, ("lat", "lon"), shifts(lat_count, lon_count, move))
 
-    def up(lat, lon):
-        return lat + 1, lon
-
-    def down(lat, lon):
-        return lat - 1, lon
+    def first_move(lat, lon):
+        return lat + 1 - 2 * (lon % 2), lon
+
+    def second_move(lat, lon):
+        return lat - 1 + 2 * (lon % 2), lon
 
     def other_core(lat, lon):
         return lat, lon ^ 1
@@ -432,13 +436,14 @@
             pltpu.SemaphoreType.DMA((4,)),
         ],
         limit=56 * 1024 * 1024,
+        pinned=True,
     )
     cross = send(far, across_z)
     beside = send(own, along_x)
-    below = send(own, up)
-    above = send(own, down)
-    beside_below = send(beside, up)
-    beside_above = send(beside, down)
+    first = send(own, first_move)
+    second = send(own, second_move)
+    beside_first = send(beside, first_move)
+    beside_second = send(beside, second_move)
     (core,) = call(
         relay_kernel,
         [((2 * EXTRA + RELAY_ROWS, obs_rows), bf16)],
@@ -458,8 +463,8 @@
         cross,
         core,
         own,
-        below,
-        above,
+        first,
+        second,
         beside,
     )
     give, keep = call(
@@ -470,8 +475,8 @@
         cross,
         core,
         beside,
-        beside_below,
-        beside_above,
+        beside_first,
+        beside_second,
         shares,
         scratch=[pltpu.VMEM((TEAM + 1, half, members), f32), pltpu.VMEM((TEAM + 1, 8, members), f32)],
     )

time: 78.6 us -> 76.6 us (0.975)
  local copies, waits for them, and re-layouts: 2.56 us -> 0.09 us
  starting transfers between devices: 44.9 us -> 45.7 us
    unnamed x10 -> x4, local copies, waits for them, and re-layouts: 2.48 us -> 0.01 us
  transfers between devices with their start and end apart: 11 -> 11, of which waited for: 5 -> 6; matrix products, arithmetic and copies ran while one was open for 0% -> 0% of each run, Pallas kernels for 2% -> 2%
where the time goes in v5:
time: 76.6 us; the launch traced here: 76.2 us
  starting transfers between devices  45.7 us (60%)
  waiting for transfers between devices  20.1 us (26%)
  Pallas kernels  9.43 us (12%)
  between operations  0.87 us (1%)
    ppermute x11, starting transfers between devices, send(): lax.ppermute(value, ('lat', 'lon'), shifts(lat_count, lon_count, move))  45.7 us
    ppermute x11, waiting for transfers between devices, send(): lax.ppermute(value, ('lat', 'lon'), shifts(lat_count, lon_count, move))  20.1 us
    pallas_call x8, Pallas kernels, call(): pl.pallas_call(kernel, out_shape=tuple(((pltpu.VMEM if pinned else jax.Sh...  9.43 us
  transfers between devices with their start and end apart: 11, of which 6 were waited for; matrix products, arithmetic and copies ran while one was open for 0% of the time, Pallas kernels for 2%

profile of v5, /device:TPU:97, one launch (start us, length us, event | category | flops | bytes accessed | tf_op | source)
XLA Modules:
  0.0 76.2 jit_solution(15115315737598163313)
XLA Ops:
  0.7 1.8 %prepare.1 = (bf16[272,512]{1,0:T(8,128)(2,1)S(1)}, bf16[2,16,512]{2,1,0:T(8,128)(2,1)S(1)}, bf16[2,16,512]{2,1,0:T(8,128)(2,1)S(1)}) custom-call(s32[1,1]{1,0:T(1,128)} %bitcast.place_ref, s32[1,1]{1,0:T(1,128)S(6)} %copy.9.blocks_ref, s32[1,60]{1,0:T(1,128)} %bitcast.6, bf16[512,256]{1,0:T(8,128)(2,1)} %bitcast.4, bf16[1,512]{1,0:T(2,128)(2,1)} %innov_hbm.1, ...), custom_call_target="tpu_custom_call" | custom-call | tf_op jit(solution)/shard_map/prepare/pallas_call | solution.py:387
  2.5 6.8 %collective-permute-start.1 = (bf16[272,512]{1,0:T(8,128)(2,1)S(1)}, bf16[272,512]{1,0:T(8,128)(2,1)S(1)}, u32[]{:S(2)}, u32[]{:S(2)}) collective-permute-start(bf16[272,512]{1,0:T(8,128)(2,1)S(1)} %get-tuple-element.17.own_ref), channel_id=1, source_target_pairs={{0,60},{1,61},{2,6},{3,7},{4,0},{5,1},{6,10},{7,11},{8,4},{9,5},{1... | collective-permute-start | bytes 835592 | tf_op jit(solution)/shard_map/ppermute | solution.py:398
  9.3 9.0 %collective-permute-start = (bf16[2,16,512]{2,1,0:T(8,128)(2,1)S(1)}, bf16[2,16,512]{2,1,0:T(8,128)(2,1)S(1)}, u32[]{:S(2)}, u32[]{:S(2)}) collective-permute-start(bf16[2,16,512]{2,1,0:T(8,128)(2,1)S(1)} %get-tuple-element.15), channel_id=1, source_target_pairs={{0,2},{1,3},{2,0},{3,1},{4,6},{5,7},{6,4},{7,5},{8,10},{9,11},{10,... | collective-permute-start | bytes 98312 | tf_op jit(solution)/shard_map/ppermute | solution.py:398
  18.4 2.6 %collective-permute-start.5 = (bf16[272,512]{1,0:T(8,128)(2,1)S(1)}, bf16[272,512]{1,0:T(8,128)(2,1)S(1)}, u32[]{:S(2)}, u32[]{:S(2)}) collective-permute-start(bf16[272,512]{1,0:T(8,128)(2,1)S(1)} %get-tuple-element.17.own_ref), channel_id=1, source_target_pairs={{0,64},{2,66},{4,68},{6,70},{8,72},{10,74},{12,76},{14,78},{16,80}... | collective-permute-start | bytes 835592 | tf_op jit(solution)/shard_map/ppermute | solution.py:398
  21.0 3.9 %collective-permute-start.6 = (bf16[272,512]{1,0:T(8,128)(2,1)S(1)}, bf16[272,512]{1,0:T(8,128)(2,1)S(1)}, u32[]{:S(2)}, u32[]{:S(2)}) collective-permute-start(bf16[272,512]{1,0:T(8,128)(2,1)S(1)} %get-tuple-element.17.own_ref), channel_id=1, source_target_pairs={{1,65},{3,67},{5,69},{7,71},{9,73},{11,75},{13,77},{15,79},{17,81}... | collective-permute-start | bytes 835592 | tf_op jit(solution)/shard_map/ppermute | solution.py:398
  24.9 1.9 %collective-permute-start.3 = (bf16[272,512]{1,0:T(8,128)(2,1)S(1)}, bf16[272,512]{1,0:T(8,128)(2,1)S(1)}, u32[]{:S(2)}, u32[]{:S(2)}) collective-permute-start(bf16[272,512]{1,0:T(8,128)(2,1)S(1)} %collective-permute-done.1.beside_ref), channel_id=1, source_target_pairs={{0,64},{2,66},{4,68},{6,70},{8,72},{10,74},{12,76},{14,78},{16,80}... | collective-permute-start | bytes 835592 | tf_op jit(solution)/shard_map/ppermute | solution.py:398
  26.8 4.6 %collective-permute-start.4 = (bf16[272,512]{1,0:T(8,128)(2,1)S(1)}, bf16[272,512]{1,0:T(8,128)(2,1)S(1)}, u32[]{:S(2)}, u32[]{:S(2)}) collective-permute-start(bf16[272,512]{1,0:T(8,128)(2,1)S(1)} %collective-permute-done.1.beside_ref), channel_id=1, source_target_pairs={{1,65},{3,67},{5,69},{7,71},{9,73},{11,75},{13,77},{15,79},{17,81}... | collective-permute-start | bytes 835592 | tf_op jit(solution)/shard_map/ppermute | solution.py:398
  31.4 2.1 %collective-permute-start.2 = (bf16[240,512]{1,0:T(8,128)(2,1)S(1)}, bf16[240,512]{1,0:T(8,128)(2,1)S(1)}, u32[]{:S(2)}, u32[]{:S(2)}) collective-permute-start(bf16[240,512]{1,0:T(8,128)(2,1)S(1)} %relay.1), channel_id=1, source_target_pairs={{0,1},{1,0},{2,3},{3,2},{4,5},{5,4},{6,7},{7,6},{8,9},{9,8},{10,11... | collective-permute-start | bytes 737288 | tf_op jit(solution)/shard_map/ppermute | solution.py:398
  33.5 1.3 %collective-permute-done.2.core_ref = bf16[240,512]{1,0:T(8,128)(2,1)S(1)} collective-permute-done((bf16[240,512]{1,0:T(8,128)(2,1)S(1)}, bf16[240,512]{1,0:T(8,128)(2,1)S(1)}, u32[]{:S(2)}, u32[]{:S(2)}) %collective-permute-start.2) | collective-permute-done | bytes 245792 | tf_op jit(solution)/shard_map/ppermute | solution.py:398
  34.8 1.3 %early.1.share_ref = f32[5,272,256]{2,1,0:T(8,128)S(1)} custom-call(s32[1,1]{1,0:T(1,128)} %bitcast.place_ref, bf16[2,16,512]{2,1,0:T(8,128)(2,1)S(1)} %get-tuple-element.16.near_ref, bf16[2,16,512]{2,1,0:T(8,128)(2,1)S(1)} %collective-permute-done.cross_ref, bf16[240,512]{1,0:T(8,128)(2,1)S(1)} %collective-permute-done.2.core_ref, ...), custom_call_target="tpu_custom_call" | custom-call | tf_op jit(solution)/shard_map/early/pallas_call | solution.py:387
  36.2 0.9 %collective-permute-done.4.second_ref = bf16[272,512]{1,0:T(8,128)(2,1)S(1)} collective-permute-done((bf16[272,512]{1,0:T(8,128)(2,1)S(1)}, bf16[272,512]{1,0:T(8,128)(2,1)S(1)}, u32[]{:S(2)}, u32[]{:S(2)}) %collective-permute-start.4) | collective-permute-done | bytes 278560 | tf_op jit(solution)/shard_map/ppermute | solution.py:398
  37.2 0.7 late.1
  37.9 4.0 %collective-permute-start.7 = (bf16[528,256]{1,0:T(8,128)(2,1)S(1)}, bf16[528,256]{1,0:T(8,128)(2,1)S(1)}, u32[]{:S(2)}, u32[]{:S(2)}) collective-permute-start(bf16[528,256]{1,0:T(8,128)(2,1)S(1)} %get-tuple-element.19), channel_id=1, source_target_pairs={{0,1},{1,0},{2,3},{3,2},{4,5},{5,4},{6,7},{7,6},{8,9},{9,8},{10,11... | collective-permute-start | bytes 811016 | tf_op jit(solution)/shard_map/ppermute | solution.py:398
  41.9 1.2 %collective-permute-done.7.give_ref = bf16[528,256]{1,0:T(8,128)(2,1)S(1)} collective-permute-done((bf16[528,256]{1,0:T(8,128)(2,1)S(1)}, bf16[528,256]{1,0:T(8,128)(2,1)S(1)}, u32[]{:S(2)}, u32[]{:S(2)}) %collective-permute-start.7) | collective-permute-done | bytes 270368 | tf_op jit(solution)/shard_map/ppermute | solution.py:398
  43.1 0.1 gather.1
  43.2 7.1 %collective-permute-start.8 = (bf16[272,256]{1,0:T(8,128)(2,1)S(1)}, bf16[272,256]{1,0:T(8,128)(2,1)S(1)}, u32[]{:S(2)}, u32[]{:S(2)}) collective-permute-start(bf16[272,256]{1,0:T(8,128)(2,1)S(1)} %get-tuple-element.21), channel_id=1, source_target_pairs={{0,2},{1,3},{2,0},{3,1},{4,6},{5,7},{6,4},{7,5},{8,10},{9,11},{10,... | collective-permute-start | bytes 417800 | tf_op jit(solution)/shard_map/ppermute | solution.py:398
  50.3 1.3 %collective-permute-start.9 = (bf16[144,256]{1,0:T(8,128)(2,1)S(1)}, bf16[144,256]{1,0:T(8,128)(2,1)S(1)}, u32[]{:S(2)}, u32[]{:S(2)}) collective-permute-start(bf16[144,256]{1,0:T(8,128)(2,1)S(1)} %get-tuple-element.22), channel_id=1, source_target_pairs={{1,4},{2,63},{5,8},{6,3},{9,12},{10,7},{13,16},{14,11},{17,20},{18... | collective-permute-start | bytes 221192 | tf_op jit(solution)/shard_map/ppermute | solution.py:398
  51.6 1.4 %collective-permute-done.9.side_ref = bf16[144,256]{1,0:T(8,128)(2,1)S(1)} collective-permute-done((bf16[144,256]{1,0:T(8,128)(2,1)S(1)}, bf16[144,256]{1,0:T(8,128)(2,1)S(1)}, u32[]{:S(2)}, u32[]{:S(2)}) %collective-permute-start.9) | collective-permute-done | bytes 73760 | tf_op jit(solution)/shard_map/ppermute | solution.py:398
  53.0 14.8 %collective-permute-done.8.cross_ref = bf16[272,256]{1,0:T(8,128)(2,1)S(1)} collective-permute-done((bf16[272,256]{1,0:T(8,128)(2,1)S(1)}, bf16[272,256]{1,0:T(8,128)(2,1)S(1)}, u32[]{:S(2)}, u32[]{:S(2)}) %collective-permute-start.8) | collective-permute-done | bytes 139296 | tf_op jit(solution)/shard_map/ppermute | solution.py:398
  67.7 4.3 %transform.1 = (bf16[256,256]{1,0:T(8,128)(2,1)S(1)}, bf16[256,256]{1,0:T(8,128)(2,1)S(1)}) custom-call(s32[1,1]{1,0:T(1,128)} %bitcast.place_ref, f32[272,256]{1,0:T(8,128)S(1)} %get-tuple-element.20.keep_ref, bf16[272,256]{1,0:T(8,128)(2,1)S(1)} %collective-permute-done.8.cross_ref, bf16[144,256]{1,0:T(8,128)(2,1)S(1)} %collective-permute-done.9.side_ref), custom_call_target="tpu_custom_call" | custom-call | tf_op jit(solution)/shard_map/transform/pallas_call | solution.py:387
  72.0 2.4 %collective-permute-start.10 = (bf16[256,256]{1,0:T(8,128)(2,1)S(1)}, bf16[256,256]{1,0:T(8,128)(2,1)S(1)}, u32[]{:S(2)}, u32[]{:S(2)}) collective-permute-start(bf16[256,256]{1,0:T(8,128)(2,1)S(1)} %get-tuple-element.23.self_ref), channel_id=1, source_target_pairs={{0,1},{1,0},{2,3},{3,2},{4,5},{5,4},{6,7},{7,6},{8,9},{9,8},{10,11... | collective-permute-start | bytes 393224 | tf_op jit(solution)/shard_map/ppermute | solution.py:398
  74.5 0.3 product.1.part_ref
  74.9 0.5 collective-permute-done.10.inner_ref
  75.4 0.8 %blend.1 = bf16[2,4,16,256]{3,2,1,0:T(8,128)(2,1)} custom-call(s32[1,1]{1,0:T(1,128)} %bitcast.place_ref, bf16[256,256]{1,0:T(8,128)(2,1)S(1)} %collective-permute-done.10.inner_ref, f32[2,4,16,256]{3,2,1,0:T(8,128)S(1)} %product.1.part_ref, bf16[2,4,16,256]{3,2,1,0:T(8,128)(2,1)S(1)} %copy-done), custom_call_target="tpu_custom_call" | custom-call | tf_op jit(solution)/shard_map/blend/pallas_call | solution.py:387
  (11 shorter events, 0.1 us)
Async XLA Ops:
  2.5 22.4 %collective-permute-start.1 = (bf16[272,512]{1,0:T(8,128)(2,1)S(1)}, bf16[272,512]{1,0:T(8,128)(2,1)S(1)}, u32[]{:S(2)}, u32[]{:S(2)}) collective-permute-start(bf16[272,512]{1,0:T(8,128)(2,1)S(1)} %get-tuple-element.17.own_ref), channel_id=1, source_target_pairs={{0,60},{1,61},{2,6},{3,7},{4,0},{5,1},{6,10},{7,11},{8,4},{9,5},{1... | collective-permute-start | bytes 835592 | tf_op jit(solution)/shard_map/ppermute | solution.py:398
  9.3 22.1 %collective-permute-start = (bf16[2,16,512]{2,1,0:T(8,128)(2,1)S(1)}, bf16[2,16,512]{2,1,0:T(8,128)(2,1)S(1)}, u32[]{:S(2)}, u32[]{:S(2)}) collective-permute-start(bf16[2,16,512]{2,1,0:T(8,128)(2,1)S(1)} %get-tuple-element.15), channel_id=1, source_target_pairs={{0,2},{1,3},{2,0},{3,1},{4,6},{5,7},{6,4},{7,5},{8,10},{9,11},{10,... | collective-permute-start | bytes 98312 | tf_op jit(solution)/shard_map/ppermute | solution.py:398
  18.4 15.1 %collective-permute-start.5 = (bf16[272,512]{1,0:T(8,128)(2,1)S(1)}, bf16[272,512]{1,0:T(8,128)(2,1)S(1)}, u32[]{:S(2)}, u32[]{:S(2)}) collective-permute-start(bf16[272,512]{1,0:T(8,128)(2,1)S(1)} %get-tuple-element.17.own_ref), channel_id=1, source_target_pairs={{0,64},{2,66},{4,68},{6,70},{8,72},{10,74},{12,76},{14,78},{16,80}... | collective-permute-start | bytes 835592 | tf_op jit(solution)/shard_map/ppermute | solution.py:398
  21.0 12.5 %collective-permute-start.6 = (bf16[272,512]{1,0:T(8,128)(2,1)S(1)}, bf16[272,512]{1,0:T(8,128)(2,1)S(1)}, u32[]{:S(2)}, u32[]{:S(2)}) collective-permute-start(bf16[272,512]{1,0:T(8,128)(2,1)S(1)} %get-tuple-element.17.own_ref), channel_id=1, source_target_pairs={{1,65},{3,67},{5,69},{7,71},{9,73},{11,75},{13,77},{15,79},{17,81}... | collective-permute-start | bytes 835592 | tf_op jit(solution)/shard_map/ppermute | solution.py:398
  24.9 11.3 %collective-permute-start.3 = (bf16[272,512]{1,0:T(8,128)(2,1)S(1)}, bf16[272,512]{1,0:T(8,128)(2,1)S(1)}, u32[]{:S(2)}, u32[]{:S(2)}) collective-permute-start(bf16[272,512]{1,0:T(8,128)(2,1)S(1)} %collective-permute-done.1.beside_ref), channel_id=1, source_target_pairs={{0,64},{2,66},{4,68},{6,70},{8,72},{10,74},{12,76},{14,78},{16,80}... | collective-permute-start | bytes 835592 | tf_op jit(solution)/shard_map/ppermute | solution.py:398
  26.8 10.3 %collective-permute-start.4 = (bf16[272,512]{1,0:T(8,128)(2,1)S(1)}, bf16[272,512]{1,0:T(8,128)(2,1)S(1)}, u32[]{:S(2)}, u32[]{:S(2)}) collective-permute-start(bf16[272,512]{1,0:T(8,128)(2,1)S(1)} %collective-permute-done.1.beside_ref), channel_id=1, source_target_pairs={{1,65},{3,67},{5,69},{7,71},{9,73},{11,75},{13,77},{15,79},{17,81}... | collective-permute-start | bytes 835592 | tf_op jit(solution)/shard_map/ppermute | solution.py:398
  31.4 3.4 %collective-permute-start.2 = (bf16[240,512]{1,0:T(8,128)(2,1)S(1)}, bf16[240,512]{1,0:T(8,128)(2,1)S(1)}, u32[]{:S(2)}, u32[]{:S(2)}) collective-permute-start(bf16[240,512]{1,0:T(8,128)(2,1)S(1)} %relay.1), channel_id=1, source_target_pairs={{0,1},{1,0},{2,3},{3,2},{4,5},{5,4},{6,7},{7,6},{8,9},{9,8},{10,11... | collective-permute-start | bytes 737288 | tf_op jit(solution)/shard_map/ppermute | solution.py:398
  36.2 38.3 %copy-start.1 = (f32[2,4,16]{2,1,0:T(4,128)S(1)}, f32[2,4,16]{2,1,0:T(4,128)}, u32[]{:S(2)}) copy-start(f32[2,4,16]{2,1,0:T(4,128)} %param.9) | copy-start | bytes 1540
  36.2 38.3 %copy-start = (bf16[2,4,16,256]{3,2,1,0:T(8,128)(2,1)S(1)}, bf16[2,4,16,256]{3,2,1,0:T(8,128)(2,1)}, u32[]{:S(2)}) copy-start(bf16[2,4,16,256]{3,2,1,0:T(8,128)(2,1)} %state_ref.3) | copy-start | bytes 196612
  37.9 5.2 %collective-permute-start.7 = (bf16[528,256]{1,0:T(8,128)(2,1)S(1)}, bf16[528,256]{1,0:T(8,128)(2,1)S(1)}, u32[]{:S(2)}, u32[]{:S(2)}) collective-permute-start(bf16[528,256]{1,0:T(8,128)(2,1)S(1)} %get-tuple-element.19), channel_id=1, source_target_pairs={{0,1},{1,0},{2,3},{3,2},{4,5},{5,4},{6,7},{7,6},{8,9},{9,8},{10,11... | collective-permute-start | bytes 811016 | tf_op jit(solution)/shard_map/ppermute | solution.py:398
  43.2 24.6 %collective-permute-start.8 = (bf16[272,256]{1,0:T(8,128)(2,1)S(1)}, bf16[272,256]{1,0:T(8,128)(2,1)S(1)}, u32[]{:S(2)}, u32[]{:S(2)}) collective-permute-start(bf16[272,256]{1,0:T(8,128)(2,1)S(1)} %get-tuple-element.21), channel_id=1, source_target_pairs={{0,2},{1,3},{2,0},{3,1},{4,6},{5,7},{6,4},{7,5},{8,10},{9,11},{10,... | collective-permute-start | bytes 417800 | tf_op jit(solution)/shard_map/ppermute | solution.py:398
  50.3 2.7 %collective-permute-start.9 = (bf16[144,256]{1,0:T(8,128)(2,1)S(1)}, bf16[144,256]{1,0:T(8,128)(2,1)S(1)}, u32[]{:S(2)}, u32[]{:S(2)}) collective-permute-start(bf16[144,256]{1,0:T(8,128)(2,1)S(1)} %get-tuple-element.22), channel_id=1, source_target_pairs={{1,4},{2,63},{5,8},{6,3},{9,12},{10,7},{13,16},{14,11},{17,20},{18... | collective-permute-start | bytes 221192 | tf_op jit(solution)/shard_map/ppermute | solution.py:398
  72.0 3.4 %collective-permute-start.10 = (bf16[256,256]{1,0:T(8,128)(2,1)S(1)}, bf16[256,256]{1,0:T(8,128)(2,1)S(1)}, u32[]{:S(2)}, u32[]{:S(2)}) collective-permute-start(bf16[256,256]{1,0:T(8,128)(2,1)S(1)} %get-tuple-element.23.self_ref), channel_id=1, source_target_pairs={{0,1},{1,0},{2,3},{3,2},{4,5},{5,4},{6,7},{7,6},{8,9},{9,8},{10,11... | collective-permute-start | bytes 393224 | tf_op jit(solution)/shard_map/ppermute | solution.py:398

commit v6 on v5

--- a/solution.py
+++ b/solution.py
@@ -273,7 +273,7 @@
         system = gram + (members - 1.0) * identity
         bound = jnp.max(jnp.sum(jnp.abs(system), axis=0, keepdims=True), axis=1, keepdims=True)
         systems.append(system / bound)
-        projections.append(tail[0:1])
+        projections.append(jnp.broadcast_to(tail[0:1], (8, members)).T[:, 0:1])
         bounds.append(bound)
 
     current = systems
@@ -285,12 +285,13 @@
         factor = [1.5 * identity - 0.5 * dot3(r, split(x)) for r, x in zip(roots, current)]
         parts = [split(x) for x in factor]
         inverse_root = [dot3(f, r) for f, r in zip(parts, roots)]
-        roots = [split(x) for x in inverse_root]
+        if sweep < NSI - 1:
+            roots = [split(x) for x in inverse_root]
     transforms = []
-    for root, parts, projection, bound in zip(inverse_root, roots, projections, bounds):
-        inner = dot3(split(jnp.broadcast_to(projection, (8, members))), parts)
-        centre = dot3(split(inner), parts) / bound
-        transforms.append(root * jnp.sqrt((members - 1.0) / bound) + centre.T[:, 0:1])
+    for root, projection, bound in zip(inverse_root, projections, bounds):
+        inner = jnp.sum(root * projection, axis=0, keepdims=True)
+        centre = jnp.sum(root * inner, axis=1, keepdims=True) / bound
+        transforms.append(root * jnp.sqrt((members - 1.0) / bound) + centre)
     even = place % 2 == 0
     self_out[...] = jnp.where(even, transforms[1], transforms[0]).astype(jnp.bfloat16)
     outer_out[...] = jnp.where(even, transforms[0], transforms[1]).astype(jnp.bfloat16)

time: 76.6 us -> 76.4 us (level)
  no operation moved by 1% of the time
where the time goes in v6:
time: 76.4 us; the launch traced here: 76 us
  starting transfers between devices  45.7 us (60%)
  waiting for transfers between devices  20.1 us (26%)
  Pallas kernels  9.28 us (12%)
  between operations  0.87 us (1%)
    ppermute x11, starting transfers between devices, send(): lax.ppermute(value, ('lat', 'lon'), shifts(lat_count, lon_count, move))  45.7 us
    ppermute x11, waiting for transfers between devices, send(): lax.ppermute(value, ('lat', 'lon'), shifts(lat_count, lon_count, move))  20.1 us
    pallas_call x8, Pallas kernels, call(): pl.pallas_call(kernel, out_shape=tuple(((pltpu.VMEM if pinned else jax.Sh...  9.28 us
  transfers between devices with their start and end apart: 11, of which 6 were waited for; matrix products, arithmetic and copies ran while one was open for 0% of the time, Pallas kernels for 2%

profile of v6, /device:TPU:97, one launch (start us, length us, event | category | flops | bytes accessed | tf_op | source)
XLA Modules:
  0.0 76.0 jit_solution(10616547456987644776)
XLA Ops:
  0.7 1.8 %prepare.1 = (bf16[272,512]{1,0:T(8,128)(2,1)S(1)}, bf16[2,16,512]{2,1,0:T(8,128)(2,1)S(1)}, bf16[2,16,512]{2,1,0:T(8,128)(2,1)S(1)}) custom-call(s32[1,1]{1,0:T(1,128)} %bitcast.place_ref, s32[1,1]{1,0:T(1,128)S(6)} %copy.9.blocks_ref, s32[1,60]{1,0:T(1,128)} %bitcast.6, bf16[512,256]{1,0:T(8,128)(2,1)} %bitcast.4, bf16[1,512]{1,0:T(2,128)(2,1)} %innov_hbm.1, ...), custom_call_target="tpu_custom_call" | custom-call | tf_op jit(solution)/shard_map/prepare/pallas_call | solution.py:388
  2.5 6.8 %collective-permute-start.1 = (bf16[272,512]{1,0:T(8,128)(2,1)S(1)}, bf16[272,512]{1,0:T(8,128)(2,1)S(1)}, u32[]{:S(2)}, u32[]{:S(2)}) collective-permute-start(bf16[272,512]{1,0:T(8,128)(2,1)S(1)} %get-tuple-element.17.own_ref), channel_id=1, source_target_pairs={{0,60},{1,61},{2,6},{3,7},{4,0},{5,1},{6,10},{7,11},{8,4},{9,5},{1... | collective-permute-start | bytes 835592 | tf_op jit(solution)/shard_map/ppermute | solution.py:399
  9.3 9.0 %collective-permute-start = (bf16[2,16,512]{2,1,0:T(8,128)(2,1)S(1)}, bf16[2,16,512]{2,1,0:T(8,128)(2,1)S(1)}, u32[]{:S(2)}, u32[]{:S(2)}) collective-permute-start(bf16[2,16,512]{2,1,0:T(8,128)(2,1)S(1)} %get-tuple-element.15), channel_id=1, source_target_pairs={{0,2},{1,3},{2,0},{3,1},{4,6},{5,7},{6,4},{7,5},{8,10},{9,11},{10,... | collective-permute-start | bytes 98312 | tf_op jit(solution)/shard_map/ppermute | solution.py:399
  18.4 2.6 %collective-permute-start.5 = (bf16[272,512]{1,0:T(8,128)(2,1)S(1)}, bf16[272,512]{1,0:T(8,128)(2,1)S(1)}, u32[]{:S(2)}, u32[]{:S(2)}) collective-permute-start(bf16[272,512]{1,0:T(8,128)(2,1)S(1)} %get-tuple-element.17.own_ref), channel_id=1, source_target_pairs={{0,64},{2,66},{4,68},{6,70},{8,72},{10,74},{12,76},{14,78},{16,80}... | collective-permute-start | bytes 835592 | tf_op jit(solution)/shard_map/ppermute | solution.py:399
  21.0 3.9 %collective-permute-start.6 = (bf16[272,512]{1,0:T(8,128)(2,1)S(1)}, bf16[272,512]{1,0:T(8,128)(2,1)S(1)}, u32[]{:S(2)}, u32[]{:S(2)}) collective-permute-start(bf16[272,512]{1,0:T(8,128)(2,1)S(1)} %get-tuple-element.17.own_ref), channel_id=1, source_target_pairs={{1,65},{3,67},{5,69},{7,71},{9,73},{11,75},{13,77},{15,79},{17,81}... | collective-permute-start | bytes 835592 | tf_op jit(solution)/shard_map/ppermute | solution.py:399
  24.9 1.9 %collective-permute-start.3 = (bf16[272,512]{1,0:T(8,128)(2,1)S(1)}, bf16[272,512]{1,0:T(8,128)(2,1)S(1)}, u32[]{:S(2)}, u32[]{:S(2)}) collective-permute-start(bf16[272,512]{1,0:T(8,128)(2,1)S(1)} %collective-permute-done.1.beside_ref), channel_id=1, source_target_pairs={{0,64},{2,66},{4,68},{6,70},{8,72},{10,74},{12,76},{14,78},{16,80}... | collective-permute-start | bytes 835592 | tf_op jit(solution)/shard_map/ppermute | solution.py:399
  26.8 4.6 %collective-permute-start.4 = (bf16[272,512]{1,0:T(8,128)(2,1)S(1)}, bf16[272,512]{1,0:T(8,128)(2,1)S(1)}, u32[]{:S(2)}, u32[]{:S(2)}) collective-permute-start(bf16[272,512]{1,0:T(8,128)(2,1)S(1)} %collective-permute-done.1.beside_ref), channel_id=1, source_target_pairs={{1,65},{3,67},{5,69},{7,71},{9,73},{11,75},{13,77},{15,79},{17,81}... | collective-permute-start | bytes 835592 | tf_op jit(solution)/shard_map/ppermute | solution.py:399
  31.4 2.1 %collective-permute-start.2 = (bf16[240,512]{1,0:T(8,128)(2,1)S(1)}, bf16[240,512]{1,0:T(8,128)(2,1)S(1)}, u32[]{:S(2)}, u32[]{:S(2)}) collective-permute-start(bf16[240,512]{1,0:T(8,128)(2,1)S(1)} %relay.1), channel_id=1, source_target_pairs={{0,1},{1,0},{2,3},{3,2},{4,5},{5,4},{6,7},{7,6},{8,9},{9,8},{10,11... | collective-permute-start | bytes 737288 | tf_op jit(solution)/shard_map/ppermute | solution.py:399
  33.5 1.3 %collective-permute-done.2.core_ref = bf16[240,512]{1,0:T(8,128)(2,1)S(1)} collective-permute-done((bf16[240,512]{1,0:T(8,128)(2,1)S(1)}, bf16[240,512]{1,0:T(8,128)(2,1)S(1)}, u32[]{:S(2)}, u32[]{:S(2)}) %collective-permute-start.2) | collective-permute-done | bytes 245792 | tf_op jit(solution)/shard_map/ppermute | solution.py:399
  34.8 1.3 %early.1.share_ref = f32[5,272,256]{2,1,0:T(8,128)S(1)} custom-call(s32[1,1]{1,0:T(1,128)} %bitcast.place_ref, bf16[2,16,512]{2,1,0:T(8,128)(2,1)S(1)} %get-tuple-element.16.near_ref, bf16[2,16,512]{2,1,0:T(8,128)(2,1)S(1)} %collective-permute-done.cross_ref, bf16[240,512]{1,0:T(8,128)(2,1)S(1)} %collective-permute-done.2.core_ref, ...), custom_call_target="tpu_custom_call" | custom-call | tf_op jit(solution)/shard_map/early/pallas_call | solution.py:388
  36.2 0.9 %collective-permute-done.4.second_ref = bf16[272,512]{1,0:T(8,128)(2,1)S(1)} collective-permute-done((bf16[272,512]{1,0:T(8,128)(2,1)S(1)}, bf16[272,512]{1,0:T(8,128)(2,1)S(1)}, u32[]{:S(2)}, u32[]{:S(2)}) %collective-permute-start.4) | collective-permute-done | bytes 278560 | tf_op jit(solution)/shard_map/ppermute | solution.py:399
  37.2 0.7 late.1
  37.9 4.0 %collective-permute-start.7 = (bf16[528,256]{1,0:T(8,128)(2,1)S(1)}, bf16[528,256]{1,0:T(8,128)(2,1)S(1)}, u32[]{:S(2)}, u32[]{:S(2)}) collective-permute-start(bf16[528,256]{1,0:T(8,128)(2,1)S(1)} %get-tuple-element.19), channel_id=1, source_target_pairs={{0,1},{1,0},{2,3},{3,2},{4,5},{5,4},{6,7},{7,6},{8,9},{9,8},{10,11... | collective-permute-start | bytes 811016 | tf_op jit(solution)/shard_map/ppermute | solution.py:399
  41.9 1.2 %collective-permute-done.7.give_ref = bf16[528,256]{1,0:T(8,128)(2,1)S(1)} collective-permute-done((bf16[528,256]{1,0:T(8,128)(2,1)S(1)}, bf16[528,256]{1,0:T(8,128)(2,1)S(1)}, u32[]{:S(2)}, u32[]{:S(2)}) %collective-permute-start.7) | collective-permute-done | bytes 270368 | tf_op jit(solution)/shard_map/ppermute | solution.py:399
  43.1 0.1 gather.1
  43.2 7.1 %collective-permute-start.8 = (bf16[272,256]{1,0:T(8,128)(2,1)S(1)}, bf16[272,256]{1,0:T(8,128)(2,1)S(1)}, u32[]{:S(2)}, u32[]{:S(2)}) collective-permute-start(bf16[272,256]{1,0:T(8,128)(2,1)S(1)} %get-tuple-element.21), channel_id=1, source_target_pairs={{0,2},{1,3},{2,0},{3,1},{4,6},{5,7},{6,4},{7,5},{8,10},{9,11},{10,... | collective-permute-start | bytes 417800 | tf_op jit(solution)/shard_map/ppermute | solution.py:399
  50.3 1.3 %collective-permute-start.9 = (bf16[144,256]{1,0:T(8,128)(2,1)S(1)}, bf16[144,256]{1,0:T(8,128)(2,1)S(1)}, u32[]{:S(2)}, u32[]{:S(2)}) collective-permute-start(bf16[144,256]{1,0:T(8,128)(2,1)S(1)} %get-tuple-element.22), channel_id=1, source_target_pairs={{1,4},{2,63},{5,8},{6,3},{9,12},{10,7},{13,16},{14,11},{17,20},{18... | collective-permute-start | bytes 221192 | tf_op jit(solution)/shard_map/ppermute | solution.py:399
  51.6 1.4 %collective-permute-done.9.side_ref = bf16[144,256]{1,0:T(8,128)(2,1)S(1)} collective-permute-done((bf16[144,256]{1,0:T(8,128)(2,1)S(1)}, bf16[144,256]{1,0:T(8,128)(2,1)S(1)}, u32[]{:S(2)}, u32[]{:S(2)}) %collective-permute-start.9) | collective-permute-done | bytes 73760 | tf_op jit(solution)/shard_map/ppermute | solution.py:399
  53.0 14.8 %collective-permute-done.8.cross_ref = bf16[272,256]{1,0:T(8,128)(2,1)S(1)} collective-permute-done((bf16[272,256]{1,0:T(8,128)(2,1)S(1)}, bf16[272,256]{1,0:T(8,128)(2,1)S(1)}, u32[]{:S(2)}, u32[]{:S(2)}) %collective-permute-start.8) | collective-permute-done | bytes 139296 | tf_op jit(solution)/shard_map/ppermute | solution.py:399
  67.7 4.1 %transform.1 = (bf16[256,256]{1,0:T(8,128)(2,1)S(1)}, bf16[256,256]{1,0:T(8,128)(2,1)S(1)}) custom-call(s32[1,1]{1,0:T(1,128)} %bitcast.place_ref, f32[272,256]{1,0:T(8,128)S(1)} %get-tuple-element.20.keep_ref, bf16[272,256]{1,0:T(8,128)(2,1)S(1)} %collective-permute-done.8.cross_ref, bf16[144,256]{1,0:T(8,128)(2,1)S(1)} %collective-permute-done.9.side_ref), custom_call_target="tpu_custom_call" | custom-call | tf_op jit(solution)/shard_map/transform/pallas_call | solution.py:388
  71.9 2.4 %collective-permute-start.10 = (bf16[256,256]{1,0:T(8,128)(2,1)S(1)}, bf16[256,256]{1,0:T(8,128)(2,1)S(1)}, u32[]{:S(2)}, u32[]{:S(2)}) collective-permute-start(bf16[256,256]{1,0:T(8,128)(2,1)S(1)} %get-tuple-element.23.self_ref), channel_id=1, source_target_pairs={{0,1},{1,0},{2,3},{3,2},{4,5},{5,4},{6,7},{7,6},{8,9},{9,8},{10,11... | collective-permute-start | bytes 393224 | tf_op jit(solution)/shard_map/ppermute | solution.py:399
  74.4 0.3 product.1.part_ref
  74.7 0.5 collective-permute-done.10.inner_ref
  75.2 0.8 %blend.1 = bf16[2,4,16,256]{3,2,1,0:T(8,128)(2,1)} custom-call(s32[1,1]{1,0:T(1,128)} %bitcast.place_ref, bf16[256,256]{1,0:T(8,128)(2,1)S(1)} %collective-permute-done.10.inner_ref, f32[2,4,16,256]{3,2,1,0:T(8,128)S(1)} %product.1.part_ref, bf16[2,4,16,256]{3,2,1,0:T(8,128)(2,1)S(1)} %copy-done), custom_call_target="tpu_custom_call" | custom-call | tf_op jit(solution)/shard_map/blend/pallas_call | solution.py:388
  (11 shorter events, 0.1 us)
Async XLA Ops:
  2.5 22.4 %collective-permute-start.1 = (bf16[272,512]{1,0:T(8,128)(2,1)S(1)}, bf16[272,512]{1,0:T(8,128)(2,1)S(1)}, u32[]{:S(2)}, u32[]{:S(2)}) collective-permute-start(bf16[272,512]{1,0:T(8,128)(2,1)S(1)} %get-tuple-element.17.own_ref), channel_id=1, source_target_pairs={{0,60},{1,61},{2,6},{3,7},{4,0},{5,1},{6,10},{7,11},{8,4},{9,5},{1... | collective-permute-start | bytes 835592 | tf_op jit(solution)/shard_map/ppermute | solution.py:399
  9.3 22.1 %collective-permute-start = (bf16[2,16,512]{2,1,0:T(8,128)(2,1)S(1)}, bf16[2,16,512]{2,1,0:T(8,128)(2,1)S(1)}, u32[]{:S(2)}, u32[]{:S(2)}) collective-permute-start(bf16[2,16,512]{2,1,0:T(8,128)(2,1)S(1)} %get-tuple-element.15), channel_id=1, source_target_pairs={{0,2},{1,3},{2,0},{3,1},{4,6},{5,7},{6,4},{7,5},{8,10},{9,11},{10,... | collective-permute-start | bytes 98312 | tf_op jit(solution)/shard_map/ppermute | solution.py:399
  18.4 15.1 %collective-permute-start.5 = (bf16[272,512]{1,0:T(8,128)(2,1)S(1)}, bf16[272,512]{1,0:T(8,128)(2,1)S(1)}, u32[]{:S(2)}, u32[]{:S(2)}) collective-permute-start(bf16[272,512]{1,0:T(8,128)(2,1)S(1)} %get-tuple-element.17.own_ref), channel_id=1, source_target_pairs={{0,64},{2,66},{4,68},{6,70},{8,72},{10,74},{12,76},{14,78},{16,80}... | collective-permute-start | bytes 835592 | tf_op jit(solution)/shard_map/ppermute | solution.py:399
  21.0 12.5 %collective-permute-start.6 = (bf16[272,512]{1,0:T(8,128)(2,1)S(1)}, bf16[272,512]{1,0:T(8,128)(2,1)S(1)}, u32[]{:S(2)}, u32[]{:S(2)}) collective-permute-start(bf16[272,512]{1,0:T(8,128)(2,1)S(1)} %get-tuple-element.17.own_ref), channel_id=1, source_target_pairs={{1,65},{3,67},{5,69},{7,71},{9,73},{11,75},{13,77},{15,79},{17,81}... | collective-permute-start | bytes 835592 | tf_op jit(solution)/shard_map/ppermute | solution.py:399
  24.9 11.3 %collective-permute-start.3 = (bf16[272,512]{1,0:T(8,128)(2,1)S(1)}, bf16[272,512]{1,0:T(8,128)(2,1)S(1)}, u32[]{:S(2)}, u32[]{:S(2)}) collective-permute-start(bf16[272,512]{1,0:T(8,128)(2,1)S(1)} %collective-permute-done.1.beside_ref), channel_id=1, source_target_pairs={{0,64},{2,66},{4,68},{6,70},{8,72},{10,74},{12,76},{14,78},{16,80}... | collective-permute-start | bytes 835592 | tf_op jit(solution)/shard_map/ppermute | solution.py:399
  26.8 10.3 %collective-permute-start.4 = (bf16[272,512]{1,0:T(8,128)(2,1)S(1)}, bf16[272,512]{1,0:T(8,128)(2,1)S(1)}, u32[]{:S(2)}, u32[]{:S(2)}) collective-permute-start(bf16[272,512]{1,0:T(8,128)(2,1)S(1)} %collective-permute-done.1.beside_ref), channel_id=1, source_target_pairs={{1,65},{3,67},{5,69},{7,71},{9,73},{11,75},{13,77},{15,79},{17,81}... | collective-permute-start | bytes 835592 | tf_op jit(solution)/shard_map/ppermute | solution.py:399
  31.4 3.4 %collective-permute-start.2 = (bf16[240,512]{1,0:T(8,128)(2,1)S(1)}, bf16[240,512]{1,0:T(8,128)(2,1)S(1)}, u32[]{:S(2)}, u32[]{:S(2)}) collective-permute-start(bf16[240,512]{1,0:T(8,128)(2,1)S(1)} %relay.1), channel_id=1, source_target_pairs={{0,1},{1,0},{2,3},{3,2},{4,5},{5,4},{6,7},{7,6},{8,9},{9,8},{10,11... | collective-permute-start | bytes 737288 | tf_op jit(solution)/shard_map/ppermute | solution.py:399
  36.2 38.1 %copy-start.1 = (f32[2,4,16]{2,1,0:T(4,128)S(1)}, f32[2,4,16]{2,1,0:T(4,128)}, u32[]{:S(2)}) copy-start(f32[2,4,16]{2,1,0:T(4,128)} %param.9) | copy-start | bytes 1540
  36.2 38.2 %copy-start = (bf16[2,4,16,256]{3,2,1,0:T(8,128)(2,1)S(1)}, bf16[2,4,16,256]{3,2,1,0:T(8,128)(2,1)}, u32[]{:S(2)}) copy-start(bf16[2,4,16,256]{3,2,1,0:T(8,128)(2,1)} %state_ref.3) | copy-start | bytes 196612
  37.9 5.2 %collective-permute-start.7 = (bf16[528,256]{1,0:T(8,128)(2,1)S(1)}, bf16[528,256]{1,0:T(8,128)(2,1)S(1)}, u32[]{:S(2)}, u32[]{:S(2)}) collective-permute-start(bf16[528,256]{1,0:T(8,128)(2,1)S(1)} %get-tuple-element.19), channel_id=1, source_target_pairs={{0,1},{1,0},{2,3},{3,2},{4,5},{5,4},{6,7},{7,6},{8,9},{9,8},{10,11... | collective-permute-start | bytes 811016 | tf_op jit(solution)/shard_map/ppermute | solution.py:399
  43.2 24.6 %collective-permute-start.8 = (bf16[272,256]{1,0:T(8,128)(2,1)S(1)}, bf16[272,256]{1,0:T(8,128)(2,1)S(1)}, u32[]{:S(2)}, u32[]{:S(2)}) collective-permute-start(bf16[272,256]{1,0:T(8,128)(2,1)S(1)} %get-tuple-element.21), channel_id=1, source_target_pairs={{0,2},{1,3},{2,0},{3,1},{4,6},{5,7},{6,4},{7,5},{8,10},{9,11},{10,... | collective-permute-start | bytes 417800 | tf_op jit(solution)/shard_map/ppermute | solution.py:399
  50.3 2.7 %collective-permute-start.9 = (bf16[144,256]{1,0:T(8,128)(2,1)S(1)}, bf16[144,256]{1,0:T(8,128)(2,1)S(1)}, u32[]{:S(2)}, u32[]{:S(2)}) collective-permute-start(bf16[144,256]{1,0:T(8,128)(2,1)S(1)} %get-tuple-element.22), channel_id=1, source_target_pairs={{1,4},{2,63},{5,8},{6,3},{9,12},{10,7},{13,16},{14,11},{17,20},{18... | collective-permute-start | bytes 221192 | tf_op jit(solution)/shard_map/ppermute | solution.py:399
  71.9 3.4 %collective-permute-start.10 = (bf16[256,256]{1,0:T(8,128)(2,1)S(1)}, bf16[256,256]{1,0:T(8,128)(2,1)S(1)}, u32[]{:S(2)}, u32[]{:S(2)}) collective-permute-start(bf16[256,256]{1,0:T(8,128)(2,1)S(1)} %get-tuple-element.23.self_ref), channel_id=1, source_target_pairs={{0,1},{1,0},{2,3},{3,2},{4,5},{5,4},{6,7},{7,6},{8,9},{9,8},{10,11... | collective-permute-start | bytes 393224 | tf_op jit(solution)/shard_map/ppermute | solution.py:399

commit v7 on v6

--- a/solution.py
+++ b/solution.py
@@ -256,7 +256,7 @@
     full_col = lax.broadcasted_iota(jnp.int32, (members, members), 1)
     identity = (full_row == full_col).astype(jnp.float32)
 
-    systems, projections, bounds = [], [], []
+    systems, projections, scales = [], [], []
     for slot in range(2):
         mine = (place < SIDE) if slot == 0 else (place >= SIDE)
         extra = jnp.where(mine, side, 0.0)
@@ -272,9 +272,10 @@
         )
         system = gram + (members - 1.0) * identity
         bound = jnp.max(jnp.sum(jnp.abs(system), axis=0, keepdims=True), axis=1, keepdims=True)
-        systems.append(system / bound)
+        scale = 1.0 / bound
+        systems.append(system * scale)
         projections.append(jnp.broadcast_to(tail[0:1], (8, members)).T[:, 0:1])
-        bounds.append(bound)
+        scales.append(scale)
 
     current = systems
     factor = [1.5 * identity - 0.5 * x for x in current]
@@ -288,10 +289,10 @@
         if sweep < NSI - 1:
             roots = [split(x) for x in inverse_root]
     transforms = []
-    for root, projection, bound in zip(inverse_root, projections, bounds):
+    for root, projection, scale in zip(inverse_root, projections, scales):
         inner = jnp.sum(root * projection, axis=0, keepdims=True)
-        centre = jnp.sum(root * inner, axis=1, keepdims=True) / bound
-        transforms.append(root * jnp.sqrt((members - 1.0) / bound) + centre)
+        centre = jnp.sum(root * inner, axis=1, keepdims=True) * scale
+        transforms.append(root * jnp.sqrt((members - 1.0) * scale) + centre)
     even = place % 2 == 0
     self_out[...] = jnp.where(even, transforms[1], transforms[0]).astype(jnp.bfloat16)
     outer_out[...] = jnp.where(even, transforms[0], transforms[1]).astype(jnp.bfloat16)

time: 76.4 us -> 76.4 us (level)
  no operation moved by 1% of the time
where the time goes in v7:
time: 76.4 us; the launch traced here: 76 us
  starting transfers between devices  45.7 us (60%)
  waiting for transfers between devices  20.1 us (26%)
  Pallas kernels  9.28 us (12%)
  between operations  0.87 us (1%)
    ppermute x11, starting transfers between devices, send(): lax.ppermute(value, ('lat', 'lon'), shifts(lat_count, lon_count, move))  45.7 us
    ppermute x11, waiting for transfers between devices, send(): lax.ppermute(value, ('lat', 'lon'), shifts(lat_count, lon_count, move))  20.1 us
    pallas_call x8, Pallas kernels, call(): pl.pallas_call(kernel, out_shape=tuple(((pltpu.VMEM if pinned else jax.Sh...  9.28 us
  transfers between devices with their start and end apart: 11, of which 6 were waited for; matrix products, arithmetic and copies ran while one was open for 0% of the time, Pallas kernels for 2%

profile of v7, /device:TPU:97, one launch (start us, length us, event | category | flops | bytes accessed | tf_op | source)
XLA Modules:
  0.0 76.0 jit_solution(10616547456987644776)
XLA Ops:
  0.7 1.8 %prepare.1 = (bf16[272,512]{1,0:T(8,128)(2,1)S(1)}, bf16[2,16,512]{2,1,0:T(8,128)(2,1)S(1)}, bf16[2,16,512]{2,1,0:T(8,128)(2,1)S(1)}) custom-call(s32[1,1]{1,0:T(1,128)} %bitcast.place_ref, s32[1,1]{1,0:T(1,128)S(6)} %copy.9.blocks_ref, s32[1,60]{1,0:T(1,128)} %bitcast.6, bf16[512,256]{1,0:T(8,128)(2,1)} %bitcast.4, bf16[1,512]{1,0:T(2,128)(2,1)} %innov_hbm.1, ...), custom_call_target="tpu_custom_call" | custom-call | tf_op jit(solution)/shard_map/prepare/pallas_call | solution.py:389
  2.5 6.8 %collective-permute-start.1 = (bf16[272,512]{1,0:T(8,128)(2,1)S(1)}, bf16[272,512]{1,0:T(8,128)(2,1)S(1)}, u32[]{:S(2)}, u32[]{:S(2)}) collective-permute-start(bf16[272,512]{1,0:T(8,128)(2,1)S(1)} %get-tuple-element.17.own_ref), channel_id=1, source_target_pairs={{0,60},{1,61},{2,6},{3,7},{4,0},{5,1},{6,10},{7,11},{8,4},{9,5},{1... | collective-permute-start | bytes 835592 | tf_op jit(solution)/shard_map/ppermute | solution.py:400
  9.3 9.0 %collective-permute-start = (bf16[2,16,512]{2,1,0:T(8,128)(2,1)S(1)}, bf16[2,16,512]{2,1,0:T(8,128)(2,1)S(1)}, u32[]{:S(2)}, u32[]{:S(2)}) collective-permute-start(bf16[2,16,512]{2,1,0:T(8,128)(2,1)S(1)} %get-tuple-element.15), channel_id=1, source_target_pairs={{0,2},{1,3},{2,0},{3,1},{4,6},{5,7},{6,4},{7,5},{8,10},{9,11},{10,... | collective-permute-start | bytes 98312 | tf_op jit(solution)/shard_map/ppermute | solution.py:400
  18.4 2.6 %collective-permute-start.5 = (bf16[272,512]{1,0:T(8,128)(2,1)S(1)}, bf16[272,512]{1,0:T(8,128)(2,1)S(1)}, u32[]{:S(2)}, u32[]{:S(2)}) collective-permute-start(bf16[272,512]{1,0:T(8,128)(2,1)S(1)} %get-tuple-element.17.own_ref), channel_id=1, source_target_pairs={{0,64},{2,66},{4,68},{6,70},{8,72},{10,74},{12,76},{14,78},{16,80}... | collective-permute-start | bytes 835592 | tf_op jit(solution)/shard_map/ppermute | solution.py:400
  21.0 3.9 %collective-permute-start.6 = (bf16[272,512]{1,0:T(8,128)(2,1)S(1)}, bf16[272,512]{1,0:T(8,128)(2,1)S(1)}, u32[]{:S(2)}, u32[]{:S(2)}) collective-permute-start(bf16[272,512]{1,0:T(8,128)(2,1)S(1)} %get-tuple-element.17.own_ref), channel_id=1, source_target_pairs={{1,65},{3,67},{5,69},{7,71},{9,73},{11,75},{13,77},{15,79},{17,81}... | collective-permute-start | bytes 835592 | tf_op jit(solution)/shard_map/ppermute | solution.py:400
  24.9 1.9 %collective-permute-start.3 = (bf16[272,512]{1,0:T(8,128)(2,1)S(1)}, bf16[272,512]{1,0:T(8,128)(2,1)S(1)}, u32[]{:S(2)}, u32[]{:S(2)}) collective-permute-start(bf16[272,512]{1,0:T(8,128)(2,1)S(1)} %collective-permute-done.1.beside_ref), channel_id=1, source_target_pairs={{0,64},{2,66},{4,68},{6,70},{8,72},{10,74},{12,76},{14,78},{16,80}... | collective-permute-start | bytes 835592 | tf_op jit(solution)/shard_map/ppermute | solution.py:400
  26.8 4.6 %collective-permute-start.4 = (bf16[272,512]{1,0:T(8,128)(2,1)S(1)}, bf16[272,512]{1,0:T(8,128)(2,1)S(1)}, u32[]{:S(2)}, u32[]{:S(2)}) collective-permute-start(bf16[272,512]{1,0:T(8,128)(2,1)S(1)} %collective-permute-done.1.beside_ref), channel_id=1, source_target_pairs={{1,65},{3,67},{5,69},{7,71},{9,73},{11,75},{13,77},{15,79},{17,81}... | collective-permute-start | bytes 835592 | tf_op jit(solution)/shard_map/ppermute | solution.py:400
  31.4 2.1 %collective-permute-start.2 = (bf16[240,512]{1,0:T(8,128)(2,1)S(1)}, bf16[240,512]{1,0:T(8,128)(2,1)S(1)}, u32[]{:S(2)}, u32[]{:S(2)}) collective-permute-start(bf16[240,512]{1,0:T(8,128)(2,1)S(1)} %relay.1), channel_id=1, source_target_pairs={{0,1},{1,0},{2,3},{3,2},{4,5},{5,4},{6,7},{7,6},{8,9},{9,8},{10,11... | collective-permute-start | bytes 737288 | tf_op jit(solution)/shard_map/ppermute | solution.py:400
  33.5 1.3 %collective-permute-done.2.core_ref = bf16[240,512]{1,0:T(8,128)(2,1)S(1)} collective-permute-done((bf16[240,512]{1,0:T(8,128)(2,1)S(1)}, bf16[240,512]{1,0:T(8,128)(2,1)S(1)}, u32[]{:S(2)}, u32[]{:S(2)}) %collective-permute-start.2) | collective-permute-done | bytes 245792 | tf_op jit(solution)/shard_map/ppermute | solution.py:400
  34.8 1.3 %early.1.share_ref = f32[5,272,256]{2,1,0:T(8,128)S(1)} custom-call(s32[1,1]{1,0:T(1,128)} %bitcast.place_ref, bf16[2,16,512]{2,1,0:T(8,128)(2,1)S(1)} %get-tuple-element.16.near_ref, bf16[2,16,512]{2,1,0:T(8,128)(2,1)S(1)} %collective-permute-done.cross_ref, bf16[240,512]{1,0:T(8,128)(2,1)S(1)} %collective-permute-done.2.core_ref, ...), custom_call_target="tpu_custom_call" | custom-call | tf_op jit(solution)/shard_map/early/pallas_call | solution.py:389
  36.2 0.9 %collective-permute-done.4.second_ref = bf16[272,512]{1,0:T(8,128)(2,1)S(1)} collective-permute-done((bf16[272,512]{1,0:T(8,128)(2,1)S(1)}, bf16[272,512]{1,0:T(8,128)(2,1)S(1)}, u32[]{:S(2)}, u32[]{:S(2)}) %collective-permute-start.4) | collective-permute-done | bytes 278560 | tf_op jit(solution)/shard_map/ppermute | solution.py:400
  37.2 0.7 late.1
  37.9 4.0 %collective-permute-start.7 = (bf16[528,256]{1,0:T(8,128)(2,1)S(1)}, bf16[528,256]{1,0:T(8,128)(2,1)S(1)}, u32[]{:S(2)}, u32[]{:S(2)}) collective-permute-start(bf16[528,256]{1,0:T(8,128)(2,1)S(1)} %get-tuple-element.19), channel_id=1, source_target_pairs={{0,1},{1,0},{2,3},{3,2},{4,5},{5,4},{6,7},{7,6},{8,9},{9,8},{10,11... | collective-permute-start | bytes 811016 | tf_op jit(solution)/shard_map/ppermute | solution.py:400
  41.9 1.2 %collective-permute-done.7.give_ref = bf16[528,256]{1,0:T(8,128)(2,1)S(1)} collective-permute-done((bf16[528,256]{1,0:T(8,128)(2,1)S(1)}, bf16[528,256]{1,0:T(8,128)(2,1)S(1)}, u32[]{:S(2)}, u32[]{:S(2)}) %collective-permute-start.7) | collective-permute-done | bytes 270368 | tf_op jit(solution)/shard_map/ppermute | solution.py:400
  43.1 0.1 gather.1
  43.2 7.1 %collective-permute-start.8 = (bf16[272,256]{1,0:T(8,128)(2,1)S(1)}, bf16[272,256]{1,0:T(8,128)(2,1)S(1)}, u32[]{:S(2)}, u32[]{:S(2)}) collective-permute-start(bf16[272,256]{1,0:T(8,128)(2,1)S(1)} %get-tuple-element.21), channel_id=1, source_target_pairs={{0,2},{1,3},{2,0},{3,1},{4,6},{5,7},{6,4},{7,5},{8,10},{9,11},{10,... | collective-permute-start | bytes 417800 | tf_op jit(solution)/shard_map/ppermute | solution.py:400
  50.3 1.3 %collective-permute-start.9 = (bf16[144,256]{1,0:T(8,128)(2,1)S(1)}, bf16[144,256]{1,0:T(8,128)(2,1)S(1)}, u32[]{:S(2)}, u32[]{:S(2)}) collective-permute-start(bf16[144,256]{1,0:T(8,128)(2,1)S(1)} %get-tuple-element.22), channel_id=1, source_target_pairs={{1,4},{2,63},{5,8},{6,3},{9,12},{10,7},{13,16},{14,11},{17,20},{18... | collective-permute-start | bytes 221192 | tf_op jit(solution)/shard_map/ppermute | solution.py:400
  51.6 1.4 %collective-permute-done.9.side_ref = bf16[144,256]{1,0:T(8,128)(2,1)S(1)} collective-permute-done((bf16[144,256]{1,0:T(8,128)(2,1)S(1)}, bf16[144,256]{1,0:T(8,128)(2,1)S(1)}, u32[]{:S(2)}, u32[]{:S(2)}) %collective-permute-start.9) | collective-permute-done | bytes 73760 | tf_op jit(solution)/shard_map/ppermute | solution.py:400
  53.0 14.8 %collective-permute-done.8.cross_ref = bf16[272,256]{1,0:T(8,128)(2,1)S(1)} collective-permute-done((bf16[272,256]{1,0:T(8,128)(2,1)S(1)}, bf16[272,256]{1,0:T(8,128)(2,1)S(1)}, u32[]{:S(2)}, u32[]{:S(2)}) %collective-permute-start.8) | collective-permute-done | bytes 139296 | tf_op jit(solution)/shard_map/ppermute | solution.py:400
  67.7 4.1 %transform.1 = (bf16[256,256]{1,0:T(8,128)(2,1)S(1)}, bf16[256,256]{1,0:T(8,128)(2,1)S(1)}) custom-call(s32[1,1]{1,0:T(1,128)} %bitcast.place_ref, f32[272,256]{1,0:T(8,128)S(1)} %get-tuple-element.20.keep_ref, bf16[272,256]{1,0:T(8,128)(2,1)S(1)} %collective-permute-done.8.cross_ref, bf16[144,256]{1,0:T(8,128)(2,1)S(1)} %collective-permute-done.9.side_ref), custom_call_target="tpu_custom_call" | custom-call | tf_op jit(solution)/shard_map/transform/pallas_call | solution.py:389
  71.9 2.4 %collective-permute-start.10 = (bf16[256,256]{1,0:T(8,128)(2,1)S(1)}, bf16[256,256]{1,0:T(8,128)(2,1)S(1)}, u32[]{:S(2)}, u32[]{:S(2)}) collective-permute-start(bf16[256,256]{1,0:T(8,128)(2,1)S(1)} %get-tuple-element.23.self_ref), channel_id=1, source_target_pairs={{0,1},{1,0},{2,3},{3,2},{4,5},{5,4},{6,7},{7,6},{8,9},{9,8},{10,11... | collective-permute-start | bytes 393224 | tf_op jit(solution)/shard_map/ppermute | solution.py:400
  74.4 0.3 product.1.part_ref
  74.7 0.5 collective-permute-done.10.inner_ref
  75.2 0.8 %blend.1 = bf16[2,4,16,256]{3,2,1,0:T(8,128)(2,1)} custom-call(s32[1,1]{1,0:T(1,128)} %bitcast.place_ref, bf16[256,256]{1,0:T(8,128)(2,1)S(1)} %collective-permute-done.10.inner_ref, f32[2,4,16,256]{3,2,1,0:T(8,128)S(1)} %product.1.part_ref, bf16[2,4,16,256]{3,2,1,0:T(8,128)(2,1)S(1)} %copy-done), custom_call_target="tpu_custom_call" | custom-call | tf_op jit(solution)/shard_map/blend/pallas_call | solution.py:389
  (11 shorter events, 0.1 us)
Async XLA Ops:
  2.5 22.4 %collective-permute-start.1 = (bf16[272,512]{1,0:T(8,128)(2,1)S(1)}, bf16[272,512]{1,0:T(8,128)(2,1)S(1)}, u32[]{:S(2)}, u32[]{:S(2)}) collective-permute-start(bf16[272,512]{1,0:T(8,128)(2,1)S(1)} %get-tuple-element.17.own_ref), channel_id=1, source_target_pairs={{0,60},{1,61},{2,6},{3,7},{4,0},{5,1},{6,10},{7,11},{8,4},{9,5},{1... | collective-permute-start | bytes 835592 | tf_op jit(solution)/shard_map/ppermute | solution.py:400
  9.3 22.1 %collective-permute-start = (bf16[2,16,512]{2,1,0:T(8,128)(2,1)S(1)}, bf16[2,16,512]{2,1,0:T(8,128)(2,1)S(1)}, u32[]{:S(2)}, u32[]{:S(2)}) collective-permute-start(bf16[2,16,512]{2,1,0:T(8,128)(2,1)S(1)} %get-tuple-element.15), channel_id=1, source_target_pairs={{0,2},{1,3},{2,0},{3,1},{4,6},{5,7},{6,4},{7,5},{8,10},{9,11},{10,... | collective-permute-start | bytes 98312 | tf_op jit(solution)/shard_map/ppermute | solution.py:400
  18.4 15.1 %collective-permute-start.5 = (bf16[272,512]{1,0:T(8,128)(2,1)S(1)}, bf16[272,512]{1,0:T(8,128)(2,1)S(1)}, u32[]{:S(2)}, u32[]{:S(2)}) collective-permute-start(bf16[272,512]{1,0:T(8,128)(2,1)S(1)} %get-tuple-element.17.own_ref), channel_id=1, source_target_pairs={{0,64},{2,66},{4,68},{6,70},{8,72},{10,74},{12,76},{14,78},{16,80}... | collective-permute-start | bytes 835592 | tf_op jit(solution)/shard_map/ppermute | solution.py:400
  21.0 12.5 %collective-permute-start.6 = (bf16[272,512]{1,0:T(8,128)(2,1)S(1)}, bf16[272,512]{1,0:T(8,128)(2,1)S(1)}, u32[]{:S(2)}, u32[]{:S(2)}) collective-permute-start(bf16[272,512]{1,0:T(8,128)(2,1)S(1)} %get-tuple-element.17.own_ref), channel_id=1, source_target_pairs={{1,65},{3,67},{5,69},{7,71},{9,73},{11,75},{13,77},{15,79},{17,81}... | collective-permute-start | bytes 835592 | tf_op jit(solution)/shard_map/ppermute | solution.py:400
  24.9 11.3 %collective-permute-start.3 = (bf16[272,512]{1,0:T(8,128)(2,1)S(1)}, bf16[272,512]{1,0:T(8,128)(2,1)S(1)}, u32[]{:S(2)}, u32[]{:S(2)}) collective-permute-start(bf16[272,512]{1,0:T(8,128)(2,1)S(1)} %collective-permute-done.1.beside_ref), channel_id=1, source_target_pairs={{0,64},{2,66},{4,68},{6,70},{8,72},{10,74},{12,76},{14,78},{16,80}... | collective-permute-start | bytes 835592 | tf_op jit(solution)/shard_map/ppermute | solution.py:400
  26.8 10.3 %collective-permute-start.4 = (bf16[272,512]{1,0:T(8,128)(2,1)S(1)}, bf16[272,512]{1,0:T(8,128)(2,1)S(1)}, u32[]{:S(2)}, u32[]{:S(2)}) collective-permute-start(bf16[272,512]{1,0:T(8,128)(2,1)S(1)} %collective-permute-done.1.beside_ref), channel_id=1, source_target_pairs={{1,65},{3,67},{5,69},{7,71},{9,73},{11,75},{13,77},{15,79},{17,81}... | collective-permute-start | bytes 835592 | tf_op jit(solution)/shard_map/ppermute | solution.py:400
  31.4 3.4 %collective-permute-start.2 = (bf16[240,512]{1,0:T(8,128)(2,1)S(1)}, bf16[240,512]{1,0:T(8,128)(2,1)S(1)}, u32[]{:S(2)}, u32[]{:S(2)}) collective-permute-start(bf16[240,512]{1,0:T(8,128)(2,1)S(1)} %relay.1), channel_id=1, source_target_pairs={{0,1},{1,0},{2,3},{3,2},{4,5},{5,4},{6,7},{7,6},{8,9},{9,8},{10,11... | collective-permute-start | bytes 737288 | tf_op jit(solution)/shard_map/ppermute | solution.py:400
  36.2 38.1 %copy-start.1 = (f32[2,4,16]{2,1,0:T(4,128)S(1)}, f32[2,4,16]{2,1,0:T(4,128)}, u32[]{:S(2)}) copy-start(f32[2,4,16]{2,1,0:T(4,128)} %param.9) | copy-start | bytes 1540
  36.2 38.2 %copy-start = (bf16[2,4,16,256]{3,2,1,0:T(8,128)(2,1)S(1)}, bf16[2,4,16,256]{3,2,1,0:T(8,128)(2,1)}, u32[]{:S(2)}) copy-start(bf16[2,4,16,256]{3,2,1,0:T(8,128)(2,1)} %state_ref.3) | copy-start | bytes 196612
  37.9 5.2 %collective-permute-start.7 = (bf16[528,256]{1,0:T(8,128)(2,1)S(1)}, bf16[528,256]{1,0:T(8,128)(2,1)S(1)}, u32[]{:S(2)}, u32[]{:S(2)}) collective-permute-start(bf16[528,256]{1,0:T(8,128)(2,1)S(1)} %get-tuple-element.19), channel_id=1, source_target_pairs={{0,1},{1,0},{2,3},{3,2},{4,5},{5,4},{6,7},{7,6},{8,9},{9,8},{10,11... | collective-permute-start | bytes 811016 | tf_op jit(solution)/shard_map/ppermute | solution.py:400
  43.2 24.6 %collective-permute-start.8 = (bf16[272,256]{1,0:T(8,128)(2,1)S(1)}, bf16[272,256]{1,0:T(8,128)(2,1)S(1)}, u32[]{:S(2)}, u32[]{:S(2)}) collective-permute-start(bf16[272,256]{1,0:T(8,128)(2,1)S(1)} %get-tuple-element.21), channel_id=1, source_target_pairs={{0,2},{1,3},{2,0},{3,1},{4,6},{5,7},{6,4},{7,5},{8,10},{9,11},{10,... | collective-permute-start | bytes 417800 | tf_op jit(solution)/shard_map/ppermute | solution.py:400
  50.3 2.7 %collective-permute-start.9 = (bf16[144,256]{1,0:T(8,128)(2,1)S(1)}, bf16[144,256]{1,0:T(8,128)(2,1)S(1)}, u32[]{:S(2)}, u32[]{:S(2)}) collective-permute-start(bf16[144,256]{1,0:T(8,128)(2,1)S(1)} %get-tuple-element.22), channel_id=1, source_target_pairs={{1,4},{2,63},{5,8},{6,3},{9,12},{10,7},{13,16},{14,11},{17,20},{18... | collective-permute-start | bytes 221192 | tf_op jit(solution)/shard_map/ppermute | solution.py:400
  71.9 3.4 %collective-permute-start.10 = (bf16[256,256]{1,0:T(8,128)(2,1)S(1)}, bf16[256,256]{1,0:T(8,128)(2,1)S(1)}, u32[]{:S(2)}, u32[]{:S(2)}) collective-permute-start(bf16[256,256]{1,0:T(8,128)(2,1)S(1)} %get-tuple-element.23.self_ref), channel_id=1, source_target_pairs={{0,1},{1,0},{2,3},{3,2},{4,5},{5,4},{6,7},{7,6},{8,9},{9,8},{10,11... | collective-permute-start | bytes 393224 | tf_op jit(solution)/shard_map/ppermute | solution.py:400

commit v8 on v6

--- a/solution.py
+++ b/solution.py
@@ -14,7 +14,7 @@
 SIDE = 2
 TEAM = 4
 EXTRA = 16
-RELAY_ROWS = 208
+RELAY_ROWS = 160
 VMEM_LIMIT = 32 * 1024 * 1024
 
 ACROSS = (((1,), (1,)), ((), ()))
@@ -140,8 +140,19 @@
 
 
 def early_kernel(
-    place_ref, near_ref, cross_ref, core_ref, own_ref, first_ref, second_ref, beside_ref, out_ref
+    place_ref,
+    near_ref,
+    cross_ref,
+    core_ref,
+    own_ref,
+    first_low_ref,
+    first_high_ref,
+    second_ref,
+    beside_ref,
+    out_ref,
+    first_ref,
 ):
+    first_ref[...] = first_low_ref[...] + first_high_ref[...]
     for index, pack in enumerate((near_ref[0], core_ref[pl.ds(0, EXTRA), :], cross_ref[0], core_ref[pl.ds(EXTRA, EXTRA), :])):
         weight = joined(pack)
         first, second = outer_lats(place_ref, weight)
@@ -441,7 +452,8 @@
     )
     cross = send(far, across_z)
     beside = send(own, along_x)
-    first = send(own, first_move)
+    first_low = send(own, lambda lat, lon: first_move(lat, lon) if lon % TEAM < SIDE else None)
+    first_high = send(own, lambda lat, lon: first_move(lat, lon) if lon % TEAM >= SIDE else None)
     second = send(own, second_move)
     beside_first = send(beside, first_move)
     beside_second = send(beside, second_move)
@@ -458,15 +470,17 @@
     (shares,) = call(
         early_kernel,
         [((TEAM + 1, members + EXTRA, members), f32)],
-        [SMEM] + [VMEM] * 7,
+        [SMEM] + [VMEM] * 8,
         place,
         near,
         cross,
         core,
         own,
-        first,
+        first_low,
+        first_high,
         second,
         beside,
+        scratch=[pltpu.VMEM((members + EXTRA, obs_rows), bf16)],
     )
     give, keep = call(
         late_kernel,

time: 76.4 us -> 77 us (level)
  starting transfers between devices: 45.7 us -> 53.2 us
  waiting for transfers between devices: 20.1 us -> 13.1 us
    ppermute x11 -> x12, starting transfers between devices: 45.7 us -> 53.2 us  [send(): lax.ppermute(value, ('lat', 'lon'), shifts(lat_count, lon_count, move))]
    ppermute x11 -> x12, waiting for transfers between devices: 20.1 us -> 13.1 us  [send(): lax.ppermute(value, ('lat', 'lon'), shifts(lat_count, lon_count, move))]
  transfers between devices with their start and end apart: 11 -> 12, of which waited for: 6 -> 5; matrix products, arithmetic and copies ran while one was open for 0% -> 0% of each run, Pallas kernels for 2% -> 2%
where the time goes in v8:
time: 77 us; the launch traced here: 76.6 us
  starting transfers between devices  53.2 us (69%)
  waiting for transfers between devices  13.1 us (17%)
  Pallas kernels  9.22 us (12%)
  between operations  0.9 us (1%)
    ppermute x12, starting transfers between devices, send(): lax.ppermute(value, ('lat', 'lon'), shifts(lat_count, lon_count, move))  53.2 us
    ppermute x12, waiting for transfers between devices, send(): lax.ppermute(value, ('lat', 'lon'), shifts(lat_count, lon_count, move))  13.1 us
    pallas_call x8, Pallas kernels, call(): pl.pallas_call(kernel, out_shape=tuple(((pltpu.VMEM if pinned else jax.Sh...  9.22 us
  transfers between devices with their start and end apart: 12, of which 5 were waited for; matrix products, arithmetic and copies ran while one was open for 0% of the time, Pallas kernels for 2%

profile of v8, /device:TPU:97, one launch (start us, length us, event | category | flops | bytes accessed | tf_op | source)
XLA Modules:
  0.0 76.6 jit_solution(9937938574579747855)
XLA Ops:
  0.7 1.8 %prepare.1 = (bf16[272,512]{1,0:T(8,128)(2,1)S(1)}, bf16[2,16,512]{2,1,0:T(8,128)(2,1)S(1)}, bf16[2,16,512]{2,1,0:T(8,128)(2,1)S(1)}) custom-call(s32[1,1]{1,0:T(1,128)} %bitcast.place_ref, s32[1,1]{1,0:T(1,128)S(6)} %copy.9.blocks_ref, s32[1,60]{1,0:T(1,128)} %bitcast.6, bf16[512,256]{1,0:T(8,128)(2,1)} %bitcast.4, bf16[1,512]{1,0:T(2,128)(2,1)} %innov_hbm.1, ...), custom_call_target="tpu_custom_call" | custom-call | tf_op jit(solution)/shard_map/prepare/pallas_call | solution.py:399
  2.5 6.8 %collective-permute-start.1 = (bf16[272,512]{1,0:T(8,128)(2,1)S(1)}, bf16[272,512]{1,0:T(8,128)(2,1)S(1)}, u32[]{:S(2)}, u32[]{:S(2)}) collective-permute-start(bf16[272,512]{1,0:T(8,128)(2,1)S(1)} %get-tuple-element.17.own_ref), channel_id=1, source_target_pairs={{0,60},{1,61},{2,6},{3,7},{4,0},{5,1},{6,10},{7,11},{8,4},{9,5},{1... | collective-permute-start | bytes 835592 | tf_op jit(solution)/shard_map/ppermute | solution.py:410
  9.3 1.9 %collective-permute-start.5 = (bf16[272,512]{1,0:T(8,128)(2,1)S(1)}, bf16[272,512]{1,0:T(8,128)(2,1)S(1)}, u32[]{:S(2)}, u32[]{:S(2)}) collective-permute-start(bf16[272,512]{1,0:T(8,128)(2,1)S(1)} %get-tuple-element.17.own_ref), channel_id=1, source_target_pairs={{0,64},{4,68},{8,72},{12,76},{16,80},{20,84},{24,88},{28,92},{32,9... | collective-permute-start | bytes 835592 | tf_op jit(solution)/shard_map/ppermute | solution.py:410
  11.3 7.8 %collective-permute-start = (bf16[2,16,512]{2,1,0:T(8,128)(2,1)S(1)}, bf16[2,16,512]{2,1,0:T(8,128)(2,1)S(1)}, u32[]{:S(2)}, u32[]{:S(2)}) collective-permute-start(bf16[2,16,512]{2,1,0:T(8,128)(2,1)S(1)} %get-tuple-element.15), channel_id=1, source_target_pairs={{0,2},{1,3},{2,0},{3,1},{4,6},{5,7},{6,4},{7,5},{8,10},{9,11},{10,... | collective-permute-start | bytes 98312 | tf_op jit(solution)/shard_map/ppermute | solution.py:410
  19.1 0.7 collective-permute-start.6
  19.7 2.6 %collective-permute-start.7 = (bf16[272,512]{1,0:T(8,128)(2,1)S(1)}, bf16[272,512]{1,0:T(8,128)(2,1)S(1)}, u32[]{:S(2)}, u32[]{:S(2)}) collective-permute-start(bf16[272,512]{1,0:T(8,128)(2,1)S(1)} %get-tuple-element.17.own_ref), channel_id=1, source_target_pairs={{1,65},{3,67},{5,69},{7,71},{9,73},{11,75},{13,77},{15,79},{17,81}... | collective-permute-start | bytes 835592 | tf_op jit(solution)/shard_map/ppermute | solution.py:410
  22.4 2.6 %collective-permute-start.3 = (bf16[272,512]{1,0:T(8,128)(2,1)S(1)}, bf16[272,512]{1,0:T(8,128)(2,1)S(1)}, u32[]{:S(2)}, u32[]{:S(2)}) collective-permute-start(bf16[272,512]{1,0:T(8,128)(2,1)S(1)} %collective-permute-done.1.beside_ref), channel_id=1, source_target_pairs={{0,64},{2,66},{4,68},{6,70},{8,72},{10,74},{12,76},{14,78},{16,80}... | collective-permute-start | bytes 835592 | tf_op jit(solution)/shard_map/ppermute | solution.py:410
  25.1 4.5 %collective-permute-start.4 = (bf16[272,512]{1,0:T(8,128)(2,1)S(1)}, bf16[272,512]{1,0:T(8,128)(2,1)S(1)}, u32[]{:S(2)}, u32[]{:S(2)}) collective-permute-start(bf16[272,512]{1,0:T(8,128)(2,1)S(1)} %collective-permute-done.1.beside_ref), channel_id=1, source_target_pairs={{1,65},{3,67},{5,69},{7,71},{9,73},{11,75},{13,77},{15,79},{17,81}... | collective-permute-start | bytes 835592 | tf_op jit(solution)/shard_map/ppermute | solution.py:410
  29.6 4.9 %collective-permute-start.2 = (bf16[192,512]{1,0:T(8,128)(2,1)S(1)}, bf16[192,512]{1,0:T(8,128)(2,1)S(1)}, u32[]{:S(2)}, u32[]{:S(2)}) collective-permute-start(bf16[192,512]{1,0:T(8,128)(2,1)S(1)} %relay.1), channel_id=1, source_target_pairs={{0,1},{1,0},{2,3},{3,2},{4,5},{5,4},{6,7},{7,6},{8,9},{9,8},{10,11... | collective-permute-start | bytes 589832 | tf_op jit(solution)/shard_map/ppermute | solution.py:410
  34.5 1.0 %collective-permute-done.2.core_ref = bf16[192,512]{1,0:T(8,128)(2,1)S(1)} collective-permute-done((bf16[192,512]{1,0:T(8,128)(2,1)S(1)}, bf16[192,512]{1,0:T(8,128)(2,1)S(1)}, u32[]{:S(2)}, u32[]{:S(2)}) %collective-permute-start.2) | collective-permute-done | bytes 196640 | tf_op jit(solution)/shard_map/ppermute | solution.py:410
  35.5 1.3 %early.1.share_ref = f32[5,272,256]{2,1,0:T(8,128)S(1)} custom-call(s32[1,1]{1,0:T(1,128)} %bitcast.place_ref, bf16[2,16,512]{2,1,0:T(8,128)(2,1)S(1)} %get-tuple-element.16.near_ref, bf16[2,16,512]{2,1,0:T(8,128)(2,1)S(1)} %collective-permute-done.cross_ref, bf16[192,512]{1,0:T(8,128)(2,1)S(1)} %collective-permute-done.2.core_ref, ...), custom_call_target="tpu_custom_call" | custom-call | tf_op jit(solution)/shard_map/early/pallas_call | solution.py:399
  36.9 0.7 late.1
  37.6 5.3 %collective-permute-start.8 = (bf16[528,256]{1,0:T(8,128)(2,1)S(1)}, bf16[528,256]{1,0:T(8,128)(2,1)S(1)}, u32[]{:S(2)}, u32[]{:S(2)}) collective-permute-start(bf16[528,256]{1,0:T(8,128)(2,1)S(1)} %get-tuple-element.19), channel_id=1, source_target_pairs={{0,1},{1,0},{2,3},{3,2},{4,5},{5,4},{6,7},{7,6},{8,9},{9,8},{10,11... | collective-permute-start | bytes 811016 | tf_op jit(solution)/shard_map/ppermute | solution.py:410
  42.9 1.2 %collective-permute-done.8.give_ref = bf16[528,256]{1,0:T(8,128)(2,1)S(1)} collective-permute-done((bf16[528,256]{1,0:T(8,128)(2,1)S(1)}, bf16[528,256]{1,0:T(8,128)(2,1)S(1)}, u32[]{:S(2)}, u32[]{:S(2)}) %collective-permute-start.8) | collective-permute-done | bytes 270368 | tf_op jit(solution)/shard_map/ppermute | solution.py:410
  44.1 0.1 gather.1
  44.2 9.9 %collective-permute-start.9 = (bf16[272,256]{1,0:T(8,128)(2,1)S(1)}, bf16[272,256]{1,0:T(8,128)(2,1)S(1)}, u32[]{:S(2)}, u32[]{:S(2)}) collective-permute-start(bf16[272,256]{1,0:T(8,128)(2,1)S(1)} %get-tuple-element.21), channel_id=1, source_target_pairs={{0,2},{1,3},{2,0},{3,1},{4,6},{5,7},{6,4},{7,5},{8,10},{9,11},{10,... | collective-permute-start | bytes 417800 | tf_op jit(solution)/shard_map/ppermute | solution.py:410
  54.1 1.3 %collective-permute-start.10 = (bf16[144,256]{1,0:T(8,128)(2,1)S(1)}, bf16[144,256]{1,0:T(8,128)(2,1)S(1)}, u32[]{:S(2)}, u32[]{:S(2)}) collective-permute-start(bf16[144,256]{1,0:T(8,128)(2,1)S(1)} %get-tuple-element.22), channel_id=1, source_target_pairs={{1,4},{2,63},{5,8},{6,3},{9,12},{10,7},{13,16},{14,11},{17,20},{18... | collective-permute-start | bytes 221192 | tf_op jit(solution)/shard_map/ppermute | solution.py:410
  55.4 1.4 %collective-permute-done.10.side_ref = bf16[144,256]{1,0:T(8,128)(2,1)S(1)} collective-permute-done((bf16[144,256]{1,0:T(8,128)(2,1)S(1)}, bf16[144,256]{1,0:T(8,128)(2,1)S(1)}, u32[]{:S(2)}, u32[]{:S(2)}) %collective-permute-start.10) | collective-permute-done | bytes 73760 | tf_op jit(solution)/shard_map/ppermute | solution.py:410
  56.8 9.0 %collective-permute-done.9.cross_ref = bf16[272,256]{1,0:T(8,128)(2,1)S(1)} collective-permute-done((bf16[272,256]{1,0:T(8,128)(2,1)S(1)}, bf16[272,256]{1,0:T(8,128)(2,1)S(1)}, u32[]{:S(2)}, u32[]{:S(2)}) %collective-permute-start.9) | collective-permute-done | bytes 139296 | tf_op jit(solution)/shard_map/ppermute | solution.py:410
  65.8 4.1 %transform.1 = (bf16[256,256]{1,0:T(8,128)(2,1)S(1)}, bf16[256,256]{1,0:T(8,128)(2,1)S(1)}) custom-call(s32[1,1]{1,0:T(1,128)} %bitcast.place_ref, f32[272,256]{1,0:T(8,128)S(1)} %get-tuple-element.20.keep_ref, bf16[272,256]{1,0:T(8,128)(2,1)S(1)} %collective-permute-done.9.cross_ref, bf16[144,256]{1,0:T(8,128)(2,1)S(1)} %collective-permute-done.10.side_ref), custom_call_target="tpu_custom_call" | custom-call | tf_op jit(solution)/shard_map/transform/pallas_call | solution.py:399
  70.0 4.8 %collective-permute-start.11 = (bf16[256,256]{1,0:T(8,128)(2,1)S(1)}, bf16[256,256]{1,0:T(8,128)(2,1)S(1)}, u32[]{:S(2)}, u32[]{:S(2)}) collective-permute-start(bf16[256,256]{1,0:T(8,128)(2,1)S(1)} %get-tuple-element.23.self_ref), channel_id=1, source_target_pairs={{0,1},{1,0},{2,3},{3,2},{4,5},{5,4},{6,7},{7,6},{8,9},{9,8},{10,11... | collective-permute-start | bytes 393224 | tf_op jit(solution)/shard_map/ppermute | solution.py:410
  74.9 0.3 product.1.part_ref
  75.2 0.5 collective-permute-done.11.inner_ref
  75.8 0.8 %blend.1 = bf16[2,4,16,256]{3,2,1,0:T(8,128)(2,1)} custom-call(s32[1,1]{1,0:T(1,128)} %bitcast.place_ref, bf16[256,256]{1,0:T(8,128)(2,1)S(1)} %collective-permute-done.11.inner_ref, f32[2,4,16,256]{3,2,1,0:T(8,128)S(1)} %product.1.part_ref, bf16[2,4,16,256]{3,2,1,0:T(8,128)(2,1)S(1)} %copy-done), custom_call_target="tpu_custom_call" | custom-call | tf_op jit(solution)/shard_map/blend/pallas_call | solution.py:399
  (13 shorter events, 0.1 us)
Async XLA Ops:
  2.5 19.9 %collective-permute-start.1 = (bf16[272,512]{1,0:T(8,128)(2,1)S(1)}, bf16[272,512]{1,0:T(8,128)(2,1)S(1)}, u32[]{:S(2)}, u32[]{:S(2)}) collective-permute-start(bf16[272,512]{1,0:T(8,128)(2,1)S(1)} %get-tuple-element.17.own_ref), channel_id=1, source_target_pairs={{0,60},{1,61},{2,6},{3,7},{4,0},{5,1},{6,10},{7,11},{8,4},{9,5},{1... | collective-permute-start | bytes 835592 | tf_op jit(solution)/shard_map/ppermute | solution.py:410
  9.3 20.2 %collective-permute-start.5 = (bf16[272,512]{1,0:T(8,128)(2,1)S(1)}, bf16[272,512]{1,0:T(8,128)(2,1)S(1)}, u32[]{:S(2)}, u32[]{:S(2)}) collective-permute-start(bf16[272,512]{1,0:T(8,128)(2,1)S(1)} %get-tuple-element.17.own_ref), channel_id=1, source_target_pairs={{0,64},{4,68},{8,72},{12,76},{16,80},{20,84},{24,88},{28,92},{32,9... | collective-permute-start | bytes 835592 | tf_op jit(solution)/shard_map/ppermute | solution.py:410
  11.3 13.8 %collective-permute-start = (bf16[2,16,512]{2,1,0:T(8,128)(2,1)S(1)}, bf16[2,16,512]{2,1,0:T(8,128)(2,1)S(1)}, u32[]{:S(2)}, u32[]{:S(2)}) collective-permute-start(bf16[2,16,512]{2,1,0:T(8,128)(2,1)S(1)} %get-tuple-element.15), channel_id=1, source_target_pairs={{0,2},{1,3},{2,0},{3,1},{4,6},{5,7},{6,4},{7,5},{8,10},{9,11},{10,... | collective-permute-start | bytes 98312 | tf_op jit(solution)/shard_map/ppermute | solution.py:410
  19.1 15.4 %collective-permute-start.6 = (bf16[272,512]{1,0:T(8,128)(2,1)S(1)}, bf16[272,512]{1,0:T(8,128)(2,1)S(1)}, u32[]{:S(2)}, u32[]{:S(2)}) collective-permute-start(bf16[272,512]{1,0:T(8,128)(2,1)S(1)} %get-tuple-element.17.own_ref), channel_id=1, source_target_pairs={{2,66},{6,70},{10,74},{14,78},{18,82},{22,86},{26,90},{30,94},{34,... | collective-permute-start | bytes 835592 | tf_op jit(solution)/shard_map/ppermute | solution.py:410
  19.7 14.8 %collective-permute-start.7 = (bf16[272,512]{1,0:T(8,128)(2,1)S(1)}, bf16[272,512]{1,0:T(8,128)(2,1)S(1)}, u32[]{:S(2)}, u32[]{:S(2)}) collective-permute-start(bf16[272,512]{1,0:T(8,128)(2,1)S(1)} %get-tuple-element.17.own_ref), channel_id=1, source_target_pairs={{1,65},{3,67},{5,69},{7,71},{9,73},{11,75},{13,77},{15,79},{17,81}... | collective-permute-start | bytes 835592 | tf_op jit(solution)/shard_map/ppermute | solution.py:410
  22.4 14.5 %collective-permute-start.3 = (bf16[272,512]{1,0:T(8,128)(2,1)S(1)}, bf16[272,512]{1,0:T(8,128)(2,1)S(1)}, u32[]{:S(2)}, u32[]{:S(2)}) collective-permute-start(bf16[272,512]{1,0:T(8,128)(2,1)S(1)} %collective-permute-done.1.beside_ref), channel_id=1, source_target_pairs={{0,64},{2,66},{4,68},{6,70},{8,72},{10,74},{12,76},{14,78},{16,80}... | collective-permute-start | bytes 835592 | tf_op jit(solution)/shard_map/ppermute | solution.py:410
  25.1 11.8 %collective-permute-start.4 = (bf16[272,512]{1,0:T(8,128)(2,1)S(1)}, bf16[272,512]{1,0:T(8,128)(2,1)S(1)}, u32[]{:S(2)}, u32[]{:S(2)}) collective-permute-start(bf16[272,512]{1,0:T(8,128)(2,1)S(1)} %collective-permute-done.1.beside_ref), channel_id=1, source_target_pairs={{1,65},{3,67},{5,69},{7,71},{9,73},{11,75},{13,77},{15,79},{17,81}... | collective-permute-start | bytes 835592 | tf_op jit(solution)/shard_map/ppermute | solution.py:410
  29.6 6.0 %collective-permute-start.2 = (bf16[192,512]{1,0:T(8,128)(2,1)S(1)}, bf16[192,512]{1,0:T(8,128)(2,1)S(1)}, u32[]{:S(2)}, u32[]{:S(2)}) collective-permute-start(bf16[192,512]{1,0:T(8,128)(2,1)S(1)} %relay.1), channel_id=1, source_target_pairs={{0,1},{1,0},{2,3},{3,2},{4,5},{5,4},{6,7},{7,6},{8,9},{9,8},{10,11... | collective-permute-start | bytes 589832 | tf_op jit(solution)/shard_map/ppermute | solution.py:410
  36.8 38.0 %copy-start.1 = (f32[2,4,16]{2,1,0:T(4,128)S(1)}, f32[2,4,16]{2,1,0:T(4,128)}, u32[]{:S(2)}) copy-start(f32[2,4,16]{2,1,0:T(4,128)} %param.9) | copy-start | bytes 1540
  36.9 38.1 %copy-start = (bf16[2,4,16,256]{3,2,1,0:T(8,128)(2,1)S(1)}, bf16[2,4,16,256]{3,2,1,0:T(8,128)(2,1)}, u32[]{:S(2)}) copy-start(bf16[2,4,16,256]{3,2,1,0:T(8,128)(2,1)} %state_ref.3) | copy-start | bytes 196612
  37.6 6.4 %collective-permute-start.8 = (bf16[528,256]{1,0:T(8,128)(2,1)S(1)}, bf16[528,256]{1,0:T(8,128)(2,1)S(1)}, u32[]{:S(2)}, u32[]{:S(2)}) collective-permute-start(bf16[528,256]{1,0:T(8,128)(2,1)S(1)} %get-tuple-element.19), channel_id=1, source_target_pairs={{0,1},{1,0},{2,3},{3,2},{4,5},{5,4},{6,7},{7,6},{8,9},{9,8},{10,11... | collective-permute-start | bytes 811016 | tf_op jit(solution)/shard_map/ppermute | solution.py:410
  44.2 21.6 %collective-permute-start.9 = (bf16[272,256]{1,0:T(8,128)(2,1)S(1)}, bf16[272,256]{1,0:T(8,128)(2,1)S(1)}, u32[]{:S(2)}, u32[]{:S(2)}) collective-permute-start(bf16[272,256]{1,0:T(8,128)(2,1)S(1)} %get-tuple-element.21), channel_id=1, source_target_pairs={{0,2},{1,3},{2,0},{3,1},{4,6},{5,7},{6,4},{7,5},{8,10},{9,11},{10,... | collective-permute-start | bytes 417800 | tf_op jit(solution)/shard_map/ppermute | solution.py:410
  54.1 2.7 %collective-permute-start.10 = (bf16[144,256]{1,0:T(8,128)(2,1)S(1)}, bf16[144,256]{1,0:T(8,128)(2,1)S(1)}, u32[]{:S(2)}, u32[]{:S(2)}) collective-permute-start(bf16[144,256]{1,0:T(8,128)(2,1)S(1)} %get-tuple-element.22), channel_id=1, source_target_pairs={{1,4},{2,63},{5,8},{6,3},{9,12},{10,7},{13,16},{14,11},{17,20},{18... | collective-permute-start | bytes 221192 | tf_op jit(solution)/shard_map/ppermute | solution.py:410
  70.0 5.8 %collective-permute-start.11 = (bf16[256,256]{1,0:T(8,128)(2,1)S(1)}, bf16[256,256]{1,0:T(8,128)(2,1)S(1)}, u32[]{:S(2)}, u32[]{:S(2)}) collective-permute-start(bf16[256,256]{1,0:T(8,128)(2,1)S(1)} %get-tuple-element.23.self_ref), channel_id=1, source_target_pairs={{0,1},{1,0},{2,3},{3,2},{4,5},{5,4},{6,7},{7,6},{8,9},{9,8},{10,11... | collective-permute-start | bytes 393224 | tf_op jit(solution)/shard_map/ppermute | solution.py:410

commit v9 on v6

--- a/solution.py
+++ b/solution.py
@@ -60,7 +60,8 @@
         ((local_hbm, local_ref), (innov_hbm, innov_ref), (prec_hbm, prec_ref), (anom_hbm, anom_ref))
     ):
         copies.append(pltpu.make_async_copy(source, target, sems.at[index]))
-        copies[-1].start()
+    for index in (3, 0, 1, 2):
+        copies[index].start()
     rows, members = anom_ref.shape
     place = place_ref[0, 0]
     blocks = rows // BLOCK_ROWS

time: 76.4 us -> 76.5 us (level)
  no operation moved by 1% of the time
where the time goes in v9:
time: 76.5 us; the launch traced here: 76.1 us
  starting transfers between devices  45.7 us (60%)
  waiting for transfers between devices  20.1 us (26%)
  Pallas kernels  9.35 us (12%)
  between operations  0.87 us (1%)
    ppermute x11, starting transfers between devices, send(): lax.ppermute(value, ('lat', 'lon'), shifts(lat_count, lon_count, move))  45.7 us
    ppermute x11, waiting for transfers between devices, send(): lax.ppermute(value, ('lat', 'lon'), shifts(lat_count, lon_count, move))  20.1 us
    pallas_call x8, Pallas kernels, call(): pl.pallas_call(kernel, out_shape=tuple(((pltpu.VMEM if pinned else jax.Sh...  9.35 us
  transfers between devices with their start and end apart: 11, of which 6 were waited for; matrix products, arithmetic and copies ran while one was open for 0% of the time, Pallas kernels for 2%

profile of v9, /device:TPU:97, one launch (start us, length us, event | category | flops | bytes accessed | tf_op | source)
XLA Modules:
  0.0 76.1 jit_solution(16569384243993357028)
XLA Ops:
  0.7 1.9 %prepare.1 = (bf16[272,512]{1,0:T(8,128)(2,1)S(1)}, bf16[2,16,512]{2,1,0:T(8,128)(2,1)S(1)}, bf16[2,16,512]{2,1,0:T(8,128)(2,1)S(1)}) custom-call(s32[1,1]{1,0:T(1,128)} %bitcast.place_ref, s32[1,1]{1,0:T(1,128)S(6)} %copy.9.blocks_ref, s32[1,60]{1,0:T(1,128)} %bitcast.6, bf16[512,256]{1,0:T(8,128)(2,1)} %bitcast.4, bf16[1,512]{1,0:T(2,128)(2,1)} %innov_hbm.1, ...), custom_call_target="tpu_custom_call" | custom-call | tf_op jit(solution)/shard_map/prepare/pallas_call | solution.py:389
  2.6 6.8 %collective-permute-start.1 = (bf16[272,512]{1,0:T(8,128)(2,1)S(1)}, bf16[272,512]{1,0:T(8,128)(2,1)S(1)}, u32[]{:S(2)}, u32[]{:S(2)}) collective-permute-start(bf16[272,512]{1,0:T(8,128)(2,1)S(1)} %get-tuple-element.17.own_ref), channel_id=1, source_target_pairs={{0,60},{1,61},{2,6},{3,7},{4,0},{5,1},{6,10},{7,11},{8,4},{9,5},{1... | collective-permute-start | bytes 835592 | tf_op jit(solution)/shard_map/ppermute | solution.py:400
  9.4 9.0 %collective-permute-start = (bf16[2,16,512]{2,1,0:T(8,128)(2,1)S(1)}, bf16[2,16,512]{2,1,0:T(8,128)(2,1)S(1)}, u32[]{:S(2)}, u32[]{:S(2)}) collective-permute-start(bf16[2,16,512]{2,1,0:T(8,128)(2,1)S(1)} %get-tuple-element.15), channel_id=1, source_target_pairs={{0,2},{1,3},{2,0},{3,1},{4,6},{5,7},{6,4},{7,5},{8,10},{9,11},{10,... | collective-permute-start | bytes 98312 | tf_op jit(solution)/shard_map/ppermute | solution.py:400
  18.4 2.6 %collective-permute-start.5 = (bf16[272,512]{1,0:T(8,128)(2,1)S(1)}, bf16[272,512]{1,0:T(8,128)(2,1)S(1)}, u32[]{:S(2)}, u32[]{:S(2)}) collective-permute-start(bf16[272,512]{1,0:T(8,128)(2,1)S(1)} %get-tuple-element.17.own_ref), channel_id=1, source_target_pairs={{0,64},{2,66},{4,68},{6,70},{8,72},{10,74},{12,76},{14,78},{16,80}... | collective-permute-start | bytes 835592 | tf_op jit(solution)/shard_map/ppermute | solution.py:400
  21.1 3.9 %collective-permute-start.6 = (bf16[272,512]{1,0:T(8,128)(2,1)S(1)}, bf16[272,512]{1,0:T(8,128)(2,1)S(1)}, u32[]{:S(2)}, u32[]{:S(2)}) collective-permute-start(bf16[272,512]{1,0:T(8,128)(2,1)S(1)} %get-tuple-element.17.own_ref), channel_id=1, source_target_pairs={{1,65},{3,67},{5,69},{7,71},{9,73},{11,75},{13,77},{15,79},{17,81}... | collective-permute-start | bytes 835592 | tf_op jit(solution)/shard_map/ppermute | solution.py:400
  25.0 1.9 %collective-permute-start.3 = (bf16[272,512]{1,0:T(8,128)(2,1)S(1)}, bf16[272,512]{1,0:T(8,128)(2,1)S(1)}, u32[]{:S(2)}, u32[]{:S(2)}) collective-permute-start(bf16[272,512]{1,0:T(8,128)(2,1)S(1)} %collective-permute-done.1.beside_ref), channel_id=1, source_target_pairs={{0,64},{2,66},{4,68},{6,70},{8,72},{10,74},{12,76},{14,78},{16,80}... | collective-permute-start | bytes 835592 | tf_op jit(solution)/shard_map/ppermute | solution.py:400
  26.9 4.6 %collective-permute-start.4 = (bf16[272,512]{1,0:T(8,128)(2,1)S(1)}, bf16[272,512]{1,0:T(8,128)(2,1)S(1)}, u32[]{:S(2)}, u32[]{:S(2)}) collective-permute-start(bf16[272,512]{1,0:T(8,128)(2,1)S(1)} %collective-permute-done.1.beside_ref), channel_id=1, source_target_pairs={{1,65},{3,67},{5,69},{7,71},{9,73},{11,75},{13,77},{15,79},{17,81}... | collective-permute-start | bytes 835592 | tf_op jit(solution)/shard_map/ppermute | solution.py:400
  31.5 2.1 %collective-permute-start.2 = (bf16[240,512]{1,0:T(8,128)(2,1)S(1)}, bf16[240,512]{1,0:T(8,128)(2,1)S(1)}, u32[]{:S(2)}, u32[]{:S(2)}) collective-permute-start(bf16[240,512]{1,0:T(8,128)(2,1)S(1)} %relay.1), channel_id=1, source_target_pairs={{0,1},{1,0},{2,3},{3,2},{4,5},{5,4},{6,7},{7,6},{8,9},{9,8},{10,11... | collective-permute-start | bytes 737288 | tf_op jit(solution)/shard_map/ppermute | solution.py:400
  33.6 1.3 %collective-permute-done.2.core_ref = bf16[240,512]{1,0:T(8,128)(2,1)S(1)} collective-permute-done((bf16[240,512]{1,0:T(8,128)(2,1)S(1)}, bf16[240,512]{1,0:T(8,128)(2,1)S(1)}, u32[]{:S(2)}, u32[]{:S(2)}) %collective-permute-start.2) | collective-permute-done | bytes 245792 | tf_op jit(solution)/shard_map/ppermute | solution.py:400
  34.9 1.3 %early.1.share_ref = f32[5,272,256]{2,1,0:T(8,128)S(1)} custom-call(s32[1,1]{1,0:T(1,128)} %bitcast.place_ref, bf16[2,16,512]{2,1,0:T(8,128)(2,1)S(1)} %get-tuple-element.16.near_ref, bf16[2,16,512]{2,1,0:T(8,128)(2,1)S(1)} %collective-permute-done.cross_ref, bf16[240,512]{1,0:T(8,128)(2,1)S(1)} %collective-permute-done.2.core_ref, ...), custom_call_target="tpu_custom_call" | custom-call | tf_op jit(solution)/shard_map/early/pallas_call | solution.py:389
  36.3 0.9 %collective-permute-done.4.second_ref = bf16[272,512]{1,0:T(8,128)(2,1)S(1)} collective-permute-done((bf16[272,512]{1,0:T(8,128)(2,1)S(1)}, bf16[272,512]{1,0:T(8,128)(2,1)S(1)}, u32[]{:S(2)}, u32[]{:S(2)}) %collective-permute-start.4) | collective-permute-done | bytes 278560 | tf_op jit(solution)/shard_map/ppermute | solution.py:400
  37.2 0.7 late.1
  38.0 4.0 %collective-permute-start.7 = (bf16[528,256]{1,0:T(8,128)(2,1)S(1)}, bf16[528,256]{1,0:T(8,128)(2,1)S(1)}, u32[]{:S(2)}, u32[]{:S(2)}) collective-permute-start(bf16[528,256]{1,0:T(8,128)(2,1)S(1)} %get-tuple-element.19), channel_id=1, source_target_pairs={{0,1},{1,0},{2,3},{3,2},{4,5},{5,4},{6,7},{7,6},{8,9},{9,8},{10,11... | collective-permute-start | bytes 811016 | tf_op jit(solution)/shard_map/ppermute | solution.py:400
  42.0 1.2 %collective-permute-done.7.give_ref = bf16[528,256]{1,0:T(8,128)(2,1)S(1)} collective-permute-done((bf16[528,256]{1,0:T(8,128)(2,1)S(1)}, bf16[528,256]{1,0:T(8,128)(2,1)S(1)}, u32[]{:S(2)}, u32[]{:S(2)}) %collective-permute-start.7) | collective-permute-done | bytes 270368 | tf_op jit(solution)/shard_map/ppermute | solution.py:400
  43.1 0.1 gather.1
  43.3 7.1 %collective-permute-start.8 = (bf16[272,256]{1,0:T(8,128)(2,1)S(1)}, bf16[272,256]{1,0:T(8,128)(2,1)S(1)}, u32[]{:S(2)}, u32[]{:S(2)}) collective-permute-start(bf16[272,256]{1,0:T(8,128)(2,1)S(1)} %get-tuple-element.21), channel_id=1, source_target_pairs={{0,2},{1,3},{2,0},{3,1},{4,6},{5,7},{6,4},{7,5},{8,10},{9,11},{10,... | collective-permute-start | bytes 417800 | tf_op jit(solution)/shard_map/ppermute | solution.py:400
  50.4 1.3 %collective-permute-start.9 = (bf16[144,256]{1,0:T(8,128)(2,1)S(1)}, bf16[144,256]{1,0:T(8,128)(2,1)S(1)}, u32[]{:S(2)}, u32[]{:S(2)}) collective-permute-start(bf16[144,256]{1,0:T(8,128)(2,1)S(1)} %get-tuple-element.22), channel_id=1, source_target_pairs={{1,4},{2,63},{5,8},{6,3},{9,12},{10,7},{13,16},{14,11},{17,20},{18... | collective-permute-start | bytes 221192 | tf_op jit(solution)/shard_map/ppermute | solution.py:400
  51.7 1.4 %collective-permute-done.9.side_ref = bf16[144,256]{1,0:T(8,128)(2,1)S(1)} collective-permute-done((bf16[144,256]{1,0:T(8,128)(2,1)S(1)}, bf16[144,256]{1,0:T(8,128)(2,1)S(1)}, u32[]{:S(2)}, u32[]{:S(2)}) %collective-permute-start.9) | collective-permute-done | bytes 73760 | tf_op jit(solution)/shard_map/ppermute | solution.py:400
  53.0 14.8 %collective-permute-done.8.cross_ref = bf16[272,256]{1,0:T(8,128)(2,1)S(1)} collective-permute-done((bf16[272,256]{1,0:T(8,128)(2,1)S(1)}, bf16[272,256]{1,0:T(8,128)(2,1)S(1)}, u32[]{:S(2)}, u32[]{:S(2)}) %collective-permute-start.8) | collective-permute-done | bytes 139296 | tf_op jit(solution)/shard_map/ppermute | solution.py:400
  67.8 4.1 %transform.1 = (bf16[256,256]{1,0:T(8,128)(2,1)S(1)}, bf16[256,256]{1,0:T(8,128)(2,1)S(1)}) custom-call(s32[1,1]{1,0:T(1,128)} %bitcast.place_ref, f32[272,256]{1,0:T(8,128)S(1)} %get-tuple-element.20.keep_ref, bf16[272,256]{1,0:T(8,128)(2,1)S(1)} %collective-permute-done.8.cross_ref, bf16[144,256]{1,0:T(8,128)(2,1)S(1)} %collective-permute-done.9.side_ref), custom_call_target="tpu_custom_call" | custom-call | tf_op jit(solution)/shard_map/transform/pallas_call | solution.py:389
  72.0 2.4 %collective-permute-start.10 = (bf16[256,256]{1,0:T(8,128)(2,1)S(1)}, bf16[256,256]{1,0:T(8,128)(2,1)S(1)}, u32[]{:S(2)}, u32[]{:S(2)}) collective-permute-start(bf16[256,256]{1,0:T(8,128)(2,1)S(1)} %get-tuple-element.23.self_ref), channel_id=1, source_target_pairs={{0,1},{1,0},{2,3},{3,2},{4,5},{5,4},{6,7},{7,6},{8,9},{9,8},{10,11... | collective-permute-start | bytes 393224 | tf_op jit(solution)/shard_map/ppermute | solution.py:400
  74.5 0.3 product.1.part_ref
  74.8 0.5 collective-permute-done.10.inner_ref
  75.3 0.8 %blend.1 = bf16[2,4,16,256]{3,2,1,0:T(8,128)(2,1)} custom-call(s32[1,1]{1,0:T(1,128)} %bitcast.place_ref, bf16[256,256]{1,0:T(8,128)(2,1)S(1)} %collective-permute-done.10.inner_ref, f32[2,4,16,256]{3,2,1,0:T(8,128)S(1)} %product.1.part_ref, bf16[2,4,16,256]{3,2,1,0:T(8,128)(2,1)S(1)} %copy-done), custom_call_target="tpu_custom_call" | custom-call | tf_op jit(solution)/shard_map/blend/pallas_call | solution.py:389
  (11 shorter events, 0.1 us)
Async XLA Ops:
  2.6 22.4 %collective-permute-start.1 = (bf16[272,512]{1,0:T(8,128)(2,1)S(1)}, bf16[272,512]{1,0:T(8,128)(2,1)S(1)}, u32[]{:S(2)}, u32[]{:S(2)}) collective-permute-start(bf16[272,512]{1,0:T(8,128)(2,1)S(1)} %get-tuple-element.17.own_ref), channel_id=1, source_target_pairs={{0,60},{1,61},{2,6},{3,7},{4,0},{5,1},{6,10},{7,11},{8,4},{9,5},{1... | collective-permute-start | bytes 835592 | tf_op jit(solution)/shard_map/ppermute | solution.py:400
  9.4 22.1 %collective-permute-start = (bf16[2,16,512]{2,1,0:T(8,128)(2,1)S(1)}, bf16[2,16,512]{2,1,0:T(8,128)(2,1)S(1)}, u32[]{:S(2)}, u32[]{:S(2)}) collective-permute-start(bf16[2,16,512]{2,1,0:T(8,128)(2,1)S(1)} %get-tuple-element.15), channel_id=1, source_target_pairs={{0,2},{1,3},{2,0},{3,1},{4,6},{5,7},{6,4},{7,5},{8,10},{9,11},{10,... | collective-permute-start | bytes 98312 | tf_op jit(solution)/shard_map/ppermute | solution.py:400
  18.4 15.1 %collective-permute-start.5 = (bf16[272,512]{1,0:T(8,128)(2,1)S(1)}, bf16[272,512]{1,0:T(8,128)(2,1)S(1)}, u32[]{:S(2)}, u32[]{:S(2)}) collective-permute-start(bf16[272,512]{1,0:T(8,128)(2,1)S(1)} %get-tuple-element.17.own_ref), channel_id=1, source_target_pairs={{0,64},{2,66},{4,68},{6,70},{8,72},{10,74},{12,76},{14,78},{16,80}... | collective-permute-start | bytes 835592 | tf_op jit(solution)/shard_map/ppermute | solution.py:400
  21.1 12.5 %collective-permute-start.6 = (bf16[272,512]{1,0:T(8,128)(2,1)S(1)}, bf16[272,512]{1,0:T(8,128)(2,1)S(1)}, u32[]{:S(2)}, u32[]{:S(2)}) collective-permute-start(bf16[272,512]{1,0:T(8,128)(2,1)S(1)} %get-tuple-element.17.own_ref), channel_id=1, source_target_pairs={{1,65},{3,67},{5,69},{7,71},{9,73},{11,75},{13,77},{15,79},{17,81}... | collective-permute-start | bytes 835592 | tf_op jit(solution)/shard_map/ppermute | solution.py:400
  25.0 11.3 %collective-permute-start.3 = (bf16[272,512]{1,0:T(8,128)(2,1)S(1)}, bf16[272,512]{1,0:T(8,128)(2,1)S(1)}, u32[]{:S(2)}, u32[]{:S(2)}) collective-permute-start(bf16[272,512]{1,0:T(8,128)(2,1)S(1)} %collective-permute-done.1.beside_ref), channel_id=1, source_target_pairs={{0,64},{2,66},{4,68},{6,70},{8,72},{10,74},{12,76},{14,78},{16,80}... | collective-permute-start | bytes 835592 | tf_op jit(solution)/shard_map/ppermute | solution.py:400
  26.9 10.3 %collective-permute-start.4 = (bf16[272,512]{1,0:T(8,128)(2,1)S(1)}, bf16[272,512]{1,0:T(8,128)(2,1)S(1)}, u32[]{:S(2)}, u32[]{:S(2)}) collective-permute-start(bf16[272,512]{1,0:T(8,128)(2,1)S(1)} %collective-permute-done.1.beside_ref), channel_id=1, source_target_pairs={{1,65},{3,67},{5,69},{7,71},{9,73},{11,75},{13,77},{15,79},{17,81}... | collective-permute-start | bytes 835592 | tf_op jit(solution)/shard_map/ppermute | solution.py:400
  31.5 3.4 %collective-permute-start.2 = (bf16[240,512]{1,0:T(8,128)(2,1)S(1)}, bf16[240,512]{1,0:T(8,128)(2,1)S(1)}, u32[]{:S(2)}, u32[]{:S(2)}) collective-permute-start(bf16[240,512]{1,0:T(8,128)(2,1)S(1)} %relay.1), channel_id=1, source_target_pairs={{0,1},{1,0},{2,3},{3,2},{4,5},{5,4},{6,7},{7,6},{8,9},{9,8},{10,11... | collective-permute-start | bytes 737288 | tf_op jit(solution)/shard_map/ppermute | solution.py:400
  36.3 38.1 %copy-start.1 = (f32[2,4,16]{2,1,0:T(4,128)S(1)}, f32[2,4,16]{2,1,0:T(4,128)}, u32[]{:S(2)}) copy-start(f32[2,4,16]{2,1,0:T(4,128)} %param.9) | copy-start | bytes 1540
  36.3 38.2 %copy-start = (bf16[2,4,16,256]{3,2,1,0:T(8,128)(2,1)S(1)}, bf16[2,4,16,256]{3,2,1,0:T(8,128)(2,1)}, u32[]{:S(2)}) copy-start(bf16[2,4,16,256]{3,2,1,0:T(8,128)(2,1)} %state_ref.3) | copy-start | bytes 196612
  38.0 5.2 %collective-permute-start.7 = (bf16[528,256]{1,0:T(8,128)(2,1)S(1)}, bf16[528,256]{1,0:T(8,128)(2,1)S(1)}, u32[]{:S(2)}, u32[]{:S(2)}) collective-permute-start(bf16[528,256]{1,0:T(8,128)(2,1)S(1)} %get-tuple-element.19), channel_id=1, source_target_pairs={{0,1},{1,0},{2,3},{3,2},{4,5},{5,4},{6,7},{7,6},{8,9},{9,8},{10,11... | collective-permute-start | bytes 811016 | tf_op jit(solution)/shard_map/ppermute | solution.py:400
  43.3 24.6 %collective-permute-start.8 = (bf16[272,256]{1,0:T(8,128)(2,1)S(1)}, bf16[272,256]{1,0:T(8,128)(2,1)S(1)}, u32[]{:S(2)}, u32[]{:S(2)}) collective-permute-start(bf16[272,256]{1,0:T(8,128)(2,1)S(1)} %get-tuple-element.21), channel_id=1, source_target_pairs={{0,2},{1,3},{2,0},{3,1},{4,6},{5,7},{6,4},{7,5},{8,10},{9,11},{10,... | collective-permute-start | bytes 417800 | tf_op jit(solution)/shard_map/ppermute | solution.py:400
  50.4 2.7 %collective-permute-start.9 = (bf16[144,256]{1,0:T(8,128)(2,1)S(1)}, bf16[144,256]{1,0:T(8,128)(2,1)S(1)}, u32[]{:S(2)}, u32[]{:S(2)}) collective-permute-start(bf16[144,256]{1,0:T(8,128)(2,1)S(1)} %get-tuple-element.22), channel_id=1, source_target_pairs={{1,4},{2,63},{5,8},{6,3},{9,12},{10,7},{13,16},{14,11},{17,20},{18... | collective-permute-start | bytes 221192 | tf_op jit(solution)/shard_map/ppermute | solution.py:400
  72.0 3.4 %collective-permute-start.10 = (bf16[256,256]{1,0:T(8,128)(2,1)S(1)}, bf16[256,256]{1,0:T(8,128)(2,1)S(1)}, u32[]{:S(2)}, u32[]{:S(2)}) collective-permute-start(bf16[256,256]{1,0:T(8,128)(2,1)S(1)} %get-tuple-element.23.self_ref), channel_id=1, source_target_pairs={{0,1},{1,0},{2,3},{3,2},{4,5},{5,4},{6,7},{7,6},{8,9},{9,8},{10,11... | collective-permute-start | bytes 393224 | tf_op jit(solution)/shard_map/ppermute | solution.py:400
